TPU v7x, 256 devices: a whole 4x4x8 slice. The times are simulated.
256 devices in a mesh: section: 8 (over z_lo, x), dp: 32 (over z_hi, y, core).
Axes of the slice: x: 4, y: 4, z: 8 (z_hi: 4, z_lo: 2; z = z_hi * 2 + z_lo), core: 2. Of those that a mesh axis runs over, the one named last changes fastest.
Arguments:
- inputs: bfloat16 [4, 1024, 4096], P(None, 'dp'), may hold values from -6 to 6
- cotangent: bfloat16 [4, 1024, 4096], P(None, 'dp'), may hold values from -0.09375 to 0.09375
- up_blocks: bfloat16 [8, 128, 128, 128], P('section', 'dp'), may hold values from -0.5 to 0.5
- up_index: int32 [8, 128, 2], P('section'), may hold values from 0 to 127, as said below
- up_left: bfloat16 [8, 4096, 16], P('section', 'dp'), may hold values from -0.09375 to 0.09375
- up_right: bfloat16 [8, 16384, 16], P('section', 'dp'), may hold values from -1.5 to 1.5
- down_blocks: bfloat16 [8, 128, 128, 128], P('section', 'dp'), may hold values from -0.25 to 0.25
- down_index: int32 [8, 128, 2], P('section'), may hold values from 0 to 127, as said below
- down_left: bfloat16 [8, 16384, 16], P('section', 'dp'), may hold values from -0.046875 to 0.046875
- down_right: bfloat16 [8, 4096, 16], P('section', 'dp'), may hold values from -1.5 to 1.5
Outputs:
- section_outputs: bfloat16 [8, 4, 1024, 4096], P('section', None, 'dp')
- up_grad: float32 [8, 128, 128, 128], P('section', 'dp')
- up_left_grad: float32 [8, 4096, 16], P('section', 'dp')
- up_right_grad: float32 [8, 16384, 16], P('section', 'dp')
- down_grad: float32 [8, 128, 128, 128], P('section', 'dp')
- down_left_grad: float32 [8, 16384, 16], P('section', 'dp')
- down_right_grad: float32 [8, 4096, 16], P('section', 'dp')
Inputs may be any that keep to these rules, and one draw needn't show every extreme that they name: `up_index`: column 0 is a block of model features (below 32), column 1 a block of hidden units; rows 4 * p to 4 * p + 3 hold model block p, and no pair repeats within a section. `down_index`: column 0 is a block of hidden units, column 1 a block of model features (below 32); rows 4 * p to 4 * p + 3 hold model block p, and no pair repeats within a section.
All inputs are finite; a program needn't handle non-finite values.
Results may differ from a plain program's by a relative error of at most 0.04.
Values may be sent and summed in bfloat16 or wider, within the bound.
No kernel may reach another device: no remote copies, remote signals or barrier semaphores. Data moves between devices by JAX's collectives and lax.ppermute only.
A program may use at most 128 MiB of HBM per device.

v0:
```python
import math

import jax
import jax.numpy as jnp
from jax import lax
from jax.sharding import PartitionSpec as P

NORM_EPS = 1e-05
GELU_CUBIC = 0.044715
GELU_ROOT = math.sqrt(2.0 / math.pi)


def shifted(block, axis, distance):
    devices = range(lax.axis_size(axis))
    route = [(i - distance, i) for i in devices if i - distance in devices]
    return lax.ppermute(block, axis, route)


def gelu_parts(values):
    inner = GELU_ROOT * (values + GELU_CUBIC * values * values * values)
    bend = jnp.tanh(inner)
    output = 0.5 * values * (1.0 + bend)
    slopes = 0.5 * (1.0 + bend) + 0.5 * values * (1.0 - bend * bend) * GELU_ROOT * (
        1.0 + 3.0 * GELU_CUBIC * values * values
    )
    return (output, slopes)


def to_hidden(products, target, count):
    merged = (
        jnp.zeros((products.shape[0], count, products.shape[2]), jnp.float32)
        .at[:, target]
        .add(products)
    )
    return merged.reshape(products.shape[0], count * products.shape[2])


def to_model(products, count):
    grouped = products.reshape(products.shape[0], count, -1, products.shape[2]).sum(axis=2)
    return grouped.reshape(products.shape[0], count * products.shape[2])


def block_product(values, tiles, source):
    tile_size = tiles.shape[-1]
    pieces = values.reshape(values.shape[0], -1, tile_size)[:, source]
    return jnp.einsum("tnb,nbc->tnc", pieces, tiles, preferred_element_type=jnp.float32)


def block_transpose(grads, tiles, target):
    tile_size = tiles.shape[-1]
    pieces = grads.reshape(grads.shape[0], -1, tile_size)[:, target]
    return jnp.einsum("tnc,nbc->tnb", pieces, tiles, preferred_element_type=jnp.float32)


def block_grad(values, grads, source, target, tile_size):
    left_pieces = values.reshape(values.shape[0], -1, tile_size)[:, source]
    right_pieces = grads.reshape(grads.shape[0], -1, tile_size)[:, target]
    return jnp.einsum("tnb,tnc->nbc", left_pieces, right_pieces, preferred_element_type=jnp.float32)


def outer_sum(left_rows, right_rows):
    return jnp.einsum("tx,ty->xy", left_rows, right_rows, preferred_element_type=jnp.float32)


def hidden_parts(values, weights):
    up_tiles, up_pairs, up_left, up_right, down_tiles, down_pairs, down_left, down_right = weights
    hidden_blocks = up_right.shape[0] // up_tiles.shape[-1]
    widened = values.astype(jnp.float32)
    scaling = lax.rsqrt(jnp.mean(widened * widened, axis=-1, keepdims=True) + NORM_EPS)
    normed = (widened * scaling).astype(jnp.bfloat16)
    up_latent = jnp.dot(normed, up_left, preferred_element_type=jnp.float32).astype(jnp.bfloat16)
    lowrank_up = jnp.einsum("tr,fr->tf", up_latent, up_right, preferred_element_type=jnp.float32)
    pre_act = (
        to_hidden(block_product(normed, up_tiles, up_pairs[:, 0]), up_pairs[:, 1], hidden_blocks)
        + lowrank_up
    )
    output, slopes = gelu_parts(pre_act)
    activation = output.astype(jnp.bfloat16)
    down_latent = jnp.dot(activation, down_left, preferred_element_type=jnp.float32).astype(
        jnp.bfloat16
    )
    return (widened, scaling, normed, up_latent, slopes, activation, down_latent)


def layer_forward(values, weights):
    widened, scaling, normed, up_latent, slopes, activation, down_latent = hidden_parts(
        values, weights
    )
    down_tiles, down_pairs, down_right = (weights[4], weights[5], weights[7])
    model_blocks = values.shape[1] // down_tiles.shape[-1]
    summed = widened + to_model(
        block_product(activation, down_tiles, down_pairs[:, 0]), model_blocks
    )
    summed = summed + jnp.einsum(
        "tr,dr->td", down_latent, down_right, preferred_element_type=jnp.float32
    )
    return summed.astype(jnp.bfloat16)


def layer_backward(values, grad_out, weights):
    up_tiles, up_pairs, up_left, up_right, down_tiles, down_pairs, down_left, down_right = weights
    widened, scaling, normed, up_latent, slopes, activation, down_latent = hidden_parts(
        values, weights
    )
    tile_size = up_tiles.shape[-1]
    hidden_blocks = up_right.shape[0] // tile_size
    model_blocks = values.shape[1] // tile_size
    grad_down_latent = jnp.dot(grad_out, down_right, preferred_element_type=jnp.float32).astype(
        jnp.bfloat16
    )
    grad_act = to_hidden(
        block_transpose(grad_out, down_tiles, down_pairs[:, 1]), down_pairs[:, 0], hidden_blocks
    )
    grad_act = grad_act + jnp.einsum(
        "tr,fr->tf", grad_down_latent, down_left, preferred_element_type=jnp.float32
    )
    grad_pre = (grad_act * slopes).astype(jnp.bfloat16)
    grad_up_latent = jnp.dot(grad_pre, up_right, preferred_element_type=jnp.float32).astype(
        jnp.bfloat16
    )
    grad_norm = to_model(block_transpose(grad_pre, up_tiles, up_pairs[:, 1]), model_blocks)
    grad_norm = grad_norm + jnp.einsum(
        "tr,dr->td", grad_up_latent, up_left, preferred_element_type=jnp.float32
    )
    unit = widened * scaling
    grad_in = grad_out.astype(jnp.float32) + scaling * (
        grad_norm - unit * jnp.mean(grad_norm * unit, axis=-1, keepdims=True)
    )
    stash = (
        normed,
        grad_pre,
        up_latent,
        grad_up_latent,
        activation,
        grad_out,
        down_latent,
        grad_down_latent,
    )
    return (grad_in.astype(jnp.bfloat16), stash)


def send_forward(values):
    return shifted(values, "section", 1)


def send_backward(values):
    return shifted(values, "section", -1)


def write_slot(buffer, value, slot, live):
    current = lax.dynamic_index_in_dim(buffer, slot, 0, False)
    return lax.dynamic_update_index_in_dim(buffer, jnp.where(live, value, current), slot, 0)


def per_device(
    inputs,
    cotangent,
    up_blocks,
    up_index,
    up_left,
    up_right,
    down_blocks,
    down_index,
    down_left,
    down_right,
):
    gathered = (
        lax.all_gather(up_blocks, "dp", axis=1, tiled=True),
        lax.all_gather(up_left, "dp", axis=1, tiled=True),
        lax.all_gather(up_right, "dp", axis=1, tiled=True),
        lax.all_gather(down_blocks, "dp", axis=1, tiled=True),
        lax.all_gather(down_left, "dp", axis=1, tiled=True),
        lax.all_gather(down_right, "dp", axis=1, tiled=True),
    )
    weights = (
        gathered[0][0],
        up_index[0],
        gathered[1][0],
        gathered[2][0],
        gathered[3][0],
        down_index[0],
        gathered[4][0],
        gathered[5][0],
    )
    sections = lax.axis_size("section")
    position = lax.axis_index("section")
    micro = inputs.shape[0]
    row_count = inputs.shape[1]
    model_width = inputs.shape[2]
    hidden_width = weights[3].shape[0]
    rank_width = weights[2].shape[1]
    tile_size = weights[0].shape[-1]
    reverse_position = sections - 1 - position

    def blank(width):
        return jnp.zeros((row_count, width), jnp.bfloat16)

    def empty_stash():
        return (
            blank(model_width),
            blank(hidden_width),
            blank(rank_width),
            blank(rank_width),
            blank(hidden_width),
            blank(model_width),
            blank(rank_width),
            blank(rank_width),
        )

    def forward_step(moment, state):
        incoming, saved, produced = state
        number = moment - position
        live = (number >= 0) & (number < micro)
        slot = jnp.clip(number, 0, micro - 1)
        source = jnp.where(
            position == 0, lax.dynamic_index_in_dim(inputs, slot, 0, False), incoming
        )
        result = lax.cond(
            live, lambda values: layer_forward(values, weights), jnp.zeros_like, source
        )
        return (
            send_forward(result),
            write_slot(saved, source, slot, live),
            write_slot(produced, result, slot, live),
        )

    def backward_step(moment, saved, state):
        incoming, buffers = state
        number = moment - reverse_position
        live = (number >= 0) & (number < micro)
        slot = jnp.clip(number, 0, micro - 1)
        grad_out = jnp.where(
            position == sections - 1, lax.dynamic_index_in_dim(cotangent, slot, 0, False), incoming
        )
        values = lax.dynamic_index_in_dim(saved, slot, 0, False)
        grad_in, parts = lax.cond(
            live,
            lambda pair: layer_backward(pair[0], pair[1], weights),
            lambda pair: (jnp.zeros_like(pair[0]), empty_stash()),
            (values, grad_out),
        )
        buffers = tuple(
            (write_slot(buffer, part, slot, live) for buffer, part in zip(buffers, parts))
        )
        return (send_backward(grad_in), buffers)

    forward_state = (blank(model_width), jnp.zeros_like(inputs), jnp.zeros_like(inputs))
    backward_state = (
        blank(model_width),
        tuple((jnp.zeros((micro,) + part.shape, part.dtype) for part in empty_stash())),
    )
    forward_state = lax.fori_loop(0, micro + sections - 1, forward_step, forward_state)
    saved_inputs = forward_state[1]
    backward_state = lax.fori_loop(
        0,
        micro + sections - 1,
        lambda moment, state: backward_step(moment, saved_inputs, state),
        backward_state,
    )
    flattened = tuple(
        (buffer.reshape(micro * row_count, buffer.shape[-1]) for buffer in backward_state[1])
    )
    (
        normed,
        grad_pre,
        up_latent,
        grad_up_latent,
        activation,
        grad_out,
        down_latent,
        grad_down_latent,
    ) = flattened
    up_pairs, down_pairs = (weights[1], weights[5])
    terms = (
        block_grad(normed, grad_pre, up_pairs[:, 0], up_pairs[:, 1], tile_size)[None],
        outer_sum(normed, grad_up_latent)[None],
        outer_sum(grad_pre, up_latent)[None],
        block_grad(activation, grad_out, down_pairs[:, 0], down_pairs[:, 1], tile_size)[None],
        outer_sum(activation, grad_down_latent)[None],
        outer_sum(grad_out, down_latent)[None],
    )
    reduced = (
        lax.psum_scatter(
            terms[0].astype(jnp.bfloat16), "dp", scatter_dimension=1, tiled=True
        ).astype(jnp.float32),
        lax.psum_scatter(
            terms[1].astype(jnp.bfloat16), "dp", scatter_dimension=1, tiled=True
        ).astype(jnp.float32),
        lax.psum_scatter(
            terms[2].astype(jnp.bfloat16), "dp", scatter_dimension=1, tiled=True
        ).astype(jnp.float32),
        lax.psum_scatter(
            terms[3].astype(jnp.bfloat16), "dp", scatter_dimension=1, tiled=True
        ).astype(jnp.float32),
        lax.psum_scatter(
            terms[4].astype(jnp.bfloat16), "dp", scatter_dimension=1, tiled=True
        ).astype(jnp.float32),
        lax.psum_scatter(
            terms[5].astype(jnp.bfloat16), "dp", scatter_dimension=1, tiled=True
        ).astype(jnp.float32),
    )
    return (
        forward_state[2][None],
        reduced[0],
        reduced[1],
        reduced[2],
        reduced[3],
        reduced[4],
        reduced[5],
    )


def solution(mesh):
    in_specs = (
        P(None, "dp", None),
        P(None, "dp", None),
        P("section", "dp", None, None),
        P("section", None, None),
        P("section", "dp", None),
        P("section", "dp", None),
        P("section", "dp", None, None),
        P("section", None, None),
        P("section", "dp", None),
        P("section", "dp", None),
    )
    out_specs = (
        P("section", None, "dp", None),
        P("section", "dp", None, None),
        P("section", "dp", None),
        P("section", "dp", None),
        P("section", "dp", None, None),
        P("section", "dp", None),
        P("section", "dp", None),
    )
    return jax.shard_map(
        per_device, mesh=mesh, in_specs=in_specs, out_specs=out_specs, check_vma=False
    )
```

profile of v0, /device:TPU:65, one launch (start us, length us, event | category | flops | bytes accessed | tf_op | source)
XLA Modules:
  0.0 2164.4 jit_solution(6880293452244641187)
XLA Ops:
  8.7 40.0 %all_gather.19 = bf16[1,4096,16]{1,2,0:T(8,128)(2,1)S(1)} all-gather(bf16[1,128,16]{1,2,0:T(8,128)(2,1)} %param.22), channel_id=1, replica_groups=mesh['section'=8,'dp'=32] {'dp'}, dimensions={1}, use_global_device_ids=true | all-gather | bytes 135168 | tf_op jit(solution)/shard_map/all_gather | solution.py:169
  48.7 43.7 %all_gather.23 = bf16[1,4096,16]{1,2,0:T(8,128)(2,1)} all-gather(bf16[1,128,16]{1,2,0:T(8,128)(2,1)} %param.27), channel_id=1, replica_groups=mesh['section'=8,'dp'=32] {'dp'}, dimensions={1}, use_global_device_ids=true | all-gather | bytes 135168 | tf_op jit(solution)/shard_map/all_gather | solution.py:173
  92.4 49.0 %all_gather.20 = bf16[1,16384,16]{1,2,0:T(8,128)(2,1)} all-gather(bf16[1,512,16]{1,2,0:T(8,128)(2,1)} %param.23), channel_id=1, replica_groups=mesh['section'=8,'dp'=32] {'dp'}, dimensions={1}, use_global_device_ids=true | all-gather | bytes 540672 | tf_op jit(solution)/shard_map/all_gather | solution.py:170
  141.4 44.6 %all_gather.22 = bf16[1,16384,16]{1,2,0:T(8,128)(2,1)} all-gather(bf16[1,512,16]{1,2,0:T(8,128)(2,1)} %param.26), channel_id=1, replica_groups=mesh['section'=8,'dp'=32] {'dp'}, dimensions={1}, use_global_device_ids=true | all-gather | bytes 540672 | tf_op jit(solution)/shard_map/all_gather | solution.py:172
  188.1 378.0 %while.49 = (s32[]{:T(128)}, bf16[32,4096]{1,0:T(8,128)(2,1)S(1)}, bf16[4,32,4096]{2,1,0:T(8,128)(2,1)}, bf16[4,32,4096]{2,1,0:T(8,128)(2,1)}, s32[]{:T(128)}, /...) while((s32[]{:T(128)}, bf16[32,4096]{1,0:T(8,128)(2,1)S(1)}, ...), condition=%wide.region_6.7_spmd, body=%wide.region_0.6_spmd.sunk | while | flops 318640288 | bytes 43793456 | solution.py:252
  190.9 32.2 %conditional.4 = (bf16[32,4096]{1,0:T(8,128)(2,1)}) conditional(s32[]{:T(128)} %convert_element_type.251, () %tuple.111, (bf16[32,4096]{1,0:T(8,128)(2,1)S(1)}, s32[128,2]{0,1:T(2,128)}, bf16[128,128,128]{2,1,0:T(8,128)(2,1)}, bf16[4096,16]{0,1:T(8,128)(2,1)S(1)}, bf16[16384,16]{0,1:T(8,128)(2,1)}, /*index=5*/s32[128,2]{0,1:T(2,128)}, ...), branch_computations={%region_1.1_spmd, %region_2.5_spmd} | conditional | flops 318247072 | bytes 39598276 | solution.py:218
  233.2 32.2 %conditional.4 = (bf16[32,4096]{1,0:T(8,128)(2,1)}) conditional(s32[]{:T(128)} %convert_element_type.251, () %tuple.111, (bf16[32,4096]{1,0:T(8,128)(2,1)S(1)}, s32[128,2]{0,1:T(2,128)}, bf16[128,128,128]{2,1,0:T(8,128)(2,1)}, bf16[4096,16]{0,1:T(8,128)(2,1)S(1)}, bf16[16384,16]{0,1:T(8,128)(2,1)}, /*index=5*/s32[128,2]{0,1:T(2,128)}, ...), branch_computations={%region_1.1_spmd, %region_2.5_spmd} | conditional | flops 318247072 | bytes 39598276 | solution.py:218
  277.3 32.2 %conditional.4 = (bf16[32,4096]{1,0:T(8,128)(2,1)}) conditional(s32[]{:T(128)} %convert_element_type.251, () %tuple.111, (bf16[32,4096]{1,0:T(8,128)(2,1)S(1)}, s32[128,2]{0,1:T(2,128)}, bf16[128,128,128]{2,1,0:T(8,128)(2,1)}, bf16[4096,16]{0,1:T(8,128)(2,1)S(1)}, bf16[16384,16]{0,1:T(8,128)(2,1)}, /*index=5*/s32[128,2]{0,1:T(2,128)}, ...), branch_computations={%region_1.1_spmd, %region_2.5_spmd} | conditional | flops 318247072 | bytes 39598276 | solution.py:218
  363.8 35.2 %collective-permute-start = (bf16[32,4096]{1,0:T(8,128)(2,1)}, bf16[32,4096]{1,0:T(8,128)(2,1)S(1)}, u32[]{:S(2)}, u32[]{:S(2)}) collective-permute-start(bf16[32,4096]{1,0:T(8,128)(2,1)} %get-tuple-element.1468), channel_id=1, source_target_pairs={{0,32},{32,64},{64,96},{96,128},{128,160},{160,192},{192,224},{1,3... | collective-permute-start | bytes 786440 | tf_op jit(solution)/shard_map/while/body/eval_jaxpr/ppermute | solution.py:16
  416.9 34.2 %collective-permute-start = (bf16[32,4096]{1,0:T(8,128)(2,1)}, bf16[32,4096]{1,0:T(8,128)(2,1)S(1)}, u32[]{:S(2)}, u32[]{:S(2)}) collective-permute-start(bf16[32,4096]{1,0:T(8,128)(2,1)} %get-tuple-element.1468), channel_id=1, source_target_pairs={{0,32},{32,64},{64,96},{96,128},{128,160},{160,192},{192,224},{1,3... | collective-permute-start | bytes 786440 | tf_op jit(solution)/shard_map/while/body/eval_jaxpr/ppermute | solution.py:16
  468.9 36.5 %collective-permute-start = (bf16[32,4096]{1,0:T(8,128)(2,1)}, bf16[32,4096]{1,0:T(8,128)(2,1)S(1)}, u32[]{:S(2)}, u32[]{:S(2)}) collective-permute-start(bf16[32,4096]{1,0:T(8,128)(2,1)} %get-tuple-element.1468), channel_id=1, source_target_pairs={{0,32},{32,64},{64,96},{96,128},{128,160},{160,192},{192,224},{1,3... | collective-permute-start | bytes 786440 | tf_op jit(solution)/shard_map/while/body/eval_jaxpr/ppermute | solution.py:16
  525.4 37.2 %collective-permute-start = (bf16[32,4096]{1,0:T(8,128)(2,1)}, bf16[32,4096]{1,0:T(8,128)(2,1)S(1)}, u32[]{:S(2)}, u32[]{:S(2)}) collective-permute-start(bf16[32,4096]{1,0:T(8,128)(2,1)} %get-tuple-element.1468), channel_id=1, source_target_pairs={{0,32},{32,64},{64,96},{96,128},{128,160},{160,192},{192,224},{1,3... | collective-permute-start | bytes 786440 | tf_op jit(solution)/shard_map/while/body/eval_jaxpr/ppermute | solution.py:16
  576.3 996.7 %while.50 = (s32[]{:T(128)}, bf16[32,4096]{1,0:T(8,128)(2,1)}, bf16[4,32,4096]{2,1,0:T(8,128)(2,1)}, bf16[4,32,16384]{2,1,0:T(8,128)(2,1)}, bf16[4,32,16]{1,2,0:...) while((s32[]{:T(128)}, bf16[32,4096]{1,0:T(8,128)(2,1)}, ...), condition=%wide.region_15.16_spmd, body=%wide.region_7.15_spmd.sunk | while | flops 503849504 | bytes 102200760 | solution.py:254
  743.9 479.7 %collective-permute-done.1 = bf16[32,4096]{1,0:T(8,128)(2,1)} collective-permute-done((bf16[32,4096]{1,0:T(8,128)(2,1)}, bf16[32,4096]{1,0:T(8,128)(2,1)}, u32[]{:S(2)}, u32[]{:S(2)}) %collective-permute-start.1) | collective-permute-done | bytes 262176 | tf_op jit(solution)/shard_map/while/body/eval_jaxpr/ppermute | solution.py:16
  1223.6 71.9 %conditional.5 = (bf16[32,4096]{1,0:T(8,128)(2,1)}, bf16[32,4096]{1,0:T(8,128)(2,1)S(1)}, bf16[32,16384]{1,0:T(8,128)(2,1)S(1)}, bf16[32,16]{0,1:T(8,128)(2,1)S(...) conditional(s32[]{:T(128)} %convert_element_type.252, ...), branch_computations={%region_8.8_spmd, %region_9.14_spmd} | conditional | flops 502536736 | bytes 87485408 | solution.py:236
  1311.1 71.9 %conditional.5 = (bf16[32,4096]{1,0:T(8,128)(2,1)}, bf16[32,4096]{1,0:T(8,128)(2,1)S(1)}, bf16[32,16384]{1,0:T(8,128)(2,1)S(1)}, bf16[32,16]{0,1:T(8,128)(2,1)S(...) conditional(s32[]{:T(128)} %convert_element_type.252, ...), branch_computations={%region_8.8_spmd, %region_9.14_spmd} | conditional | flops 502536736 | bytes 87485408 | solution.py:236
  1398.7 71.9 %conditional.5 = (bf16[32,4096]{1,0:T(8,128)(2,1)}, bf16[32,4096]{1,0:T(8,128)(2,1)S(1)}, bf16[32,16384]{1,0:T(8,128)(2,1)S(1)}, bf16[32,16]{0,1:T(8,128)(2,1)S(...) conditional(s32[]{:T(128)} %convert_element_type.252, ...), branch_computations={%region_8.8_spmd, %region_9.14_spmd} | conditional | flops 502536736 | bytes 87485408 | solution.py:236
  1486.2 71.9 %conditional.5 = (bf16[32,4096]{1,0:T(8,128)(2,1)}, bf16[32,4096]{1,0:T(8,128)(2,1)S(1)}, bf16[32,16384]{1,0:T(8,128)(2,1)S(1)}, bf16[32,16]{0,1:T(8,128)(2,1)S(...) conditional(s32[]{:T(128)} %convert_element_type.252, ...), branch_computations={%region_8.8_spmd, %region_9.14_spmd} | conditional | flops 502536736 | bytes 87485408 | solution.py:236
  1645.7 37.5 %reduce-scatter.19.cloned.1.call-done = bf16[128,16]{1,0:T(8,128)(2,1)} async-done(((bf16[4096,16]{1,0:T(8,128)(2,1)}), bf16[128,16]{1,0:T(8,128)(2,1)}) %reduce-scatter.19.cloned.1.call-update) | async-done | bytes 4112
  1684.7 89.2 %reduce-scatter.21.cloned.1.call-done = bf16[128,16]{1,0:T(8,128)(2,1)} async-done(((bf16[4096,16]{1,0:T(8,128)(2,1)}), bf16[128,16]{1,0:T(8,128)(2,1)}) %reduce-scatter.21.cloned.1.call-update) | async-done | bytes 4112
  1775.4 88.0 %reduce-scatter.13.cloned.1.call-done = bf16[1,512,16]{1,2,0:T(8,128)(2,1)} async-done(((bf16[1,16384,16]{1,2,0:T(8,128)(2,1)}), bf16[1,512,16]{1,2,0:T(8,128)(2,1)}) %reduce-scatter.13.cloned.1.call-update) | async-done | bytes 16400 | tf_op jit(solution)/shard_map/reduce_scatter | solution.py:289
  1864.7 88.2 %reduce-scatter.17.cloned.1.call-done = bf16[1,512,16]{1,2,0:T(8,128)(2,1)} async-done(((bf16[1,16384,16]{1,2,0:T(8,128)(2,1)}), bf16[1,512,16]{1,2,0:T(8,128)(2,1)}) %reduce-scatter.17.cloned.1.call-update) | async-done | bytes 16400 | tf_op jit(solution)/shard_map/reduce_scatter | solution.py:295
  1954.2 100.1 %reduce-scatter.11.cloned.1.call-done = bf16[1,4,128,128]{3,2,1,0:T(8,128)(2,1)} async-done(((bf16[1,128,128,128]{3,2,1,0:T(8,128)(2,1)}), bf16[1,4,128,128]{3,2,1,0:T(8,128)(2,1)}) %reduce-scatter.11.cloned.1.call-update) | async-done | bytes 131088 | tf_op jit(solution)/shard_map/reduce_scatter | solution.py:283
  2055.9 99.8 %reduce-scatter.15.cloned.1.call-done = bf16[1,4,128,128]{3,2,1,0:T(8,128)(2,1)} async-done(((bf16[1,128,128,128]{3,2,1,0:T(8,128)(2,1)}), bf16[1,4,128,128]{3,2,1,0:T(8,128)(2,1)}) %reduce-scatter.15.cloned.1.call-update) | async-done | bytes 131088 | tf_op jit(solution)/shard_map/reduce_scatter | solution.py:292
  (742 shorter events, 901.2 us)
Async XLA Ops:
  7.2 178.8 %all-gather.3.cloned.1.call-start = ((), (), s32[]{:S(2)}) async-start(), calls=%async_computation.6 | async-start | bytes 4325376 | tf_op jit(solution)/shard_map/all_gather | solution.py:168
  7.9 178.1 %all-gather.5.cloned.1.call-start = ((), (), s32[]{:S(2)}) async-start(), calls=%async_computation.7 | async-start | bytes 4325376 | tf_op jit(solution)/shard_map/all_gather | solution.py:171
  8.6 1674.5 %reduce-scatter.19.cloned.1.call-start = ((), (), s32[]{:S(2)}) async-start(), calls=%async_computation.12 | async-start | bytes 1081344
  363.8 38.8 %collective-permute-start = (bf16[32,4096]{1,0:T(8,128)(2,1)}, bf16[32,4096]{1,0:T(8,128)(2,1)S(1)}, u32[]{:S(2)}, u32[]{:S(2)}) collective-permute-start(bf16[32,4096]{1,0:T(8,128)(2,1)} %get-tuple-element.1468), channel_id=1, source_target_pairs={{0,32},{32,64},{64,96},{96,128},{128,160},{160,192},{192,224},{1,3... | collective-permute-start | bytes 786440 | tf_op jit(solution)/shard_map/while/body/eval_jaxpr/ppermute | solution.py:16
  416.9 37.8 %collective-permute-start = (bf16[32,4096]{1,0:T(8,128)(2,1)}, bf16[32,4096]{1,0:T(8,128)(2,1)S(1)}, u32[]{:S(2)}, u32[]{:S(2)}) collective-permute-start(bf16[32,4096]{1,0:T(8,128)(2,1)} %get-tuple-element.1468), channel_id=1, source_target_pairs={{0,32},{32,64},{64,96},{96,128},{128,160},{160,192},{192,224},{1,3... | collective-permute-start | bytes 786440 | tf_op jit(solution)/shard_map/while/body/eval_jaxpr/ppermute | solution.py:16
  468.9 40.1 %collective-permute-start = (bf16[32,4096]{1,0:T(8,128)(2,1)}, bf16[32,4096]{1,0:T(8,128)(2,1)S(1)}, u32[]{:S(2)}, u32[]{:S(2)}) collective-permute-start(bf16[32,4096]{1,0:T(8,128)(2,1)} %get-tuple-element.1468), channel_id=1, source_target_pairs={{0,32},{32,64},{64,96},{96,128},{128,160},{160,192},{192,224},{1,3... | collective-permute-start | bytes 786440 | tf_op jit(solution)/shard_map/while/body/eval_jaxpr/ppermute | solution.py:16
  512.5 9.4 collective-permute-start
  525.4 40.8 %collective-permute-start = (bf16[32,4096]{1,0:T(8,128)(2,1)}, bf16[32,4096]{1,0:T(8,128)(2,1)S(1)}, u32[]{:S(2)}, u32[]{:S(2)}) collective-permute-start(bf16[32,4096]{1,0:T(8,128)(2,1)} %get-tuple-element.1468), channel_id=1, source_target_pairs={{0,32},{32,64},{64,96},{96,128},{128,160},{160,192},{192,224},{1,3... | collective-permute-start | bytes 786440 | tf_op jit(solution)/shard_map/while/body/eval_jaxpr/ppermute | solution.py:16
  579.5 12.6 collective-permute-start.1
  594.8 32.6 %collective-permute-start.1 = (bf16[32,4096]{1,0:T(8,128)(2,1)}, bf16[32,4096]{1,0:T(8,128)(2,1)}, u32[]{:S(2)}, u32[]{:S(2)}) collective-permute-start(bf16[32,4096]{1,0:T(8,128)(2,1)} %get-tuple-element.1298), channel_id=1, source_target_pairs={{32,0},{64,32},{96,64},{128,96},{160,128},{192,160},{224,192},{33,... | collective-permute-start | bytes 786440 | tf_op jit(solution)/shard_map/while/body/eval_jaxpr/ppermute | solution.py:16
  630.1 13.2 collective-permute-start.1
  646.0 31.9 %collective-permute-start.1 = (bf16[32,4096]{1,0:T(8,128)(2,1)}, bf16[32,4096]{1,0:T(8,128)(2,1)}, u32[]{:S(2)}, u32[]{:S(2)}) collective-permute-start(bf16[32,4096]{1,0:T(8,128)(2,1)} %get-tuple-element.1298), channel_id=1, source_target_pairs={{32,0},{64,32},{96,64},{128,96},{160,128},{192,160},{224,192},{33,... | collective-permute-start | bytes 786440 | tf_op jit(solution)/shard_map/while/body/eval_jaxpr/ppermute | solution.py:16
  680.6 13.2 collective-permute-start.1
  696.6 32.0 %collective-permute-start.1 = (bf16[32,4096]{1,0:T(8,128)(2,1)}, bf16[32,4096]{1,0:T(8,128)(2,1)}, u32[]{:S(2)}, u32[]{:S(2)}) collective-permute-start(bf16[32,4096]{1,0:T(8,128)(2,1)} %get-tuple-element.1298), channel_id=1, source_target_pairs={{32,0},{64,32},{96,64},{128,96},{160,128},{192,160},{224,192},{33,... | collective-permute-start | bytes 786440 | tf_op jit(solution)/shard_map/while/body/eval_jaxpr/ppermute | solution.py:16
  731.3 492.3 %collective-permute-start.1 = (bf16[32,4096]{1,0:T(8,128)(2,1)}, bf16[32,4096]{1,0:T(8,128)(2,1)}, u32[]{:S(2)}, u32[]{:S(2)}) collective-permute-start(bf16[32,4096]{1,0:T(8,128)(2,1)} %get-tuple-element.1298), channel_id=1, source_target_pairs={{32,0},{64,32},{96,64},{128,96},{160,128},{192,160},{224,192},{33,... | collective-permute-start | bytes 786440 | tf_op jit(solution)/shard_map/while/body/eval_jaxpr/ppermute | solution.py:16
  1295.5 15.6 collective-permute-start.1
  1383.0 15.6 collective-permute-start.1
  1470.6 15.6 collective-permute-start.1
  1558.1 14.8 collective-permute-start.1
  1581.1 192.8 %reduce-scatter.21.cloned.1.call-start = ((), (), s32[]{:S(2)}) async-start(), calls=%async_computation.13 | async-start | bytes 1081344
  1588.2 275.1 %reduce-scatter.13.cloned.1.call-start = ((), (), s32[]{:S(2)}) async-start(), calls=%async_computation.9 | async-start | bytes 540672 | tf_op jit(solution)/shard_map/reduce_scatter | solution.py:289
  1592.2 360.7 %reduce-scatter.17.cloned.1.call-start = ((), (), s32[]{:S(2)}) async-start(), calls=%async_computation.11 | async-start | bytes 540672 | tf_op jit(solution)/shard_map/reduce_scatter | solution.py:295
  1596.1 458.2 %reduce-scatter.11.cloned.1.call-start = ((), (), s32[]{:S(2)}) async-start(), calls=%async_computation.8 | async-start | bytes 4325376 | tf_op jit(solution)/shard_map/reduce_scatter | solution.py:283
  1621.1 534.6 %reduce-scatter.15.cloned.1.call-start = ((), (), s32[]{:S(2)}) async-start(), calls=%async_computation.10 | async-start | bytes 4325376 | tf_op jit(solution)/shard_map/reduce_scatter | solution.py:292
  (100 other events, 1369.2 us)
Sparse Core Ops, SparseCore 0:
  10.6 62.2 all-gather.2
  75.4 59.5 all-gather.4
  1581.2 101.8 reduce-scatter.18
  1687.3 86.5 reduce-scatter.20
  1777.5 85.8 reduce-scatter.12
  1866.9 85.8 reduce-scatter.16
  1956.8 97.4 reduce-scatter.10
  2058.7 96.9 reduce-scatter.14
where the time goes:
time: 2190 us; the launch traced here: 2160 us
  waiting for transfers between devices  1070 us (49%)
  other arithmetic  318 us (15%)
  local copies, waits for them, and re-layouts  227 us (10%)
  starting transfers between devices  184 us (8%)
  blocking collectives  177 us (8%)
  matrix products  173 us (8%)
    ppermute x22, waiting for transfers between devices, shifted(): return lax.ppermute(block, axis, route)  563 us
    scatter-add x12, other arithmetic, to_hidden(): merged = jnp.zeros((products.shape[0], count, products.shape[2]), jnp.flo...  186 us
    ppermute x22, starting transfers between devices, shifted(): return lax.ppermute(block, axis, route)  184 us
    unnamed x10, waiting for transfers between devices  128 us
    dynamic_slice x110, local copies, waits for them, and re-layouts, write_slot(): current = lax.dynamic_index_in_dim(buffer, slot, 0, False)  101 us
    reduce_scatter x1, waiting for transfers between devices, per_device(): lax.psum_scatter(terms[0].astype(jnp.bfloat16), 'dp', scatter_dimension=1...  100 us
    reduce_scatter x1, waiting for transfers between devices, per_device(): lax.psum_scatter(terms[3].astype(jnp.bfloat16), 'dp', scatter_dimension=1...  99.8 us
    reduce_scatter x1, waiting for transfers between devices, per_device(): lax.psum_scatter(terms[4].astype(jnp.bfloat16), 'dp', scatter_dimension=1...  88.2 us
  transfers between devices with their start and end apart: 30, of which 26 were waited for; matrix products, arithmetic and copies ran while one was open for 10% of the time, Pallas kernels for 0%

commit v1 on v0

v1 whole, which is shorter than its diff:
```python
import math
from functools import partial

import jax
import jax.numpy as jnp
from jax import lax
from jax.experimental import pallas as pl
from jax.experimental.pallas import tpu as pltpu
from jax.sharding import Mesh
from jax.sharding import PartitionSpec as P

NORM_EPS = 1e-05
GELU_CUBIC = 0.044715
GELU_ROOT = math.sqrt(2.0 / math.pi)

TILE = 128
PER_ROW = 4
RANK = 16
UP = 0
DOWN = PER_ROW * TILE
LOW = 2 * PER_ROW * TILE
UP_LEFT = LOW
UP_RIGHT = UP_LEFT + RANK
DOWN_LEFT = UP_RIGHT + PER_ROW * RANK
DOWN_RIGHT = DOWN_LEFT + PER_ROW * RANK
PACKED = DOWN_RIGHT + RANK
WEIGHT_CHUNKS = 8
VMEM_LIMIT = 48 * 1024 * 1024
F32 = jnp.float32
BF16 = jnp.bfloat16


def mm(left, right):
    return lax.dot_general(left, right, (((1,), (0,)), ((), ())), preferred_element_type=F32)


def mm_nt(left, right):
    return lax.dot_general(left, right, (((1,), (1,)), ((), ())), preferred_element_type=F32)


def mm_tn(left, right):
    return lax.dot_general(left, right, (((0,), (0,)), ((), ())), preferred_element_type=F32)


def lanes(pieces):
    return jnp.concatenate(pieces, axis=1)


def low_rows(w, base, index):
    return lanes([w[index, base + RANK * i : base + RANK * (i + 1), :] for i in range(PER_ROW)])


def weight_copies(w_hbm, w, sem, first, second):
    blocks = w.shape[0]
    step = blocks // WEIGHT_CHUNKS
    copies = [
        pltpu.make_async_copy(w_hbm.at[:, LOW:PACKED, :], w.at[:, LOW:PACKED, :], sem.at[0])
    ]
    for number, base in enumerate((first, second)):
        for chunk in range(WEIGHT_CHUNKS):
            rows = pl.ds(chunk * step, step)
            cols = pl.ds(base, PER_ROW * TILE)
            copies.append(
                pltpu.make_async_copy(
                    w_hbm.at[rows, cols, :],
                    w.at[rows, cols, :],
                    sem.at[1 + number * WEIGHT_CHUNKS + chunk],
                )
            )
    return copies


def normalised(x_ref):
    xf = x_ref[...].astype(F32)
    scaling = lax.rsqrt(jnp.mean(xf * xf, axis=-1, keepdims=True) + NORM_EPS)
    return xf, scaling


def forward_kernel(
    info, upq, dnq, inputs, incoming, w_hbm, xs_in, outs_in, act_in, slope_in, lat_in,
    y_hbm, xs, outs, act, slope, lat,
    w, x, pre, av, sv, y, latv, sem, in_sem, out_sem,
):
    live, slot, first = info[0], info[1], info[2]
    blocks = w.shape[0]
    hidden = pre.shape[0]
    step = blocks // WEIGHT_CHUNKS

    @pl.when(live == 1)
    def _():
        @pl.when(first == 1)
        def _():
            pltpu.make_async_copy(inputs.at[slot], x, in_sem).start()

        @pl.when(first == 0)
        def _():
            pltpu.make_async_copy(incoming, x, in_sem).start()

        copies = weight_copies(w_hbm, w, sem, UP, DOWN)
        for copy in copies:
            copy.start()
        pltpu.make_async_copy(incoming, x, in_sem).wait()
        keep_x = pltpu.make_async_copy(x, xs.at[slot], out_sem.at[0])
        keep_x.start()
        xf, scaling = normalised(x)
        normed = (xf * scaling).astype(BF16)
        copies[0].wait()
        up_latent = jnp.zeros((x.shape[0], RANK), F32)
        for j in range(0, blocks, 2):
            up_latent += mm_nt(
                normed[:, j * TILE : (j + 2) * TILE],
                lanes([w[j + i, UP_LEFT : UP_LEFT + RANK, :] for i in range(2)]),
            )
        up_latent = up_latent.astype(BF16)
        latv[0, :, 0:RANK] = up_latent
        for p in range(blocks):
            low = mm(up_latent, low_rows(w, UP_RIGHT, p))
            for i in range(PER_ROW):
                pre[PER_ROW * p + i] = low[:, i * TILE : (i + 1) * TILE]
        for p in range(blocks):
            if p % step == 0:
                copies[1 + p // step].wait()
            piece = lanes([w[p, UP + i * TILE : UP + (i + 1) * TILE, :] for i in range(PER_ROW)])
            product = mm(normed[:, p * TILE : (p + 1) * TILE], piece)
            where = [upq[PER_ROW * p + i] for i in range(PER_ROW)]
            sums = [pre[q] + product[:, i * TILE : (i + 1) * TILE] for i, q in enumerate(where)]
            for q, value in zip(where, sums):
                pre[q] = value

        def gelu(q, carry):
            u = pre[q]
            square = u * u
            bend = jnp.tanh(GELU_ROOT * (u * (1.0 + GELU_CUBIC * square)))
            half = 0.5 + 0.5 * bend
            av[q] = (u * half).astype(BF16)
            slopes = half + 0.5 * u * (1.0 - bend * bend) * (
                GELU_ROOT * (1.0 + 3.0 * GELU_CUBIC * square)
            )
            sv[q] = slopes.astype(BF16)
            return carry

        lax.fori_loop(0, hidden, gelu, 0, unroll=8)
        keep_act = pltpu.make_async_copy(av, act.at[slot], out_sem.at[1])
        keep_slope = pltpu.make_async_copy(sv, slope.at[slot], out_sem.at[2])
        keep_act.start()
        keep_slope.start()
        down_latent = jnp.zeros((x.shape[0], RANK), F32)
        for p in range(blocks):
            down_latent += mm_nt(
                lanes([av[PER_ROW * p + i] for i in range(PER_ROW)]), low_rows(w, DOWN_LEFT, p)
            )
        down_latent = down_latent.astype(BF16)
        latv[1, :, 0:RANK] = down_latent
        keep_lat = pltpu.make_async_copy(latv, lat.at[slot], out_sem.at[3])
        keep_lat.start()
        for p in range(blocks):
            if p % step == 0:
                copies[1 + WEIGHT_CHUNKS + p // step].wait()
            left = lanes([av[dnq[PER_ROW * p + i]] for i in range(PER_ROW)])
            product = mm(left, w[p, DOWN : DOWN + PER_ROW * TILE, :])
            product += mm(down_latent, w[p, DOWN_RIGHT : DOWN_RIGHT + RANK, :])
            cols = slice(p * TILE, (p + 1) * TILE)
            y[:, cols] = (x[:, cols].astype(F32) + product).astype(BF16)
        send = pltpu.make_async_copy(y, y_hbm, out_sem.at[4])
        keep_y = pltpu.make_async_copy(y, outs.at[slot], out_sem.at[5])
        send.start()
        keep_y.start()
        for copy in (keep_x, keep_act, keep_slope, keep_lat, send, keep_y):
            copy.wait()


def backward_kernel(
    info, upq, dnq, cotangent, incoming, w_hbm, xs, slope, gs_in, gp_in, lat_in,
    y_hbm, gs, gp, lat,
    w, x, g, ga, sv, gpv, y, norm, latv, sem, in_sem, out_sem,
):
    live, slot, first = info[0], info[1], info[2]
    blocks = w.shape[0]
    hidden = ga.shape[0]
    step = blocks // WEIGHT_CHUNKS

    @pl.when(live == 1)
    def _():
        @pl.when(first == 1)
        def _():
            pltpu.make_async_copy(cotangent.at[slot], g, in_sem.at[0]).start()

        @pl.when(first == 0)
        def _():
            pltpu.make_async_copy(incoming, g, in_sem.at[0]).start()

        copies = weight_copies(w_hbm, w, sem, DOWN, UP)
        for copy in copies:
            copy.start()
        get_x = pltpu.make_async_copy(xs.at[slot], x, in_sem.at[1])
        get_slope = pltpu.make_async_copy(slope.at[slot], sv, in_sem.at[2])
        get_slope.start()
        get_x.start()
        pltpu.make_async_copy(incoming, g, in_sem.at[0]).wait()
        keep_g = pltpu.make_async_copy(g, gs.at[slot], out_sem.at[0])
        keep_g.start()
        copies[0].wait()
        down = jnp.zeros((g.shape[0], RANK), F32)
        for j in range(0, blocks, 2):
            down += mm_nt(
                g[:, j * TILE : (j + 2) * TILE],
                lanes([w[j + i, DOWN_RIGHT : DOWN_RIGHT + RANK, :] for i in range(2)]),
            )
        down = down.astype(BF16)
        latv[1, :, 0:RANK] = down
        for p in range(blocks):
            low = mm(down, low_rows(w, DOWN_LEFT, p))
            for i in range(PER_ROW):
                ga[PER_ROW * p + i] = low[:, i * TILE : (i + 1) * TILE]
        for p in range(blocks):
            if p % step == 0:
                copies[1 + p // step].wait()
            product = mm_nt(g[:, p * TILE : (p + 1) * TILE], w[p, DOWN : DOWN + PER_ROW * TILE, :])
            where = [dnq[PER_ROW * p + i] for i in range(PER_ROW)]
            sums = [ga[q] + product[:, i * TILE : (i + 1) * TILE] for i, q in enumerate(where)]
            for q, value in zip(where, sums):
                ga[q] = value
        get_slope.wait()

        def slopes(q, carry):
            gpv[q] = (ga[q] * sv[q].astype(F32)).astype(BF16)
            return carry

        lax.fori_loop(0, hidden, slopes, 0, unroll=8)
        keep_gp = pltpu.make_async_copy(gpv, gp.at[slot], out_sem.at[1])
        keep_gp.start()
        up = jnp.zeros((g.shape[0], RANK), F32)
        for p in range(blocks):
            up += mm_nt(
                lanes([gpv[PER_ROW * p + i] for i in range(PER_ROW)]), low_rows(w, UP_RIGHT, p)
            )
        up = up.astype(BF16)
        latv[0, :, 0:RANK] = up
        keep_lat = pltpu.make_async_copy(latv, lat.at[slot], out_sem.at[2])
        keep_lat.start()
        get_x.wait()
        xf, scaling = normalised(x)
        along = jnp.zeros((g.shape[0], TILE), F32)
        for p in range(blocks):
            if p % step == 0:
                copies[1 + WEIGHT_CHUNKS + p // step].wait()
            left = lanes([gpv[upq[PER_ROW * p + i]] for i in range(PER_ROW)])
            piece = lanes([w[p, UP + i * TILE : UP + (i + 1) * TILE, :] for i in range(PER_ROW)])
            product = mm_nt(left, piece)
            product += mm(up, w[p, UP_LEFT : UP_LEFT + RANK, :])
            cols = slice(p * TILE, (p + 1) * TILE)
            norm[:, cols] = product
            along += product * (xf[:, cols] * scaling)
        mean = jnp.sum(along, axis=-1, keepdims=True) * (1.0 / (blocks * TILE))
        y[...] = (
            g[...].astype(F32) + scaling * (norm[...] - (xf * scaling) * mean)
        ).astype(BF16)
        send = pltpu.make_async_copy(y, y_hbm, out_sem.at[3])
        send.start()
        for copy in (keep_g, keep_gp, keep_lat, send):
            copy.wait()


def grads_kernel(upq, dnq, xs, gs, act, gp, flat, blat, out, normed):
    blocks = out.shape[0]
    micro, rows, width = xs.shape
    tokens = micro * rows
    xf, scaling = normalised(xs)
    normed[...] = (xf * scaling).astype(BF16)

    def column(ref, p):
        return ref[:, :, pl.ds(pl.multiple_of(p * TILE, TILE), TILE)].reshape(tokens, TILE)

    def hidden(ref, q):
        return ref[:, pl.ds(q, 1)].reshape(tokens, TILE)

    def latent(ref, kind):
        return ref[:, kind, :, 0:RANK].reshape(tokens, RANK)

    up_latent, down_latent = latent(flat, 0), latent(flat, 1)
    grad_up_latent, grad_down_latent = latent(blat, 0), latent(blat, 1)

    def one(p, carry):
        n, g = column(normed, p), column(gs, p)
        ups = [upq[PER_ROW * p + i] for i in range(PER_ROW)]
        downs = [dnq[PER_ROW * p + i] for i in range(PER_ROW)]
        up = mm_tn(n, lanes([hidden(gp, q) for q in ups]))
        for i in range(PER_ROW):
            out[p, UP + i * TILE : UP + (i + 1) * TILE, :] = up[:, i * TILE : (i + 1) * TILE].astype(BF16)
        for i, q in enumerate(downs):
            out[p, DOWN + i * TILE : DOWN + (i + 1) * TILE, :] = mm_tn(hidden(act, q), g).astype(BF16)
        out[p, UP_LEFT : UP_LEFT + RANK, :] = mm_tn(grad_up_latent, n).astype(BF16)
        out[p, DOWN_RIGHT : DOWN_RIGHT + RANK, :] = mm_tn(down_latent, g).astype(BF16)
        for base, rows_of, ref in ((UP_RIGHT, up_latent, gp), (DOWN_LEFT, grad_down_latent, act)):
            low = mm_tn(rows_of, lanes([hidden(ref, PER_ROW * p + i) for i in range(PER_ROW)]))
            for i in range(PER_ROW):
                out[p, base + RANK * i : base + RANK * (i + 1), :] = low[:, i * TILE : (i + 1) * TILE].astype(BF16)
        return carry

    lax.fori_loop(0, blocks, one, 0)


SMEM = pl.BlockSpec(memory_space=pltpu.SMEM)
VMEM = pl.BlockSpec(memory_space=pltpu.VMEM)
HBM = pl.BlockSpec(memory_space=pl.ANY)


def forward_call(info, upq, dnq, inputs, incoming, packed, kept):
    rows, width = incoming.shape
    blocks = packed.shape[0]
    hidden = blocks * PER_ROW
    return pl.pallas_call(
        forward_kernel,
        out_shape=(jax.ShapeDtypeStruct(incoming.shape, BF16),)
        + tuple(jax.ShapeDtypeStruct(item.shape, item.dtype) for item in kept),
        in_specs=[SMEM] * 3 + [HBM] * (3 + len(kept)),
        out_specs=(HBM,) * (1 + len(kept)),
        input_output_aliases={6 + i: 1 + i for i in range(len(kept))},
        scratch_shapes=[
            pltpu.VMEM(packed.shape, BF16),
            pltpu.VMEM((rows, width), BF16),
            pltpu.VMEM((hidden, rows, TILE), F32),
            pltpu.VMEM((hidden, rows, TILE), BF16),
            pltpu.VMEM((hidden, rows, TILE), BF16),
            pltpu.VMEM((rows, width), BF16),
            pltpu.VMEM((2, rows, TILE), BF16),
            pltpu.SemaphoreType.DMA((1 + 2 * WEIGHT_CHUNKS,)),
            pltpu.SemaphoreType.DMA,
            pltpu.SemaphoreType.DMA((6,)),
        ],
        compiler_params=pltpu.CompilerParams(vmem_limit_bytes=VMEM_LIMIT),
        name="layer_forward",
    )(info, upq, dnq, inputs, incoming, packed, *kept)


def backward_call(info, upq, dnq, cotangent, incoming, packed, xs, slope, kept):
    rows, width = incoming.shape
    blocks = packed.shape[0]
    hidden = blocks * PER_ROW
    return pl.pallas_call(
        backward_kernel,
        out_shape=(jax.ShapeDtypeStruct(incoming.shape, BF16),)
        + tuple(jax.ShapeDtypeStruct(item.shape, item.dtype) for item in kept),
        in_specs=[SMEM] * 3 + [HBM] * (5 + len(kept)),
        out_specs=(HBM,) * (1 + len(kept)),
        input_output_aliases={8 + i: 1 + i for i in range(len(kept))},
        scratch_shapes=[
            pltpu.VMEM(packed.shape, BF16),
            pltpu.VMEM((rows, width), BF16),
            pltpu.VMEM((rows, width), BF16),
            pltpu.VMEM((hidden, rows, TILE), F32),
            pltpu.VMEM((hidden, rows, TILE), BF16),
            pltpu.VMEM((hidden, rows, TILE), BF16),
            pltpu.VMEM((rows, width), BF16),
            pltpu.VMEM((rows, width), F32),
            pltpu.VMEM((2, rows, TILE), BF16),
            pltpu.SemaphoreType.DMA((1 + 2 * WEIGHT_CHUNKS,)),
            pltpu.SemaphoreType.DMA((3,)),
            pltpu.SemaphoreType.DMA((4,)),
        ],
        compiler_params=pltpu.CompilerParams(vmem_limit_bytes=VMEM_LIMIT),
        name="layer_backward",
    )(info, upq, dnq, cotangent, incoming, packed, xs, slope, *kept)


def grads_call(upq, dnq, xs, gs, act, gp, flat, blat, blocks):
    return pl.pallas_call(
        grads_kernel,
        out_shape=jax.ShapeDtypeStruct((blocks, PACKED, TILE), BF16),
        in_specs=[SMEM] * 2 + [VMEM] * 6,
        out_specs=VMEM,
        scratch_shapes=[pltpu.VMEM(xs.shape, BF16)],
        compiler_params=pltpu.CompilerParams(vmem_limit_bytes=VMEM_LIMIT),
        name="weight_grads",
    )(upq, dnq, xs, gs, act, gp, flat, blat)


def buffers(*shapes):
    return pl.pallas_call(
        lambda *refs: None,
        out_shape=tuple(jax.ShapeDtypeStruct(shape, BF16) for shape in shapes),
        out_specs=(HBM,) * len(shapes),
        name="buffers",
    )()


def rank_first(factor, groups):
    return factor.reshape(groups, TILE, RANK).swapaxes(1, 2).reshape(groups * RANK, TILE)


def rank_last(rows, groups):
    return rows.reshape(groups, RANK, TILE).swapaxes(1, 2).reshape(groups * TILE, RANK)


def gather(packed):
    return lax.all_gather(packed, "dp", axis=0)


def scatter_sum(terms):
    return lax.psum_scatter(terms, "dp", scatter_dimension=0)


def per_device(
    inputs, cotangent, up_blocks, up_index, up_left, up_right, down_blocks, down_index,
    down_left, down_right,
):
    sections = lax.axis_size("section")
    position = lax.axis_index("section")
    micro, rows, width = inputs.shape
    blocks = width // TILE
    hidden = blocks * PER_ROW
    upq, dnq = up_index[0, :, 1], down_index[0, :, 0]
    packed = gather(
        jnp.concatenate(
            [
                up_blocks[0].reshape(PER_ROW * TILE, TILE),
                down_blocks[0].reshape(PER_ROW * TILE, TILE),
                rank_first(up_left[0], 1),
                rank_first(up_right[0], PER_ROW),
                rank_first(down_left[0], PER_ROW),
                rank_first(down_right[0], 1),
            ]
        )
    )

    def info(number, first):
        live = (number >= 0) & (number < micro)
        slot = jnp.clip(number, 0, micro - 1)
        return jnp.stack([live, slot, first]).astype(jnp.int32)

    wide, tall, thin = (micro, rows, width), (micro, hidden, rows, TILE), (micro, 2, rows, TILE)
    xs, outs, act, slope, flat, gs, gp, blat = buffers(
        wide, wide, tall, tall, thin, wide, tall, thin
    )
    moments = micro + sections - 1
    incoming = inputs[0]
    for moment in range(moments):
        result, xs, outs, act, slope, flat = forward_call(
            info(moment - position, position == 0), upq, dnq, inputs, incoming, packed,
            (xs, outs, act, slope, flat),
        )
        route = [(s, s + 1) for s in range(sections - 1) if 0 <= moment - s < micro]
        if route:
            incoming = lax.ppermute(result, "section", route)

    incoming = cotangent[0]
    for moment in range(moments):
        result, gs, gp, blat = backward_call(
            info(moment - (sections - 1 - position), position == sections - 1),
            upq, dnq, cotangent, incoming, packed, xs, slope, (gs, gp, blat),
        )
        route = [
            (s, s - 1) for s in range(1, sections) if 0 <= moment - (sections - 1 - s) < micro
        ]
        if route:
            incoming = lax.ppermute(result, "section", route)

    terms = grads_call(upq, dnq, xs, gs, act, gp, flat, blat, blocks)
    total = scatter_sum(terms).astype(F32)
    return (
        outs[None],
        total[UP:DOWN].reshape(1, PER_ROW, TILE, TILE),
        rank_last(total[UP_LEFT:UP_RIGHT], 1)[None],
        rank_last(total[UP_RIGHT:DOWN_LEFT], PER_ROW)[None],
        total[DOWN:LOW].reshape(1, PER_ROW, TILE, TILE),
        rank_last(total[DOWN_LEFT:DOWN_RIGHT], PER_ROW)[None],
        rank_last(total[DOWN_RIGHT:PACKED], 1)[None],
    )


def solution(mesh):
    in_specs = (
        P(None, "dp", None),
        P(None, "dp", None),
        P("section", "dp", None, None),
        P("section", None, None),
        P("section", "dp", None),
        P("section", "dp", None),
        P("section", "dp", None, None),
        P("section", None, None),
        P("section", "dp", None),
        P("section", "dp", None),
    )
    out_specs = (
        P("section", None, "dp", None),
        P("section", "dp", None, None),
        P("section", "dp", None),
        P("section", "dp", None),
        P("section", "dp", None, None),
        P("section", "dp", None),
        P("section", "dp", None),
    )
    return jax.shard_map(
        per_device, mesh=mesh, in_specs=in_specs, out_specs=out_specs, check_vma=False
    )
```

time: 2190 us -> 694 us (0.32)
  waiting for transfers between devices: 1070 us -> 453 us
  other arithmetic: 318 us -> 2.7 us
  blocking collectives: 177 us -> 0 us
  matrix products: 173 us -> 0 us
  local copies, waits for them, and re-layouts: 227 us -> 55.5 us
  starting transfers between devices: 184 us -> 26.9 us
  Pallas kernels: 0 us -> 128 us
    ppermute x22 -> x20, waiting for transfers between devices: 563 us -> 227 us  [per_device(): incoming = lax.ppermute(result, 'section', route)]
    reduce_scatter x4 -> x1, waiting for transfers between devices: 376 us -> 146 us  [scatter_sum(): return lax.psum_scatter(terms, 'dp', scatter_dimension=0)]
    scatter-add x12 -> x0, other arithmetic: 186 us -> none  [to_hidden(): merged = jnp.zeros((products.shape[0], count, products.shape[2]), jnp.flo...]
    all_gather x4 -> x0, blocking collectives: 177 us -> none  [the longest x1 49 us: per_device(): lax.all_gather(up_right, 'dp', axis=1, tiled=True)]
    dot_general x62 -> x0, matrix products: 173 us -> none  [the longest x12 41 us: block_product(): jnp.einsum('tnb,nbc->tnc', pieces, tiles, preferred_element_type=jnp.floa...]
    ppermute x22 -> x20, starting transfers between devices: 184 us -> 26.8 us  [per_device(): incoming = lax.ppermute(result, 'section', route)]
    pallas_call x0 -> x24, Pallas kernels: none -> 128 us  [the longest x11 59.5 us: backward_call(): pl.pallas_call(backward_kernel, out_shape=(jax.ShapeDtypeStruct(incoming....]
    unnamed x10 -> x2, waiting for transfers between devices: 128 us -> 0.03 us
  transfers between devices with their start and end apart: 30 -> 22, of which waited for: 26 -> 10; matrix products, arithmetic and copies ran while one was open for 10% -> 0% of each run, Pallas kernels for 0% -> 0%
where the time goes in v1:
time: 694 us; the launch traced here: 682 us
  waiting for transfers between devices  453 us (65%)
  Pallas kernels  128 us (18%)
  local copies, waits for them, and re-layouts  55.5 us (8%)
  starting transfers between devices  26.9 us (4%)
  between operations  15.5 us (2%)
    ppermute x20, waiting for transfers between devices, per_device(): incoming = lax.ppermute(result, 'section', route)  227 us
    reduce_scatter x1, waiting for transfers between devices, scatter_sum(): return lax.psum_scatter(terms, 'dp', scatter_dimension=0)  146 us
    all_gather x1, waiting for transfers between devices, gather(): return lax.all_gather(packed, 'dp', axis=0)  80.9 us
    pallas_call x11, Pallas kernels, backward_call(): pl.pallas_call(backward_kernel, out_shape=(jax.ShapeDtypeStruct(incoming....  59.5 us
    pallas_call x11, Pallas kernels, forward_call(): pl.pallas_call(forward_kernel, out_shape=(jax.ShapeDtypeStruct(incoming.s...  51.3 us
    unnamed x115, local copies, waits for them, and re-layouts  47.2 us
    ppermute x20, starting transfers between devices, per_device(): incoming = lax.ppermute(result, 'section', route)  26.8 us
    pallas_call x1, Pallas kernels, grads_call(): pl.pallas_call(grads_kernel, out_shape=jax.ShapeDtypeStruct((blocks, PACK...  17.5 us
  transfers between devices with their start and end apart: 22, of which 10 were waited for; matrix products, arithmetic and copies ran while one was open for 0% of the time, Pallas kernels for 0%

profile of v1, /device:TPU:65, one launch (start us, length us, event | category | flops | bytes accessed | tf_op | source)
XLA Modules:
  0.0 682.3 jit_solution(15582237444105486087)
XLA Ops:
  14.5 80.9 %all-gather.3.cloned.1.call-done = bf16[37888,128]{1,0:T(8,128)(2,1)} async-done(((bf16[1184,128]{1,0:T(8,128)(2,1)}), bf16[37888,128]{1,0:T(8,128)(2,1)}) %all-gather.3.cloned.1.call-update) | async-done | bytes 9699344 | tf_op jit(solution)/shard_map/all_gather | solution.py:396
  98.7 9.5 %layer_forward.11 = (bf16[32,4096]{1,0:T(8,128)(2,1)S(1)}, bf16[4,32,4096]{2,1,0:T(8,128)(2,1)S(1)}, bf16[4,32,4096]{2,1,0:T(8,128)(2,1)}, bf16[4,128,32,128]{3,...) custom-call(s32[3]{0:T(128)S(1)} %add_add_fusion.10.info, ...), custom_call_target="tpu_custom_call", output_to_operand_aliasing={{1}: (6, {}), {2}: (7, {}), {3}: (8, {}), {4}: (9, {}), {5}... | custom-call | tf_op jit(solution)/shard_map/layer_forward/pallas_call | solution.py:312
  111.3 5.7 collective-permute-done.incoming
  119.0 9.5 %layer_forward.12 = (bf16[32,4096]{1,0:T(8,128)(2,1)S(1)}, bf16[4,32,4096]{2,1,0:T(8,128)(2,1)S(1)}, bf16[4,32,4096]{2,1,0:T(8,128)(2,1)}, bf16[4,128,32,128]{3,...) custom-call(s32[3]{0:T(128)S(1)} %add_add_fusion.9.info, ...), custom_call_target="tpu_custom_call", output_to_operand_aliasing={{1}: (6, {}), {2}: (7, {}), {3}: (8, {}), {4}: (9, {}), {5}... | custom-call | tf_op jit(solution)/shard_map/layer_forward/pallas_call | solution.py:312
  130.1 4.1 collective-permute-start.1
  134.3 4.8 collective-permute-done.1.incoming
  141.2 9.5 %layer_forward.13 = (bf16[32,4096]{1,0:T(8,128)(2,1)S(1)}, bf16[4,32,4096]{2,1,0:T(8,128)(2,1)S(1)}, bf16[4,32,4096]{2,1,0:T(8,128)(2,1)}, bf16[4,128,32,128]{3,...) custom-call(s32[3]{0:T(128)S(1)} %add_add_fusion.8.info, ...), custom_call_target="tpu_custom_call", output_to_operand_aliasing={{1}: (6, {}), {2}: (7, {}), {3}: (8, {}), {4}: (9, {}), {5}... | custom-call | tf_op jit(solution)/shard_map/layer_forward/pallas_call | solution.py:312
  152.3 4.1 collective-permute-start.2
  156.5 3.8 collective-permute-done.2.incoming
  162.4 9.9 %layer_forward.14 = (bf16[32,4096]{1,0:T(8,128)(2,1)S(1)}, bf16[4,32,4096]{2,1,0:T(8,128)(2,1)S(1)}, bf16[4,32,4096]{2,1,0:T(8,128)(2,1)}, bf16[4,128,32,128]{3,...) custom-call(s32[3]{0:T(128)S(1)} %add_add_fusion.7.info, ...), custom_call_target="tpu_custom_call", output_to_operand_aliasing={{1}: (6, {}), {2}: (7, {}), {3}: (8, {}), {4}: (9, {}), {5}... | custom-call | tf_op jit(solution)/shard_map/layer_forward/pallas_call | solution.py:312
  174.0 4.1 collective-permute-start.3
  199.4 8.3 %layer_forward.18 = (bf16[32,4096]{1,0:T(8,128)(2,1)S(1)}, bf16[4,32,4096]{2,1,0:T(8,128)(2,1)S(1)}, bf16[4,32,4096]{2,1,0:T(8,128)(2,1)}, bf16[4,128,32,128]{3,...) custom-call(s32[3]{0:T(128)S(1)} %add_add_fusion.3.info, ...), custom_call_target="tpu_custom_call", output_to_operand_aliasing={{1}: (6, {}), {2}: (7, {}), {3}: (8, {}), {4}: (9, {}), {5}... | custom-call | tf_op jit(solution)/shard_map/layer_forward/pallas_call | solution.py:312
  225.8 7.9 %layer_backward.11 = (bf16[32,4096]{1,0:T(8,128)(2,1)S(1)}, bf16[4,32,4096]{2,1,0:T(8,128)(2,1)S(1)}, bf16[4,128,32,128]{3,2,1,0:T(8,128)(2,1)}, bf16[4,2,32,128]{3,2,1,0:T(8,128)(2,1)S(1)}) custom-call(s32[3]{0:T(128)S(1)} %add_add_fusion.21.info, s32[128]{0:T(128)S(1)} %get-tuple-element.246.upq, ...), custom_call_target="tpu_custom_call", output_to_operand_aliasing={{1}: (8, {}), {2}: (9, {}), {3}: (10, {})} | custom-call | tf_op jit(solution)/shard_map/layer_backward/pallas_call | solution.py:340
  240.4 7.9 %layer_backward.15 = (bf16[32,4096]{1,0:T(8,128)(2,1)}, bf16[4,32,4096]{2,1,0:T(8,128)(2,1)S(1)}, bf16[4,128,32,128]{3,2,1,0:T(8,128)(2,1)}, bf16[4,2,32,128]{3,2,1,0:T(8,128)(2,1)S(1)}) custom-call(s32[3]{0:T(128)S(1)} %add_add_fusion.17.info, s32[128]{0:T(128)S(1)} %get-tuple-element.246.upq, ...), custom_call_target="tpu_custom_call", output_to_operand_aliasing={{1}: (8, {}), {2}: (9, {}), {3}: (10, {})} | custom-call | tf_op jit(solution)/shard_map/layer_backward/pallas_call | solution.py:340
  252.9 185.2 %collective-permute-done.16.incoming = bf16[32,4096]{1,0:T(8,128)(2,1)S(1)} collective-permute-done((bf16[32,4096]{1,0:T(8,128)(2,1)}, bf16[32,4096]{1,0:T(8,128)(2,1)S(1)}, u32[]{:S(2)}, u32[]{:S(2)}) %collective-permute-start.16) | collective-permute-done | bytes 262176 | tf_op jit(solution)/shard_map/ppermute | solution.py:456
  438.1 9.8 %layer_backward.18 = (bf16[32,4096]{1,0:T(8,128)(2,1)}, bf16[4,32,4096]{2,1,0:T(8,128)(2,1)S(1)}, bf16[4,128,32,128]{3,2,1,0:T(8,128)(2,1)}, bf16[4,2,32,128]{3,2,1,0:T(8,128)(2,1)S(1)}) custom-call(s32[3]{0:T(128)S(1)} %add_add_fusion.14.info, s32[128]{0:T(128)S(1)} %get-tuple-element.246.upq, ...), custom_call_target="tpu_custom_call", output_to_operand_aliasing={{1}: (8, {}), {2}: (9, {}), {3}: (10, {})} | custom-call | tf_op jit(solution)/shard_map/layer_backward/pallas_call | solution.py:340
  449.2 8.0 %collective-permute-done.17.incoming = bf16[32,4096]{1,0:T(8,128)(2,1)S(1)} collective-permute-done((bf16[32,4096]{1,0:T(8,128)(2,1)}, bf16[32,4096]{1,0:T(8,128)(2,1)S(1)}, u32[]{:S(2)}, u32[]{:S(2)}) %collective-permute-start.17) | collective-permute-done | bytes 262176 | tf_op jit(solution)/shard_map/ppermute | solution.py:456
  457.3 10.5 %layer_backward.19 = (bf16[32,4096]{1,0:T(8,128)(2,1)}, bf16[4,32,4096]{2,1,0:T(8,128)(2,1)S(1)}, bf16[4,128,32,128]{3,2,1,0:T(8,128)(2,1)}, bf16[4,2,32,128]{3,2,1,0:T(8,128)(2,1)S(1)}) custom-call(s32[3]{0:T(128)S(1)} %add_add_fusion.13.info, s32[128]{0:T(128)S(1)} %get-tuple-element.246.upq, ...), custom_call_target="tpu_custom_call", output_to_operand_aliasing={{1}: (8, {}), {2}: (9, {}), {3}: (10, {})} | custom-call | tf_op jit(solution)/shard_map/layer_backward/pallas_call | solution.py:340
  469.1 8.0 %collective-permute-done.18.incoming = bf16[32,4096]{1,0:T(8,128)(2,1)S(1)} collective-permute-done((bf16[32,4096]{1,0:T(8,128)(2,1)}, bf16[32,4096]{1,0:T(8,128)(2,1)S(1)}, u32[]{:S(2)}, u32[]{:S(2)}) %collective-permute-start.18) | collective-permute-done | bytes 262176 | tf_op jit(solution)/shard_map/ppermute | solution.py:456
  477.2 9.8 %layer_backward.20 = (bf16[32,4096]{1,0:T(8,128)(2,1)}, bf16[4,32,4096]{2,1,0:T(8,128)(2,1)S(1)}, bf16[4,128,32,128]{3,2,1,0:T(8,128)(2,1)}, bf16[4,2,32,128]{3,2,1,0:T(8,128)(2,1)S(1)}) custom-call(s32[3]{0:T(128)S(1)} %add_add_fusion.12.info, s32[128]{0:T(128)S(1)} %get-tuple-element.246.upq, ...), custom_call_target="tpu_custom_call", output_to_operand_aliasing={{1}: (8, {}), {2}: (9, {}), {3}: (10, {})} | custom-call | tf_op jit(solution)/shard_map/layer_backward/pallas_call | solution.py:340
  488.4 8.0 %collective-permute-done.19.incoming = bf16[32,4096]{1,0:T(8,128)(2,1)S(1)} collective-permute-done((bf16[32,4096]{1,0:T(8,128)(2,1)}, bf16[32,4096]{1,0:T(8,128)(2,1)S(1)}, u32[]{:S(2)}, u32[]{:S(2)}) %collective-permute-start.19) | collective-permute-done | bytes 262176 | tf_op jit(solution)/shard_map/ppermute | solution.py:456
  496.4 9.8 %layer_backward.21 = (bf16[32,4096]{1,0:T(8,128)(2,1)}, bf16[4,32,4096]{2,1,0:T(8,128)(2,1)S(1)}, bf16[4,128,32,128]{3,2,1,0:T(8,128)(2,1)}, bf16[4,2,32,128]{3,2,1,0:T(8,128)(2,1)S(1)}) custom-call(s32[3]{0:T(128)S(1)} %add_add_fusion.11.info, s32[128]{0:T(128)S(1)} %get-tuple-element.246.upq, ...), custom_call_target="tpu_custom_call", output_to_operand_aliasing={{1}: (8, {}), {2}: (9, {}), {3}: (10, {})} | custom-call | tf_op jit(solution)/shard_map/layer_backward/pallas_call | solution.py:340
  506.2 17.5 %weight_grads.1 = bf16[32,1184,128]{2,1,0:T(8,128)(2,1)} custom-call(s32[128]{0:T(128)S(1)} %get-tuple-element.246.upq, s32[128]{0:T(128)S(1)} %get-tuple-element.245.dnq, bf16[4,32,4096]{2,1,0:T(8,128)(2,1)S(1)} %copy-done.23, bf16[4,32,4096]{2,1,0:T(8,128)(2,1)S(1)} %get-tuple-element.234.gs, bf16[4,128,32,128]{3,2,1,0:T(8,128)(2,1)} %get-tuple-element.235.act, ...), custom_call_target="tpu_custom_call" | custom-call | tf_op jit(solution)/shard_map/weight_grads/pallas_call | solution.py:367
  523.6 145.8 %reduce-scatter.2.cloned.1.call-done = bf16[1,1184,128]{2,1,0:T(8,128)(2,1)} async-done(((bf16[32,1184,128]{2,1,0:T(8,128)(2,1)}), bf16[1,1184,128]{2,1,0:T(8,128)(2,1)}) %reduce-scatter.2.cloned.1.call-update) | async-done | bytes 303120 | tf_op jit(solution)/shard_map/reduce_scatter | solution.py:400
  (199 shorter events, 84.6 us)
Async XLA Ops:
  7.2 88.3 %all-gather.3.cloned.1.call-start = ((), (), s32[]{:S(2)}) async-start(), calls=%async_computation.2 | async-start | bytes 10002432 | tf_op jit(solution)/shard_map/all_gather | solution.py:396
  12.7 656.7 %reduce-scatter.2.cloned.1.call-start = ((), (), s32[]{:S(2)}) async-start(), calls=%async_computation.1 | async-start | bytes 10002432 | tf_op jit(solution)/shard_map/reduce_scatter | solution.py:400
  98.7 18.2 %copy-start.26 = (bf16[4,32,4096]{2,1,0:T(8,128)(2,1)S(1)}, bf16[4,32,4096]{2,1,0:T(8,128)(2,1)}, u32[]{:S(2)}) copy-start(bf16[4,32,4096]{2,1,0:T(8,128)(2,1)} %inputs.21) | copy-start | bytes 3145732
  109.9 7.0 %collective-permute-start = (bf16[32,4096]{1,0:T(8,128)(2,1)S(1)}, bf16[32,4096]{1,0:T(8,128)(2,1)S(1)}, u32[]{:S(2)}, u32[]{:S(2)}) collective-permute-start(bf16[32,4096]{1,0:T(8,128)(2,1)S(1)} %get-tuple-element.128), channel_id=1, source_target_pairs={{0,32},{1,33},{2,34},{3,35},{4,36},{5,37},{6,38},{7,39},{8,40},{9,... | collective-permute-start | bytes 786440 | tf_op jit(solution)/shard_map/ppermute | solution.py:444
  130.1 9.0 %collective-permute-start.1 = (bf16[32,4096]{1,0:T(8,128)(2,1)S(1)}, bf16[32,4096]{1,0:T(8,128)(2,1)S(1)}, u32[]{:S(2)}, u32[]{:S(2)}) collective-permute-start(bf16[32,4096]{1,0:T(8,128)(2,1)S(1)} %get-tuple-element.134), channel_id=1, source_target_pairs={{0,32},{32,64},{1,33},{33,65},{2,34},{34,66},{3,35},{35,67},{4,36}... | collective-permute-start | bytes 786440 | tf_op jit(solution)/shard_map/ppermute | solution.py:444
  152.3 8.0 %collective-permute-start.2 = (bf16[32,4096]{1,0:T(8,128)(2,1)S(1)}, bf16[32,4096]{1,0:T(8,128)(2,1)S(1)}, u32[]{:S(2)}, u32[]{:S(2)}) collective-permute-start(bf16[32,4096]{1,0:T(8,128)(2,1)S(1)} %get-tuple-element.140), channel_id=1, source_target_pairs={{0,32},{32,64},{64,96},{1,33},{33,65},{65,97},{2,34},{34,66},{66,9... | collective-permute-start | bytes 786440 | tf_op jit(solution)/shard_map/ppermute | solution.py:444
  174.0 7.4 %collective-permute-start.3 = (bf16[32,4096]{1,0:T(8,128)(2,1)S(1)}, bf16[32,4096]{1,0:T(8,128)(2,1)S(1)}, u32[]{:S(2)}, u32[]{:S(2)}) collective-permute-start(bf16[32,4096]{1,0:T(8,128)(2,1)S(1)} %get-tuple-element.146), channel_id=1, source_target_pairs={{0,32},{32,64},{64,96},{96,128},{1,33},{33,65},{65,97},{97,129},{2... | collective-permute-start | bytes 786440 | tf_op jit(solution)/shard_map/ppermute | solution.py:444
  185.9 0.8 collective-permute-start.4
  191.2 0.8 collective-permute-start.5
  196.5 0.8 collective-permute-start.6
  209.4 0.8 collective-permute-start.7
  214.7 0.8 collective-permute-start.8
  220.0 0.9 collective-permute-start.9
  233.7 0.8 collective-permute-start.10
  236.5 0.8 collective-permute-start.11
  238.1 0.8 collective-permute-start.12
  239.6 0.8 collective-permute-start.13
  248.4 0.8 collective-permute-start.14
  249.9 0.8 collective-permute-start.15
  251.5 186.6 %collective-permute-start.16 = (bf16[32,4096]{1,0:T(8,128)(2,1)}, bf16[32,4096]{1,0:T(8,128)(2,1)S(1)}, u32[]{:S(2)}, u32[]{:S(2)}) collective-permute-start(bf16[32,4096]{1,0:T(8,128)(2,1)} %get-tuple-element.218), channel_id=1, source_target_pairs={{32,0},{64,32},{96,64},{128,96},{33,1},{65,33},{97,65},{129,97},{3... | collective-permute-start | bytes 786440 | tf_op jit(solution)/shard_map/ppermute | solution.py:456
  447.9 9.4 %collective-permute-start.17 = (bf16[32,4096]{1,0:T(8,128)(2,1)}, bf16[32,4096]{1,0:T(8,128)(2,1)S(1)}, u32[]{:S(2)}, u32[]{:S(2)}) collective-permute-start(bf16[32,4096]{1,0:T(8,128)(2,1)} %get-tuple-element.222), channel_id=1, source_target_pairs={{32,0},{64,32},{96,64},{33,1},{65,33},{97,65},{34,2},{66,34},{98,6... | collective-permute-start | bytes 786440 | tf_op jit(solution)/shard_map/ppermute | solution.py:456
  467.8 9.4 %collective-permute-start.18 = (bf16[32,4096]{1,0:T(8,128)(2,1)}, bf16[32,4096]{1,0:T(8,128)(2,1)S(1)}, u32[]{:S(2)}, u32[]{:S(2)}) collective-permute-start(bf16[32,4096]{1,0:T(8,128)(2,1)} %get-tuple-element.226), channel_id=1, source_target_pairs={{32,0},{64,32},{33,1},{65,33},{34,2},{66,34},{35,3},{67,35},{36,4}... | collective-permute-start | bytes 786440 | tf_op jit(solution)/shard_map/ppermute | solution.py:456
  487.0 9.4 %collective-permute-start.19 = (bf16[32,4096]{1,0:T(8,128)(2,1)}, bf16[32,4096]{1,0:T(8,128)(2,1)S(1)}, u32[]{:S(2)}, u32[]{:S(2)}) collective-permute-start(bf16[32,4096]{1,0:T(8,128)(2,1)} %get-tuple-element.230), channel_id=1, source_target_pairs={{32,0},{33,1},{34,2},{35,3},{36,4},{37,5},{38,6},{39,7},{40,8},{41... | collective-permute-start | bytes 786440 | tf_op jit(solution)/shard_map/ppermute | solution.py:456
  496.4 9.8 %copy-start.51 = (bf16[4,2,32,128]{3,2,1,0:T(8,128)(2,1)S(1)}, bf16[4,2,32,128]{3,2,1,0:T(8,128)(2,1)}, u32[]{:S(2)}) copy-start(bf16[4,2,32,128]{3,2,1,0:T(8,128)(2,1)} %copy-done.50) | copy-start | bytes 196612
  (53 other events, 68.1 us)
Sparse Core Ops, SparseCore 0:
  12.8 82.5 all-gather.2
  523.8 145.5 reduce-scatter.1

commit v2 on v1

v2 whole, which is shorter than its diff:
```python
import math
from functools import partial

import jax
import jax.numpy as jnp
from jax import lax
from jax.experimental import pallas as pl
from jax.experimental.pallas import tpu as pltpu
from jax.sharding import Mesh
from jax.sharding import PartitionSpec as P

NORM_EPS = 1e-05
GELU_CUBIC = 0.044715
GELU_ROOT = math.sqrt(2.0 / math.pi)

TILE = 128
PER_ROW = 4
RANK = 16
MODEL = PER_ROW * TILE
HIDDEN = MODEL + RANK
SIDE = HIDDEN + PER_ROW * RANK
UP = 0
DOWN = 1
ALONG = 4
CORES = 2
SMALL_VMEM = 12 * 1024 * 1024
LAYER_VMEM = 12 * 1024 * 1024
F32 = jnp.float32
BF16 = jnp.bfloat16


def mm(left, right):
    return lax.dot_general(left, right, (((1,), (0,)), ((), ())), preferred_element_type=F32)


def mm_nt(left, right):
    return lax.dot_general(left, right, (((1,), (1,)), ((), ())), preferred_element_type=F32)


def mm_tn(left, right):
    return lax.dot_general(left, right, (((0,), (0,)), ((), ())), preferred_element_type=F32)


def lanes(pieces):
    return jnp.concatenate(pieces, axis=1)


def low_rows(side, index):
    return lanes(
        [side[index, HIDDEN + RANK * i : HIDDEN + RANK * (i + 1), :] for i in range(PER_ROW)]
    )


def normalised(x_ref):
    xf = x_ref[...].astype(F32)
    scaling = lax.rsqrt(jnp.mean(xf * xf, axis=-1, keepdims=True) + NORM_EPS)
    return xf, scaling


def slot_at(number, micro):
    live = (number >= 0) & (number < micro)
    return live, jnp.clip(number, 0, micro - 1)


def forward_kernel(
    moment, place, upq, dnq, inputs, incoming, wu, wd, xs_in, outs_in, act_in, slope_in, lat_in,
    y, xs, outs, act, slope, lat,
    pre,
):
    position = place[3]
    live, slot = slot_at(moment - 2 * position, inputs.shape[0])
    blocks = wu.shape[0]
    hidden = pre.shape[0]
    rows = y.shape[0]

    @pl.when(live)
    def _():
        @pl.when(position == 0)
        def _():
            xs[slot] = inputs[slot]

        @pl.when(position != 0)
        def _():
            xs[slot] = incoming[...]

        x = xs[slot]
        xf, scaling = normalised(x)
        normed = (xf * scaling).astype(BF16)
        up_latent = jnp.zeros((rows, RANK), F32)
        for j in range(0, blocks, 2):
            up_latent += mm_nt(
                normed[:, j * TILE : (j + 2) * TILE],
                lanes([wu[j + i, MODEL:HIDDEN, :] for i in range(2)]),
            )
        up_latent = up_latent.astype(BF16)
        lat[slot, 0, :, 0:RANK] = up_latent
        for p in range(blocks):
            low = mm(up_latent, low_rows(wu, p))
            for i in range(PER_ROW):
                pre[PER_ROW * p + i] = low[:, i * TILE : (i + 1) * TILE]
        for p in range(blocks):
            piece = lanes([wu[p, i * TILE : (i + 1) * TILE, :] for i in range(PER_ROW)])
            product = mm(normed[:, p * TILE : (p + 1) * TILE], piece)
            where = [upq[PER_ROW * p + i] for i in range(PER_ROW)]
            sums = [pre[q] + product[:, i * TILE : (i + 1) * TILE] for i, q in enumerate(where)]
            for q, value in zip(where, sums):
                pre[q] = value

        def gelu(q, carry):
            u = pre[q]
            square = u * u
            bend = jnp.tanh(u * (GELU_ROOT + GELU_ROOT * GELU_CUBIC * square))
            half = 0.5 + 0.5 * bend
            act[slot, q] = (u * half).astype(BF16)
            inner = 0.5 * GELU_ROOT + 1.5 * GELU_ROOT * GELU_CUBIC * square
            slopes = half + (u * inner) * (1.0 - bend * bend)
            slope[slot, q] = slopes.astype(BF16)
            return carry

        lax.fori_loop(0, hidden, gelu, 0, unroll=8)
        down_latent = jnp.zeros((rows, RANK), F32)
        for p in range(blocks):
            down_latent += mm_nt(
                lanes([act[slot, PER_ROW * p + i] for i in range(PER_ROW)]),
                low_rows(wd, p),
            )
        down_latent = down_latent.astype(BF16)
        lat[slot, 1, :, 0:RANK] = down_latent
        for p in range(blocks):
            left = lanes([act[slot, dnq[PER_ROW * p + i]] for i in range(PER_ROW)])
            product = mm(left, wd[p, 0:MODEL, :])
            product += mm(down_latent, wd[p, MODEL:HIDDEN, :])
            cols = slice(p * TILE, (p + 1) * TILE)
            result = (x[:, cols].astype(F32) + product).astype(BF16)
            y[:, cols] = result
            outs[slot, :, cols] = result


def backward_kernel(
    moment, sections, place, upq, dnq, cotangent, incoming, wu, wd, xs, gs_in, slope, lat_in,
    y, gs, gp, lat,
    ga, norm,
):
    position = place[3]
    live, slot = slot_at(moment - 2 * (sections - 1 - position), cotangent.shape[0])
    blocks = wu.shape[0]
    hidden = ga.shape[0]
    rows = y.shape[0]

    @pl.when(live)
    def _():
        @pl.when(position == sections - 1)
        def _():
            gs[slot] = cotangent[slot]

        @pl.when(position != sections - 1)
        def _():
            gs[slot] = incoming[...]

        g = gs[slot]
        down = jnp.zeros((rows, RANK), F32)
        for j in range(0, blocks, 2):
            down += mm_nt(
                g[:, j * TILE : (j + 2) * TILE],
                lanes([wd[j + i, MODEL:HIDDEN, :] for i in range(2)]),
            )
        down = down.astype(BF16)
        lat[slot, 1, :, 0:RANK] = down
        for p in range(blocks):
            low = mm(down, low_rows(wd, p))
            for i in range(PER_ROW):
                ga[PER_ROW * p + i] = low[:, i * TILE : (i + 1) * TILE]
        for p in range(blocks):
            product = mm_nt(g[:, p * TILE : (p + 1) * TILE], wd[p, 0:MODEL, :])
            where = [dnq[PER_ROW * p + i] for i in range(PER_ROW)]
            sums = [ga[q] + product[:, i * TILE : (i + 1) * TILE] for i, q in enumerate(where)]
            for q, value in zip(where, sums):
                ga[q] = value

        def slopes(q, carry):
            gp[slot, q] = (ga[q] * slope[slot, q].astype(F32)).astype(BF16)
            return carry

        lax.fori_loop(0, hidden, slopes, 0, unroll=8)
        up = jnp.zeros((rows, RANK), F32)
        for p in range(blocks):
            up += mm_nt(
                lanes([gp[slot, PER_ROW * p + i] for i in range(PER_ROW)]),
                low_rows(wu, p),
            )
        up = up.astype(BF16)
        lat[slot, 0, :, 0:RANK] = up
        xf, scaling = normalised(xs[slot])
        along = jnp.zeros((rows, TILE), F32)
        for p in range(blocks):
            left = lanes([gp[slot, upq[PER_ROW * p + i]] for i in range(PER_ROW)])
            piece = lanes([wu[p, i * TILE : (i + 1) * TILE, :] for i in range(PER_ROW)])
            product = mm_nt(left, piece)
            product += mm(up, wu[p, MODEL:HIDDEN, :])
            cols = slice(p * TILE, (p + 1) * TILE)
            norm[:, cols] = product
            along += product * (xf[:, cols] * scaling)
        mean = jnp.sum(along, axis=-1, keepdims=True) * (1.0 / (blocks * TILE))
        y[...] = (
            g.astype(F32) + scaling * (norm[...] - (xf * scaling) * mean)
        ).astype(BF16)


def place_of(place, p, side):
    dz = lax.rem(p // (ALONG * CORES) - place[0] + ALONG, ALONG)
    dy = lax.rem(lax.rem(p // CORES, ALONG) - place[1] + ALONG, ALONG)
    other = lax.rem(lax.rem(p, CORES) + side, CORES)
    return (dz, dy, other) if side == UP else (dy, dz, other)


def column(ref, p):
    tokens = ref.shape[0] * ref.shape[1]
    return ref[:, :, pl.ds(pl.multiple_of(p * TILE, TILE), TILE)].reshape(tokens, TILE)


def of_hidden(ref, q):
    return ref[:, pl.ds(q, 1)].reshape(ref.shape[0] * ref.shape[2], TILE)


def latent(ref, kind):
    return ref[:, kind, :, 0:RANK].reshape(ref.shape[0] * ref.shape[2], RANK)


def put_low(out, where, low):
    for i in range(PER_ROW):
        rows = slice(HIDDEN + RANK * i, HIDDEN + RANK * (i + 1))
        out[(*where, rows, slice(None))] = low[:, i * TILE : (i + 1) * TILE].astype(BF16)


def down_grads(place, dnq, gs, act, flat, blat, out):
    blocks = gs.shape[2] // TILE
    down_latent, grad_down_latent = latent(flat, 1), latent(blat, 1)

    def one(p, carry):
        where = place_of(place, p, DOWN)
        g = column(gs, p)
        for i in range(PER_ROW):
            product = mm_tn(of_hidden(act, dnq[PER_ROW * p + i]), g)
            out[(*where, slice(i * TILE, (i + 1) * TILE), slice(None))] = product.astype(BF16)
        out[(*where, slice(MODEL, HIDDEN), slice(None))] = mm_tn(down_latent, g).astype(BF16)
        here = lanes([of_hidden(act, PER_ROW * p + i) for i in range(PER_ROW)])
        put_low(out, where, mm_tn(grad_down_latent, here))
        return carry

    lax.fori_loop(0, blocks, one, 0, unroll=2)


def up_grads(place, upq, xs, gp, flat, blat, out, normed):
    blocks = xs.shape[2] // TILE
    xf, scaling = normalised(xs)
    normed[...] = (xf * scaling).astype(BF16)
    up_latent, grad_up_latent = latent(flat, 0), latent(blat, 0)

    def one(p, carry):
        where = place_of(place, p, UP)
        n = column(normed, p)
        there = lanes([of_hidden(gp, upq[PER_ROW * p + i]) for i in range(PER_ROW)])
        product = mm_tn(n, there)
        for i in range(PER_ROW):
            out[(*where, slice(i * TILE, (i + 1) * TILE), slice(None))] = product[
                :, i * TILE : (i + 1) * TILE
            ].astype(BF16)
        out[(*where, slice(MODEL, HIDDEN), slice(None))] = mm_tn(grad_up_latent, n).astype(BF16)
        here = lanes([of_hidden(gp, PER_ROW * p + i) for i in range(PER_ROW)])
        put_low(out, where, mm_tn(up_latent, here))
        return carry

    lax.fori_loop(0, blocks, one, 0, unroll=2)


def grads_kernel(keep, place, upq, dnq, xs, gs, act, gp, flat, blat, out, normed):
    core = place[2]

    @pl.when(core == (UP if keep else DOWN))
    def _():
        up_grads(place, upq, xs, gp, flat, blat, out, normed)

    @pl.when(core == (DOWN if keep else UP))
    def _():
        down_grads(place, dnq, gs, act, flat, blat, out)


def pack_kernel(
    place, up_blocks, up_left, up_right, down_blocks, down_left, down_right, mine, other
):
    for side, tiles, model, hidden in (
        (UP, up_blocks, up_left, up_right),
        (DOWN, down_blocks, down_right, down_left),
    ):
        for out, core in ((mine, side), (other, 1 - side)):

            @pl.when(place[2] == core)
            def _():
                for i in range(PER_ROW):
                    out[i * TILE : (i + 1) * TILE, :] = tiles[i]
                out[MODEL:HIDDEN, :] = model[...]
                for i in range(PER_ROW):
                    rows = slice(HIDDEN + RANK * i, HIDDEN + RANK * (i + 1))
                    out[rows, :] = hidden[:, i * TILE : (i + 1) * TILE]


def stack_kernel(*refs):
    for d, piece in enumerate(refs[:-1]):
        refs[-1][d] = piece[...]


def spread_kernel(place, *refs):
    mine, other, sides = refs[:ALONG], refs[ALONG : 2 * ALONG], refs[2 * ALONG :]
    z, y, core = place[0], place[1], place[2]
    for side, out in zip((UP, DOWN), sides):
        for pieces, holder in ((mine, side), (other, 1 - side)):

            @pl.when(core == holder)
            def _():
                for outer in range(ALONG):
                    for inner in range(ALONG):
                        dz, dy = (outer, inner) if side == UP else (inner, outer)
                        back_z = lax.rem(z - dz + ALONG, ALONG)
                        back_y = lax.rem(y - dy + ALONG, ALONG)
                        chip = back_z * ALONG + back_y
                        for far in range(CORES):
                            out[chip * CORES + (side + far) % CORES] = pieces[outer][inner, far]


def add_cores_kernel(mine, came, *outs):
    for outer, out in enumerate(outs):
        for inner in range(ALONG):
            total = mine[outer, inner].astype(F32) + came[outer, inner].astype(F32)
            out[inner] = total.astype(BF16)


def add_far_kernel(*refs):
    terms, outs = refs[:ALONG], refs[ALONG:]
    for inner, out in enumerate(outs):
        total = terms[0][inner].astype(F32)
        for came in terms[1:]:
            total += came[inner].astype(F32)
        out[...] = total.astype(BF16)


def add_last_kernel(*refs):
    terms, outs = refs[:ALONG], refs[ALONG:]
    for far, out in enumerate(outs):
        total = terms[0][far].astype(F32)
        for came in terms[1:]:
            total += came[far].astype(F32)
        out[...] = total


def finish_kernel(place, mine, other, *outs):
    for side, (tiles, model, hidden) in ((UP, outs[:3]), (DOWN, outs[3:])):
        for total, core in ((mine, side), (other, 1 - side)):

            @pl.when(place[2] == core)
            def _():
                for i in range(PER_ROW):
                    tiles[i] = total[i * TILE : (i + 1) * TILE, :]
                model[...] = total[MODEL:HIDDEN, :]
                for i in range(PER_ROW):
                    rows = slice(HIDDEN + RANK * i, HIDDEN + RANK * (i + 1))
                    hidden[:, i * TILE : (i + 1) * TILE] = total[rows, :]


SMEM = pl.BlockSpec(memory_space=pltpu.SMEM)
VMEM = pl.BlockSpec(memory_space=pltpu.VMEM)
HBM = pl.BlockSpec(memory_space=pl.ANY)


def near(array):
    return pltpu.with_memory_space_constraint(array, pltpu.VMEM)


def forward_call(moment, place, upq, dnq, inputs, incoming, packed, kept):
    rows, width = incoming.shape
    hidden = packed[0].shape[0] * PER_ROW
    return pl.pallas_call(
        partial(forward_kernel, moment),
        out_shape=(pltpu.VMEM(incoming.shape, BF16),)
        + tuple(pltpu.VMEM(item.shape, item.dtype) for item in kept),
        in_specs=[SMEM] * 3 + [VMEM] * (4 + len(kept)),
        out_specs=(VMEM,) * (1 + len(kept)),
        input_output_aliases={7 + i: 1 + i for i in range(len(kept))},
        scratch_shapes=[pltpu.VMEM((hidden, rows, TILE), F32)],
        compiler_params=pltpu.CompilerParams(vmem_limit_bytes=LAYER_VMEM),
        cost_estimate=pl.CostEstimate(flops=10**9, bytes_accessed=10**7, transcendentals=0),
        name="layer_forward",
    )(place, upq, dnq, *map(near, (inputs, incoming, *packed, *kept)))


def backward_call(moment, sections, place, upq, dnq, cotangent, incoming, packed, xs, kept):
    rows, width = incoming.shape
    hidden = packed[0].shape[0] * PER_ROW
    return pl.pallas_call(
        partial(backward_kernel, moment, sections),
        out_shape=(pltpu.VMEM(incoming.shape, BF16),)
        + tuple(pltpu.VMEM(item.shape, item.dtype) for item in kept),
        in_specs=[SMEM] * 3 + [VMEM] * (5 + len(kept)),
        out_specs=(VMEM,) * (1 + len(kept)),
        input_output_aliases={8 + i: 1 + i for i in range(len(kept))},
        scratch_shapes=[pltpu.VMEM((hidden, rows, TILE), F32), pltpu.VMEM((rows, width), F32)],
        compiler_params=pltpu.CompilerParams(vmem_limit_bytes=LAYER_VMEM),
        cost_estimate=pl.CostEstimate(flops=10**9, bytes_accessed=10**7, transcendentals=0),
        name="layer_backward",
    )(place, upq, dnq, *map(near, (cotangent, incoming, *packed, xs, *kept)))


def near_call(kernel, name, shapes, scalars, arrays, scratch=(), far=False):
    specs = [SMEM] * len(scalars) + [VMEM] * len(arrays)
    made = jax.ShapeDtypeStruct if far else pltpu.VMEM
    return pl.pallas_call(
        kernel,
        out_shape=tuple(made(*shape) for shape in shapes),
        in_specs=specs,
        out_specs=(VMEM,) * len(shapes),
        scratch_shapes=list(scratch),
        compiler_params=pltpu.CompilerParams(vmem_limit_bytes=SMALL_VMEM),
        name=name,
    )(*scalars, *map(near, arrays))


def dp_send(value, *steps):
    def index(z, y, c):
        return ((z % ALONG) * ALONG + y % ALONG) * CORES + c % CORES

    route = []
    for z in range(ALONG):
        for y in range(ALONG):
            for c in range(CORES):
                dz, dy, dc = steps[c % len(steps)]
                route.append((index(z, y, c), index(z + dz, y + dy, c + dc)))
    return lax.ppermute(value, "dp", route)


def swap_cores(value):
    return dp_send(value, (0, 0, 1))


def along_first(value, d):
    return dp_send(value, (0, d, 0), (d, 0, 0))


def along_second(value, d):
    return dp_send(value, (d, 0, 0), (0, d, 0))


FAR = range(1, ALONG)


def gather(place, mine, other):
    side = mine.shape
    pair = near_call(
        stack_kernel, "pair", [((CORES, *side), BF16)], (), (mine, swap_cores(other))
    )[0]
    pairs = [pair] + [along_first(pair, d) for d in FAR]
    line = near_call(stack_kernel, "line", [((ALONG, CORES, *side), BF16)], (), pairs)[0]
    lines = [line] + [along_second(line, d) for d in FAR]
    others = [swap_cores(piece) for piece in lines]
    full = ((CORES * ALONG * ALONG, *side), BF16)
    return near_call(spread_kernel, "spread", (full, full), (place,), lines + others)


def scatter_sum(place, keep, give):
    side = keep.shape[3:]
    line, pair = ((ALONG, CORES, *side), BF16), ((CORES, *side), BF16)
    came = swap_cores(give)
    lines = near_call(add_cores_kernel, "add_cores", [line] * ALONG, (), (keep, came))
    terms = [lines[0]] + [along_second(lines[d], d) for d in FAR]
    pairs = near_call(add_far_kernel, "add_far", [pair] * ALONG, (), terms)
    terms = [pairs[0]] + [along_first(pairs[d], d) for d in FAR]
    mine, other = near_call(add_last_kernel, "add_last", [(side, F32)] * CORES, (), terms)
    three = (((PER_ROW, TILE, TILE), F32), ((RANK, TILE), F32), ((RANK, MODEL), F32))
    return near_call(
        finish_kernel, "finish", three + three, (place,), (mine, swap_cores(other)), far=True
    )


def buffers(after, *shapes):
    shapes = [(shape, BF16) for shape in shapes]
    return near_call(lambda *refs: None, "buffers", shapes, (), (after,))


def per_device(
    inputs, cotangent, up_blocks, up_index, up_left, up_right, down_blocks, down_index,
    down_left, down_right,
):
    sections = lax.axis_size("section")
    micro, rows, width = inputs.shape
    hidden = width // TILE * PER_ROW
    rank = lax.axis_index("dp")
    place = jnp.stack(
        [
            rank // (ALONG * CORES),
            rank // CORES % ALONG,
            rank % CORES,
            lax.axis_index("section"),
        ]
    ).astype(jnp.int32)
    place, upq, dnq = lax.optimization_barrier((place, up_index[0, :, 1], down_index[0, :, 0]))
    side = ((SIDE, TILE), BF16)
    factors = [item[0].T for item in (up_left, up_right, down_left, down_right)]
    packed = gather(
        place,
        *near_call(
            pack_kernel,
            "pack",
            (side, side),
            (place,),
            (up_blocks[0], *factors[:2], down_blocks[0], *factors[2:]),
        ),
    )

    wide, tall, thin = (micro, rows, width), (micro, hidden, rows, TILE), (micro, 2, rows, TILE)
    xs, outs, act, slope, flat, arrived, travelling = buffers(
        packed[0], wide, wide, tall, tall, thin, (rows, width), (rows, width)
    )
    moments = micro + 2 * (sections - 1)
    for moment in range(moments):
        result, xs, outs, act, slope, flat = forward_call(
            moment, place, upq, dnq, inputs, arrived, packed, (xs, outs, act, slope, flat)
        )
        route = [(s, s + 1) for s in range(sections - 1) if 0 <= moment - 2 * s < micro]
        arrived = travelling
        if route:
            travelling = lax.ppermute(result, "section", route)

    gs, blat, arrived, travelling = buffers(act, wide, thin, (rows, width), (rows, width))
    gp = slope
    for moment in range(moments):
        result, gs, gp, blat = backward_call(
            moment, sections, place, upq, dnq, cotangent, arrived, packed, xs, (gs, gp, blat)
        )
        route = [
            (s, s - 1) for s in range(1, sections) if 0 <= moment - 2 * (sections - 1 - s) < micro
        ]
        arrived = travelling
        if route:
            travelling = lax.ppermute(result, "section", route)

    terms = [
        near_call(
            partial(grads_kernel, keep),
            "grads",
            [((ALONG, ALONG, CORES, SIDE, TILE), BF16)],
            (place, upq, dnq),
            (xs, gs, act, gp, flat, blat),
            (pltpu.VMEM(wide, BF16),),
        )[0]
        for keep in (False, True)
    ]
    up_grad, up_left_grad, up_right_grad, down_grad, down_right_grad, down_left_grad = scatter_sum(
        place, terms[1], terms[0]
    )
    return (
        outs[None],
        up_grad[None],
        up_left_grad.T[None],
        up_right_grad.T[None],
        down_grad[None],
        down_left_grad.T[None],
        down_right_grad.T[None],
    )


def solution(mesh):
    in_specs = (
        P(None, "dp", None),
        P(None, "dp", None),
        P("section", "dp", None, None),
        P("section", None, None),
        P("section", "dp", None),
        P("section", "dp", None),
        P("section", "dp", None, None),
        P("section", None, None),
        P("section", "dp", None),
        P("section", "dp", None),
    )
    out_specs = (
        P("section", None, "dp", None),
        P("section", "dp", None, None),
        P("section", "dp", None),
        P("section", "dp", None),
        P("section", "dp", None, None),
        P("section", "dp", None),
        P("section", "dp", None),
    )
    return jax.shard_map(
        per_device, mesh=mesh, in_specs=in_specs, out_specs=out_specs, check_vma=False
    )
```

time: 694 us -> 529 us (0.76)
  waiting for transfers between devices: 453 us -> 133 us
  starting transfers between devices: 26.9 us -> 255 us
  local copies, waits for them, and re-layouts: 55.5 us -> 8.72 us
  between operations: 15.5 us -> 1.9 us
  Pallas kernels: 128 us -> 119 us
    ppermute x20 -> x51, starting transfers between devices: 26.8 us -> 255 us  [the longest x32 153 us: per_device(): travelling = lax.ppermute(result, 'section', route)]
    reduce_scatter x1 -> x0, waiting for transfers between devices: 146 us -> none  [scatter_sum(): return lax.psum_scatter(terms, 'dp', scatter_dimension=0)]
    ppermute x20 -> x51, waiting for transfers between devices: 227 us -> 133 us  [the longest x19 84.7 us: dp_send(): return lax.ppermute(value, 'dp', route)]
    all_gather x1 -> x0, waiting for transfers between devices: 80.9 us -> none  [gather(): return lax.all_gather(packed, 'dp', axis=0)]
    unnamed x115 -> x17, local copies, waits for them, and re-layouts: 47.2 us -> 8.02 us
    pallas_call x24 -> x48, Pallas kernels: 128 us -> 119 us  [the longest x18 62.1 us: backward_call(): pl.pallas_call(partial(backward_kernel, moment, sections), out_shape=(plt...]
  transfers between devices with their start and end apart: 22 -> 51, of which waited for: 10 -> 15; matrix products, arithmetic and copies ran while one was open for 0% -> 0% of each run, Pallas kernels for 0% -> 17%
where the time goes in v2:
time: 529 us; the launch traced here: 518 us
  starting transfers between devices  255 us (48%)
  waiting for transfers between devices  133 us (25%)
  Pallas kernels  119 us (22%)
  local copies, waits for them, and re-layouts  8.72 us (2%)
    ppermute x32, starting transfers between devices, per_device(): travelling = lax.ppermute(result, 'section', route)  153 us
    ppermute x19, starting transfers between devices, dp_send(): return lax.ppermute(value, 'dp', route)  102 us
    ppermute x19, waiting for transfers between devices, dp_send(): return lax.ppermute(value, 'dp', route)  84.7 us
    pallas_call x18, Pallas kernels, backward_call(): pl.pallas_call(partial(backward_kernel, moment, sections), out_shape=(plt...  62.1 us
    ppermute x32, waiting for transfers between devices, per_device(): travelling = lax.ppermute(result, 'section', route)  48.2 us
    pallas_call x18, Pallas kernels, forward_call(): pl.pallas_call(partial(forward_kernel, moment), out_shape=(pltpu.VMEM(inc...  40.5 us
    pallas_call x12, Pallas kernels, near_call(): pl.pallas_call(kernel, out_shape=tuple((made(*shape) for shape in shapes)...  16.6 us
  transfers between devices with their start and end apart: 51, of which 15 were waited for; matrix products, arithmetic and copies ran while one was open for 0% of the time, Pallas kernels for 17%

profile of v2, /device:TPU:65, one launch (start us, length us, event | category | flops | bytes accessed | tf_op | source)
XLA Modules:
  0.0 518.1 jit_solution(14125059097252963452)
XLA Ops:
  21.0 5.8 %collective-permute-done.1.refs_1_ = bf16[2,592,128]{2,1,0:T(8,128)(2,1)S(1)} collective-permute-done((bf16[2,592,128]{2,1,0:T(8,128)(2,1)S(1)}, bf16[2,592,128]{2,1,0:T(8,128)(2,1)S(1)}, u32[]{:S(2)}, u32[]{:S(2)}) %collective-permute-start.1) | collective-permute-done | bytes 303136 | tf_op jit(solution)/shard_map/ppermute | solution.py:436
  33.2 23.4 %collective-permute-done.6.refs_3_ = bf16[4,2,592,128]{3,2,1,0:T(8,128)(2,1)S(1)} collective-permute-done((bf16[4,2,592,128]{3,2,1,0:T(8,128)(2,1)S(1)}, bf16[4,2,592,128]{3,2,1,0:T(8,128)(2,1)S(1)}, u32[]{:S(2)}, u32[]{:S(2)}) %collective-permute-start.6) | collective-permute-done | bytes 1212448 | tf_op jit(solution)/shard_map/ppermute | solution.py:436
  56.6 34.9 %collective-permute-start.10 = (bf16[4,2,592,128]{3,2,1,0:T(8,128)(2,1)S(1)}, bf16[4,2,592,128]{3,2,1,0:T(8,128)(2,1)S(1)}, u32[]{:S(2)}, u32[]{:S(2)}) collective-permute-start(bf16[4,2,592,128]{3,2,1,0:T(8,128)(2,1)S(1)} %collective-permute-done.6.refs_3_), channel_id=1, source_target_pairs={{0,1},{1,0},{2,3},{3,2},{4,5},{5,4},{6,7},{7,6},{8,9},{9,8},{10,11... | collective-permute-start | bytes 3637256 | tf_op jit(solution)/shard_map/ppermute | solution.py:436
  91.4 11.8 %collective-permute-start.9 = (bf16[4,2,592,128]{3,2,1,0:T(8,128)(2,1)S(1)}, bf16[4,2,592,128]{3,2,1,0:T(8,128)(2,1)S(1)}, u32[]{:S(2)}, u32[]{:S(2)}) collective-permute-start(bf16[4,2,592,128]{3,2,1,0:T(8,128)(2,1)S(1)} %collective-permute-done.5.refs_2_), channel_id=1, source_target_pairs={{0,1},{1,0},{2,3},{3,2},{4,5},{5,4},{6,7},{7,6},{8,9},{9,8},{10,11... | collective-permute-start | bytes 3637256 | tf_op jit(solution)/shard_map/ppermute | solution.py:436
  103.3 11.8 %collective-permute-start.8 = (bf16[4,2,592,128]{3,2,1,0:T(8,128)(2,1)S(1)}, bf16[4,2,592,128]{3,2,1,0:T(8,128)(2,1)S(1)}, u32[]{:S(2)}, u32[]{:S(2)}) collective-permute-start(bf16[4,2,592,128]{3,2,1,0:T(8,128)(2,1)S(1)} %collective-permute-done.4.refs_1_), channel_id=1, source_target_pairs={{0,1},{1,0},{2,3},{3,2},{4,5},{5,4},{6,7},{7,6},{8,9},{9,8},{10,11... | collective-permute-start | bytes 3637256 | tf_op jit(solution)/shard_map/ppermute | solution.py:436
  156.3 10.7 %layer_forward.25 = (bf16[32,4096]{1,0:T(8,128)(2,1)S(1)}, bf16[4,32,4096]{2,1,0:T(8,128)(2,1)S(1)}, bf16[4,32,4096]{2,1,0:T(8,128)(2,1)S(1)}, bf16[4,128,32,128...) custom-call(s32[4]{0:T(128)S(1)} %pad_add_fusion.place, ...), custom_call_target="tpu_custom_call", output_to_operand_aliasing={{1}: (7, {}), {2}: (8, {}), {3}: (9, {}), {4}: (10, {}), {5... | custom-call | flops 1000000000 | bytes 10000000 | tf_op jit(solution)/shard_map/layer_forward/pallas_call | solution.py:381
  173.4 55.1 %collective-permute-start.24 = (bf16[32,4096]{1,0:T(8,128)(2,1)S(1)}, bf16[32,4096]{1,0:T(8,128)(2,1)S(1)}, u32[]{:S(2)}, u32[]{:S(2)}) collective-permute-start(bf16[32,4096]{1,0:T(8,128)(2,1)S(1)} %get-tuple-element.309), channel_id=1, source_target_pairs={{160,192},{192,224},{161,193},{193,225},{162,194},{194,226},{163,1... | collective-permute-start | bytes 786440 | tf_op jit(solution)/shard_map/ppermute | solution.py:529
  236.3 8.7 %layer_backward.18 = (bf16[32,4096]{1,0:T(8,128)(2,1)S(1)}, bf16[4,32,4096]{2,1,0:T(8,128)(2,1)S(1)}, bf16[4,128,32,128]{3,2,1,0:T(8,128)(2,1)S(1)}, bf16[4,2,32,128]{3,2,1,0:T(8,128)(2,1)S(1)}) custom-call(s32[4]{0:T(128)S(1)} %pad_add_fusion.place, s32[128]{0:T(128)S(1)} %get-tuple-element.218.upq, ...), custom_call_target="tpu_custom_call", output_to_operand_aliasing={{1}: (8, {}), {2}: (9, {}), {3}: (10, {})} | custom-call | flops 1000000000 | bytes 10000000 | tf_op jit(solution)/shard_map/layer_backward/pallas_call | solution.py:398
  247.6 53.0 %collective-permute-start.30 = (bf16[32,4096]{1,0:T(8,128)(2,1)S(1)}, bf16[32,4096]{1,0:T(8,128)(2,1)S(1)}, u32[]{:S(2)}, u32[]{:S(2)}) collective-permute-start(bf16[32,4096]{1,0:T(8,128)(2,1)S(1)} %get-tuple-element.352), channel_id=1, source_target_pairs={{192,160},{224,192},{193,161},{225,193},{194,162},{226,194},{195,1... | collective-permute-start | bytes 786440 | tf_op jit(solution)/shard_map/ppermute | solution.py:542
  301.1 17.8 %collective-permute-start.29 = (bf16[32,4096]{1,0:T(8,128)(2,1)S(1)}, bf16[32,4096]{1,0:T(8,128)(2,1)S(1)}, u32[]{:S(2)}, u32[]{:S(2)}) collective-permute-start(bf16[32,4096]{1,0:T(8,128)(2,1)S(1)} %get-tuple-element.351), channel_id=1, source_target_pairs={{192,160},{224,192},{193,161},{225,193},{194,162},{226,194},{195,1... | collective-permute-start | bytes 786440 | tf_op jit(solution)/shard_map/ppermute | solution.py:542
  320.2 8.6 %layer_backward.23 = (bf16[32,4096]{1,0:T(8,128)(2,1)S(1)}, bf16[4,32,4096]{2,1,0:T(8,128)(2,1)S(1)}, bf16[4,128,32,128]{3,2,1,0:T(8,128)(2,1)S(1)}, bf16[4,2,32,128]{3,2,1,0:T(8,128)(2,1)S(1)}) custom-call(s32[4]{0:T(128)S(1)} %pad_add_fusion.place, s32[128]{0:T(128)S(1)} %get-tuple-element.218.upq, ...), custom_call_target="tpu_custom_call", output_to_operand_aliasing={{1}: (8, {}), {2}: (9, {}), {3}: (10, {})} | custom-call | flops 1000000000 | bytes 10000000 | tf_op jit(solution)/shard_map/layer_backward/pallas_call | solution.py:398
  334.5 8.8 %layer_backward.28 = (bf16[32,4096]{1,0:T(8,128)(2,1)S(1)}, bf16[4,32,4096]{2,1,0:T(8,128)(2,1)S(1)}, bf16[4,128,32,128]{3,2,1,0:T(8,128)(2,1)S(1)}, bf16[4,2,32,128]{3,2,1,0:T(8,128)(2,1)S(1)}) custom-call(s32[4]{0:T(128)S(1)} %pad_add_fusion.place, s32[128]{0:T(128)S(1)} %get-tuple-element.218.upq, ...), custom_call_target="tpu_custom_call", output_to_operand_aliasing={{1}: (8, {}), {2}: (9, {}), {3}: (10, {})} | custom-call | flops 1000000000 | bytes 10000000 | tf_op jit(solution)/shard_map/layer_backward/pallas_call | solution.py:398
  349.0 43.2 %collective-permute-done.40.incoming = bf16[32,4096]{1,0:T(8,128)(2,1)S(1)} collective-permute-done((bf16[32,4096]{1,0:T(8,128)(2,1)S(1)}, bf16[32,4096]{1,0:T(8,128)(2,1)S(1)}, u32[]{:S(2)}, u32[]{:S(2)}) %collective-permute-start.40) | collective-permute-done | bytes 262176 | tf_op jit(solution)/shard_map/ppermute | solution.py:542
  392.2 5.8 %layer_backward.32 = (bf16[32,4096]{1,0:T(8,128)(2,1)S(1)}, bf16[4,32,4096]{2,1,0:T(8,128)(2,1)S(1)}, bf16[4,128,32,128]{3,2,1,0:T(8,128)(2,1)S(1)}, bf16[4,2,32,128]{3,2,1,0:T(8,128)(2,1)S(1)}) custom-call(s32[4]{0:T(128)S(1)} %pad_add_fusion.place, s32[128]{0:T(128)S(1)} %get-tuple-element.218.upq, ...), custom_call_target="tpu_custom_call", output_to_operand_aliasing={{1}: (8, {}), {2}: (9, {}), {3}: (10, {})} | custom-call | flops 1000000000 | bytes 10000000 | tf_op jit(solution)/shard_map/layer_backward/pallas_call | solution.py:398
  400.0 10.9 %layer_backward.33 = (bf16[32,4096]{1,0:T(8,128)(2,1)S(1)}, bf16[4,32,4096]{2,1,0:T(8,128)(2,1)S(1)}, bf16[4,128,32,128]{3,2,1,0:T(8,128)(2,1)S(1)}, bf16[4,2,32,128]{3,2,1,0:T(8,128)(2,1)S(1)}) custom-call(s32[4]{0:T(128)S(1)} %pad_add_fusion.place, s32[128]{0:T(128)S(1)} %get-tuple-element.218.upq, ...), custom_call_target="tpu_custom_call", output_to_operand_aliasing={{1}: (8, {}), {2}: (9, {}), {3}: (10, {})} | custom-call | flops 1000000000 | bytes 10000000 | tf_op jit(solution)/shard_map/layer_backward/pallas_call | solution.py:398
  412.2 6.5 %layer_backward.34 = (bf16[32,4096]{1,0:T(8,128)(2,1)}, bf16[4,32,4096]{2,1,0:T(8,128)(2,1)S(1)}, bf16[4,128,32,128]{3,2,1,0:T(8,128)(2,1)S(1)}, bf16[4,2,32,128]{3,2,1,0:T(8,128)(2,1)S(1)}) custom-call(s32[4]{0:T(128)S(1)} %pad_add_fusion.place, s32[128]{0:T(128)S(1)} %get-tuple-element.218.upq, ...), custom_call_target="tpu_custom_call", output_to_operand_aliasing={{1}: (8, {}), {2}: (9, {}), {3}: (10, {})} | custom-call | flops 1000000000 | bytes 10000000 | tf_op jit(solution)/shard_map/layer_backward/pallas_call | solution.py:398
  419.4 6.5 %layer_backward.35 = (bf16[32,4096]{1,0:T(8,128)(2,1)}, bf16[4,32,4096]{2,1,0:T(8,128)(2,1)S(1)}, bf16[4,128,32,128]{3,2,1,0:T(8,128)(2,1)S(1)}, bf16[4,2,32,128]{3,2,1,0:T(8,128)(2,1)S(1)}) custom-call(s32[4]{0:T(128)S(1)} %pad_add_fusion.place, s32[128]{0:T(128)S(1)} %get-tuple-element.218.upq, ...), custom_call_target="tpu_custom_call", output_to_operand_aliasing={{1}: (8, {}), {2}: (9, {}), {3}: (10, {})} | custom-call | flops 1000000000 | bytes 10000000 | tf_op jit(solution)/shard_map/layer_backward/pallas_call | solution.py:398
  425.9 5.9 %grads.3 = bf16[4,4,2,592,128]{4,3,2,1,0:T(8,128)(2,1)S(1)} custom-call(s32[4]{0:T(128)S(1)} %pad_add_fusion.place, s32[128]{0:T(128)S(1)} %get-tuple-element.218.upq, s32[128]{0:T(128)S(1)} %get-tuple-element.219.dnq, bf16[4,32,4096]{2,1,0:T(8,128)(2,1)S(1)} %get-tuple-element.333.xs, bf16[4,32,4096]{2,1,0:T(8,128)(2,1)S(1)} %get-tuple-element.407.gs, ...), custom_call_target="tpu_custom_call" | custom-call | tf_op jit(solution)/shard_map/grads/pallas_call | solution.py:415
  435.5 5.5 %grads.2.mine = bf16[4,4,2,592,128]{4,3,2,1,0:T(8,128)(2,1)S(1)} custom-call(s32[4]{0:T(128)S(1)} %pad_add_fusion.place, s32[128]{0:T(128)S(1)} %get-tuple-element.218.upq, s32[128]{0:T(128)S(1)} %get-tuple-element.219.dnq, bf16[4,32,4096]{2,1,0:T(8,128)(2,1)S(1)} %get-tuple-element.333.xs, bf16[4,32,4096]{2,1,0:T(8,128)(2,1)S(1)} %get-tuple-element.407.gs, ...), custom_call_target="tpu_custom_call" | custom-call | tf_op jit(solution)/shard_map/grads/pallas_call | solution.py:415
  449.3 12.0 %collective-permute-done.44.refs_1_ = bf16[4,2,592,128]{3,2,1,0:T(8,128)(2,1)S(1)} collective-permute-done((bf16[4,2,592,128]{3,2,1,0:T(8,128)(2,1)S(1)}, bf16[4,2,592,128]{3,2,1,0:T(8,128)(2,1)S(1)}, u32[]{:S(2)}, u32[]{:S(2)}) %collective-permute-start.44) | collective-permute-done | bytes 1212448 | tf_op jit(solution)/shard_map/ppermute | solution.py:436
  461.3 14.1 %collective-permute-done.45.refs_2_ = bf16[4,2,592,128]{3,2,1,0:T(8,128)(2,1)S(1)} collective-permute-done((bf16[4,2,592,128]{3,2,1,0:T(8,128)(2,1)S(1)}, bf16[4,2,592,128]{3,2,1,0:T(8,128)(2,1)S(1)}, u32[]{:S(2)}, u32[]{:S(2)}) %collective-permute-start.45) | collective-permute-done | bytes 1212448 | tf_op jit(solution)/shard_map/ppermute | solution.py:436
  481.9 6.3 %collective-permute-done.47.refs_1_ = bf16[2,592,128]{2,1,0:T(8,128)(2,1)S(1)} collective-permute-done((bf16[2,592,128]{2,1,0:T(8,128)(2,1)S(1)}, bf16[2,592,128]{2,1,0:T(8,128)(2,1)S(1)}, u32[]{:S(2)}, u32[]{:S(2)}) %collective-permute-start.47) | collective-permute-done | bytes 303136 | tf_op jit(solution)/shard_map/ppermute | solution.py:436
  488.2 13.2 %collective-permute-done.48.refs_2_ = bf16[2,592,128]{2,1,0:T(8,128)(2,1)S(1)} collective-permute-done((bf16[2,592,128]{2,1,0:T(8,128)(2,1)S(1)}, bf16[2,592,128]{2,1,0:T(8,128)(2,1)S(1)}, u32[]{:S(2)}, u32[]{:S(2)}) %collective-permute-start.48) | collective-permute-done | bytes 303136 | tf_op jit(solution)/shard_map/ppermute | solution.py:436
  501.5 13.5 %collective-permute-start.50 = (f32[592,128]{1,0:T(8,128)S(1)}, f32[592,128]{1,0:T(8,128)S(1)}, u32[]{:S(2)}, u32[]{:S(2)}) collective-permute-start(f32[592,128]{1,0:T(8,128)S(1)} %get-tuple-element.420), channel_id=1, source_target_pairs={{0,1},{1,0},{2,3},{3,2},{4,5},{5,4},{6,7},{7,6},{8,9},{9,8},{10,11... | collective-permute-start | bytes 909320 | tf_op jit(solution)/shard_map/ppermute | solution.py:436
  (145 shorter events, 122.3 us)
Async XLA Ops:
  8.5 12.6 %collective-permute-start.3 = (bf16[2,592,128]{2,1,0:T(8,128)(2,1)S(1)}, bf16[2,592,128]{2,1,0:T(8,128)(2,1)S(1)}, u32[]{:S(2)}, u32[]{:S(2)}) collective-permute-start(bf16[2,592,128]{2,1,0:T(8,128)(2,1)S(1)} %pair.1.refs_0_), channel_id=1, source_target_pairs={{0,6},{1,25},{2,0},{3,27},{4,2},{5,29},{6,4},{7,31},{8,14},{9,1},{... | collective-permute-start | bytes 909320 | tf_op jit(solution)/shard_map/ppermute | solution.py:436
  26.9 29.7 %collective-permute-start.6 = (bf16[4,2,592,128]{3,2,1,0:T(8,128)(2,1)S(1)}, bf16[4,2,592,128]{3,2,1,0:T(8,128)(2,1)S(1)}, u32[]{:S(2)}, u32[]{:S(2)}) collective-permute-start(bf16[4,2,592,128]{3,2,1,0:T(8,128)(2,1)S(1)} %line.1.refs_0_), channel_id=1, source_target_pairs={{0,24},{1,7},{2,26},{3,1},{4,28},{5,3},{6,30},{7,5},{8,0},{9,15},{... | collective-permute-start | bytes 3637256 | tf_op jit(solution)/shard_map/ppermute | solution.py:436
  30.1 61.3 %collective-permute-start.5 = (bf16[4,2,592,128]{3,2,1,0:T(8,128)(2,1)S(1)}, bf16[4,2,592,128]{3,2,1,0:T(8,128)(2,1)S(1)}, u32[]{:S(2)}, u32[]{:S(2)}) collective-permute-start(bf16[4,2,592,128]{3,2,1,0:T(8,128)(2,1)S(1)} %line.1.refs_0_), channel_id=1, source_target_pairs={{0,16},{1,5},{2,18},{3,7},{4,20},{5,1},{6,22},{7,3},{8,24},{9,13},... | collective-permute-start | bytes 3637256 | tf_op jit(solution)/shard_map/ppermute | solution.py:436
  30.4 72.8 %collective-permute-start.4 = (bf16[4,2,592,128]{3,2,1,0:T(8,128)(2,1)S(1)}, bf16[4,2,592,128]{3,2,1,0:T(8,128)(2,1)S(1)}, u32[]{:S(2)}, u32[]{:S(2)}) collective-permute-start(bf16[4,2,592,128]{3,2,1,0:T(8,128)(2,1)S(1)} %line.1.refs_0_), channel_id=1, source_target_pairs={{0,8},{1,3},{2,10},{3,5},{4,12},{5,7},{6,14},{7,1},{8,16},{9,11},{... | collective-permute-start | bytes 3637256 | tf_op jit(solution)/shard_map/ppermute | solution.py:436
  31.1 84.0 %collective-permute-start.7 = (bf16[4,2,592,128]{3,2,1,0:T(8,128)(2,1)S(1)}, bf16[4,2,592,128]{3,2,1,0:T(8,128)(2,1)S(1)}, u32[]{:S(2)}, u32[]{:S(2)}) collective-permute-start(bf16[4,2,592,128]{3,2,1,0:T(8,128)(2,1)S(1)} %line.1.refs_0_), channel_id=1, source_target_pairs={{0,1},{1,0},{2,3},{3,2},{4,5},{5,4},{6,7},{7,6},{8,9},{9,8},{10,11... | collective-permute-start | bytes 3637256 | tf_op jit(solution)/shard_map/ppermute | solution.py:436
  56.6 58.5 %collective-permute-start.10 = (bf16[4,2,592,128]{3,2,1,0:T(8,128)(2,1)S(1)}, bf16[4,2,592,128]{3,2,1,0:T(8,128)(2,1)S(1)}, u32[]{:S(2)}, u32[]{:S(2)}) collective-permute-start(bf16[4,2,592,128]{3,2,1,0:T(8,128)(2,1)S(1)} %collective-permute-done.6.refs_3_), channel_id=1, source_target_pairs={{0,1},{1,0},{2,3},{3,2},{4,5},{5,4},{6,7},{7,6},{8,9},{9,8},{10,11... | collective-permute-start | bytes 3637256 | tf_op jit(solution)/shard_map/ppermute | solution.py:436
  91.4 23.7 %collective-permute-start.9 = (bf16[4,2,592,128]{3,2,1,0:T(8,128)(2,1)S(1)}, bf16[4,2,592,128]{3,2,1,0:T(8,128)(2,1)S(1)}, u32[]{:S(2)}, u32[]{:S(2)}) collective-permute-start(bf16[4,2,592,128]{3,2,1,0:T(8,128)(2,1)S(1)} %collective-permute-done.5.refs_2_), channel_id=1, source_target_pairs={{0,1},{1,0},{2,3},{3,2},{4,5},{5,4},{6,7},{7,6},{8,9},{9,8},{10,11... | collective-permute-start | bytes 3637256 | tf_op jit(solution)/shard_map/ppermute | solution.py:436
  103.3 14.6 %collective-permute-start.8 = (bf16[4,2,592,128]{3,2,1,0:T(8,128)(2,1)S(1)}, bf16[4,2,592,128]{3,2,1,0:T(8,128)(2,1)S(1)}, u32[]{:S(2)}, u32[]{:S(2)}) collective-permute-start(bf16[4,2,592,128]{3,2,1,0:T(8,128)(2,1)S(1)} %collective-permute-done.4.refs_1_), channel_id=1, source_target_pairs={{0,1},{1,0},{2,3},{3,2},{4,5},{5,4},{6,7},{7,6},{8,9},{9,8},{10,11... | collective-permute-start | bytes 3637256 | tf_op jit(solution)/shard_map/ppermute | solution.py:436
  155.6 12.1 %collective-permute-start.18 = (bf16[32,4096]{1,0:T(8,128)(2,1)S(1)}, bf16[32,4096]{1,0:T(8,128)(2,1)S(1)}, u32[]{:S(2)}, u32[]{:S(2)}) collective-permute-start(bf16[32,4096]{1,0:T(8,128)(2,1)S(1)} %get-tuple-element.273), channel_id=1, source_target_pairs={{64,96},{96,128},{65,97},{97,129},{66,98},{98,130},{67,99},{99,131... | collective-permute-start | bytes 786440 | tf_op jit(solution)/shard_map/ppermute | solution.py:529
  172.1 56.4 %collective-permute-start.21 = (bf16[32,4096]{1,0:T(8,128)(2,1)S(1)}, bf16[32,4096]{1,0:T(8,128)(2,1)S(1)}, u32[]{:S(2)}, u32[]{:S(2)}) collective-permute-start(bf16[32,4096]{1,0:T(8,128)(2,1)S(1)} %get-tuple-element.296), channel_id=1, source_target_pairs={{128,160},{160,192},{129,161},{161,193},{130,162},{162,194},{131,1... | collective-permute-start | bytes 786440 | tf_op jit(solution)/shard_map/ppermute | solution.py:529
  173.4 56.6 %collective-permute-start.24 = (bf16[32,4096]{1,0:T(8,128)(2,1)S(1)}, bf16[32,4096]{1,0:T(8,128)(2,1)S(1)}, u32[]{:S(2)}, u32[]{:S(2)}) collective-permute-start(bf16[32,4096]{1,0:T(8,128)(2,1)S(1)} %get-tuple-element.309), channel_id=1, source_target_pairs={{160,192},{192,224},{161,193},{193,225},{162,194},{194,226},{163,1... | collective-permute-start | bytes 786440 | tf_op jit(solution)/shard_map/ppermute | solution.py:529
  246.3 54.2 %collective-permute-start.27 = (bf16[32,4096]{1,0:T(8,128)(2,1)S(1)}, bf16[32,4096]{1,0:T(8,128)(2,1)S(1)}, u32[]{:S(2)}, u32[]{:S(2)}) collective-permute-start(bf16[32,4096]{1,0:T(8,128)(2,1)S(1)} %get-tuple-element.343), channel_id=1, source_target_pairs={{224,192},{225,193},{226,194},{227,195},{228,196},{229,197},{230,1... | collective-permute-start | bytes 786440 | tf_op jit(solution)/shard_map/ppermute | solution.py:542
  247.6 71.3 %collective-permute-start.30 = (bf16[32,4096]{1,0:T(8,128)(2,1)S(1)}, bf16[32,4096]{1,0:T(8,128)(2,1)S(1)}, u32[]{:S(2)}, u32[]{:S(2)}) collective-permute-start(bf16[32,4096]{1,0:T(8,128)(2,1)S(1)} %get-tuple-element.352), channel_id=1, source_target_pairs={{192,160},{224,192},{193,161},{225,193},{194,162},{226,194},{195,1... | collective-permute-start | bytes 786440 | tf_op jit(solution)/shard_map/ppermute | solution.py:542
  301.1 19.0 %collective-permute-start.29 = (bf16[32,4096]{1,0:T(8,128)(2,1)S(1)}, bf16[32,4096]{1,0:T(8,128)(2,1)S(1)}, u32[]{:S(2)}, u32[]{:S(2)}) collective-permute-start(bf16[32,4096]{1,0:T(8,128)(2,1)S(1)} %get-tuple-element.351), channel_id=1, source_target_pairs={{192,160},{224,192},{193,161},{225,193},{194,162},{226,194},{195,1... | collective-permute-start | bytes 786440 | tf_op jit(solution)/shard_map/ppermute | solution.py:542
  345.8 46.4 %collective-permute-start.40 = (bf16[32,4096]{1,0:T(8,128)(2,1)S(1)}, bf16[32,4096]{1,0:T(8,128)(2,1)S(1)}, u32[]{:S(2)}, u32[]{:S(2)}) collective-permute-start(bf16[32,4096]{1,0:T(8,128)(2,1)S(1)} %get-tuple-element.392), channel_id=1, source_target_pairs={{32,0},{64,32},{33,1},{65,33},{34,2},{66,34},{35,3},{67,35},{36,4}... | collective-permute-start | bytes 786440 | tf_op jit(solution)/shard_map/ppermute | solution.py:542
  347.7 52.3 %collective-permute-start.39 = (bf16[32,4096]{1,0:T(8,128)(2,1)S(1)}, bf16[32,4096]{1,0:T(8,128)(2,1)S(1)}, u32[]{:S(2)}, u32[]{:S(2)}) collective-permute-start(bf16[32,4096]{1,0:T(8,128)(2,1)S(1)} %get-tuple-element.391), channel_id=1, source_target_pairs={{32,0},{64,32},{33,1},{65,33},{34,2},{66,34},{35,3},{67,35},{36,4}... | collective-permute-start | bytes 786440 | tf_op jit(solution)/shard_map/ppermute | solution.py:542
  398.0 14.2 %collective-permute-start.42 = (bf16[32,4096]{1,0:T(8,128)(2,1)S(1)}, bf16[32,4096]{1,0:T(8,128)(2,1)S(1)}, u32[]{:S(2)}, u32[]{:S(2)}) collective-permute-start(bf16[32,4096]{1,0:T(8,128)(2,1)S(1)} %get-tuple-element.400), channel_id=1, source_target_pairs={{32,0},{33,1},{34,2},{35,3},{36,4},{37,5},{38,6},{39,7},{40,8},{41... | collective-permute-start | bytes 786440 | tf_op jit(solution)/shard_map/ppermute | solution.py:542
  444.3 17.0 %collective-permute-start.44 = (bf16[4,2,592,128]{3,2,1,0:T(8,128)(2,1)S(1)}, bf16[4,2,592,128]{3,2,1,0:T(8,128)(2,1)S(1)}, u32[]{:S(2)}, u32[]{:S(2)}) collective-permute-start(bf16[4,2,592,128]{3,2,1,0:T(8,128)(2,1)S(1)} %get-tuple-element.412), channel_id=1, source_target_pairs={{0,8},{1,3},{2,10},{3,5},{4,12},{5,7},{6,14},{7,1},{8,16},{9,11},{... | collective-permute-start | bytes 3637256 | tf_op jit(solution)/shard_map/ppermute | solution.py:436
  445.6 29.7 %collective-permute-start.45 = (bf16[4,2,592,128]{3,2,1,0:T(8,128)(2,1)S(1)}, bf16[4,2,592,128]{3,2,1,0:T(8,128)(2,1)S(1)}, u32[]{:S(2)}, u32[]{:S(2)}) collective-permute-start(bf16[4,2,592,128]{3,2,1,0:T(8,128)(2,1)S(1)} %get-tuple-element.413), channel_id=1, source_target_pairs={{0,16},{1,5},{2,18},{3,7},{4,20},{5,1},{6,22},{7,3},{8,24},{9,13},... | collective-permute-start | bytes 3637256 | tf_op jit(solution)/shard_map/ppermute | solution.py:436
  448.2 27.2 %collective-permute-start.46 = (bf16[4,2,592,128]{3,2,1,0:T(8,128)(2,1)S(1)}, bf16[4,2,592,128]{3,2,1,0:T(8,128)(2,1)S(1)}, u32[]{:S(2)}, u32[]{:S(2)}) collective-permute-start(bf16[4,2,592,128]{3,2,1,0:T(8,128)(2,1)S(1)} %get-tuple-element.414), channel_id=1, source_target_pairs={{0,24},{1,7},{2,26},{3,1},{4,28},{5,3},{6,30},{7,5},{8,0},{9,15},{... | collective-permute-start | bytes 3637256 | tf_op jit(solution)/shard_map/ppermute | solution.py:436
  476.0 12.2 %collective-permute-start.47 = (bf16[2,592,128]{2,1,0:T(8,128)(2,1)S(1)}, bf16[2,592,128]{2,1,0:T(8,128)(2,1)S(1)}, u32[]{:S(2)}, u32[]{:S(2)}) collective-permute-start(bf16[2,592,128]{2,1,0:T(8,128)(2,1)S(1)} %get-tuple-element.416), channel_id=1, source_target_pairs={{0,2},{1,9},{2,4},{3,11},{4,6},{5,13},{6,0},{7,15},{8,10},{9,17},{... | collective-permute-start | bytes 909320 | tf_op jit(solution)/shard_map/ppermute | solution.py:436
  479.0 22.4 %collective-permute-start.48 = (bf16[2,592,128]{2,1,0:T(8,128)(2,1)S(1)}, bf16[2,592,128]{2,1,0:T(8,128)(2,1)S(1)}, u32[]{:S(2)}, u32[]{:S(2)}) collective-permute-start(bf16[2,592,128]{2,1,0:T(8,128)(2,1)S(1)} %get-tuple-element.417), channel_id=1, source_target_pairs={{0,4},{1,17},{2,6},{3,19},{4,0},{5,21},{6,2},{7,23},{8,12},{9,25},... | collective-permute-start | bytes 909320 | tf_op jit(solution)/shard_map/ppermute | solution.py:436
  479.6 21.7 %collective-permute-start.49 = (bf16[2,592,128]{2,1,0:T(8,128)(2,1)S(1)}, bf16[2,592,128]{2,1,0:T(8,128)(2,1)S(1)}, u32[]{:S(2)}, u32[]{:S(2)}) collective-permute-start(bf16[2,592,128]{2,1,0:T(8,128)(2,1)S(1)} %get-tuple-element.418), channel_id=1, source_target_pairs={{0,6},{1,25},{2,0},{3,27},{4,2},{5,29},{6,4},{7,31},{8,14},{9,1},{... | collective-permute-start | bytes 909320 | tf_op jit(solution)/shard_map/ppermute | solution.py:436
  501.5 14.8 %collective-permute-start.50 = (f32[592,128]{1,0:T(8,128)S(1)}, f32[592,128]{1,0:T(8,128)S(1)}, u32[]{:S(2)}, u32[]{:S(2)}) collective-permute-start(f32[592,128]{1,0:T(8,128)S(1)} %get-tuple-element.420), channel_id=1, source_target_pairs={{0,1},{1,0},{2,3},{3,2},{4,5},{5,4},{6,7},{7,6},{8,9},{9,8},{10,11... | collective-permute-start | bytes 909320 | tf_op jit(solution)/shard_map/ppermute | solution.py:436
  (35 other events, 142.5 us)

commit v3 on v2

--- a/solution.py
+++ b/solution.py
@@ -24,6 +24,8 @@
 ALONG = 4
 CORES = 2
 SMALL_VMEM = 12 * 1024 * 1024
+UNROLL = 16
+MOMENT_GROUP = 4
 LAYER_VMEM = 12 * 1024 * 1024
 F32 = jnp.float32
 BF16 = jnp.bfloat16
@@ -65,7 +67,7 @@
 def forward_kernel(
     moment, place, upq, dnq, inputs, incoming, wu, wd, xs_in, outs_in, act_in, slope_in, lat_in,
     y, xs, outs, act, slope, lat,
-    pre,
+    pre, nv,
 ):
     position = place[3]
     live, slot = slot_at(moment - 2 * position, inputs.shape[0])
@@ -83,28 +85,37 @@
         def _():
             xs[slot] = incoming[...]
 
-        x = xs[slot]
-        xf, scaling = normalised(x)
+        xf, scaling = normalised(xs.at[slot])
         normed = (xf * scaling).astype(BF16)
-        up_latent = jnp.zeros((rows, RANK), F32)
-        for j in range(0, blocks, 2):
-            up_latent += mm_nt(
-                normed[:, j * TILE : (j + 2) * TILE],
-                lanes([wu[j + i, MODEL:HIDDEN, :] for i in range(2)]),
-            )
-        up_latent = up_latent.astype(BF16)
+        for p in range(blocks):
+            nv[p] = normed[:, p * TILE : (p + 1) * TILE]
+
+        def to_latent(j, total):
+            pair = lanes([nv[2 * j], nv[2 * j + 1]])
+            factor = lanes([wu[2 * j + i, MODEL:HIDDEN, :] for i in range(2)])
+            return total + mm_nt(pair, factor)
+
+        none = jnp.zeros((rows, RANK), F32)
+        up_latent = lax.fori_loop(0, blocks // 2, to_latent, none, unroll=UNROLL // 2).astype(BF16)
         lat[slot, 0, :, 0:RANK] = up_latent
-        for p in range(blocks):
+
+        def low_rank(p, carry):
             low = mm(up_latent, low_rows(wu, p))
             for i in range(PER_ROW):
                 pre[PER_ROW * p + i] = low[:, i * TILE : (i + 1) * TILE]
-        for p in range(blocks):
-            piece = lanes([wu[p, i * TILE : (i + 1) * TILE, :] for i in range(PER_ROW)])
-            product = mm(normed[:, p * TILE : (p + 1) * TILE], piece)
+            return carry
+
+        lax.fori_loop(0, blocks, low_rank, 0, unroll=UNROLL)
+
+        def up_blocks(p, carry):
+            product = mm(nv[p], lanes([wu[p, i * TILE : (i + 1) * TILE, :] for i in range(PER_ROW)]))
             where = [upq[PER_ROW * p + i] for i in range(PER_ROW)]
             sums = [pre[q] + product[:, i * TILE : (i + 1) * TILE] for i, q in enumerate(where)]
             for q, value in zip(where, sums):
                 pre[q] = value
+            return carry
+
+        lax.fori_loop(0, blocks, up_blocks, 0, unroll=UNROLL)
 
         def gelu(q, carry):
             u = pre[q]
@@ -118,28 +129,32 @@
             return carry
 
         lax.fori_loop(0, hidden, gelu, 0, unroll=8)
-        down_latent = jnp.zeros((rows, RANK), F32)
-        for p in range(blocks):
-            down_latent += mm_nt(
-                lanes([act[slot, PER_ROW * p + i] for i in range(PER_ROW)]),
-                low_rows(wd, p),
+
+        def from_hidden(p, total):
+            return total + mm_nt(
+                lanes([act[slot, PER_ROW * p + i] for i in range(PER_ROW)]), low_rows(wd, p)
             )
-        down_latent = down_latent.astype(BF16)
+
+        down_latent = lax.fori_loop(0, blocks, from_hidden, none, unroll=UNROLL).astype(BF16)
         lat[slot, 1, :, 0:RANK] = down_latent
-        for p in range(blocks):
+
+        def down_blocks(p, carry):
             left = lanes([act[slot, dnq[PER_ROW * p + i]] for i in range(PER_ROW)])
             product = mm(left, wd[p, 0:MODEL, :])
             product += mm(down_latent, wd[p, MODEL:HIDDEN, :])
-            cols = slice(p * TILE, (p + 1) * TILE)
-            result = (x[:, cols].astype(F32) + product).astype(BF16)
+            cols = pl.ds(pl.multiple_of(p * TILE, TILE), TILE)
+            result = (xs[slot, :, cols].astype(F32) + product).astype(BF16)
             y[:, cols] = result
             outs[slot, :, cols] = result
+            return carry
+
+        lax.fori_loop(0, blocks, down_blocks, 0, unroll=UNROLL)
 
 
 def backward_kernel(
     moment, sections, place, upq, dnq, cotangent, incoming, wu, wd, xs, gs_in, slope, lat_in,
     y, gs, gp, lat,
-    ga, norm,
+    ga, norm, unit,
 ):
     position = place[3]
     live, slot = slot_at(moment - 2 * (sections - 1 - position), cotangent.shape[0])
@@ -157,52 +172,64 @@
         def _():
             gs[slot] = incoming[...]
 
-        g = gs[slot]
-        down = jnp.zeros((rows, RANK), F32)
-        for j in range(0, blocks, 2):
-            down += mm_nt(
-                g[:, j * TILE : (j + 2) * TILE],
-                lanes([wd[j + i, MODEL:HIDDEN, :] for i in range(2)]),
-            )
-        down = down.astype(BF16)
+        def columns(p, count=1):
+            return pl.ds(pl.multiple_of(p * TILE, TILE), count * TILE)
+
+        def to_latent(j, total):
+            factor = lanes([wd[2 * j + i, MODEL:HIDDEN, :] for i in range(2)])
+            return total + mm_nt(gs[slot, :, columns(2 * j, 2)], factor)
+
+        none = jnp.zeros((rows, RANK), F32)
+        down = lax.fori_loop(0, blocks // 2, to_latent, none, unroll=UNROLL // 2).astype(BF16)
         lat[slot, 1, :, 0:RANK] = down
-        for p in range(blocks):
+
+        def low_rank(p, carry):
             low = mm(down, low_rows(wd, p))
             for i in range(PER_ROW):
                 ga[PER_ROW * p + i] = low[:, i * TILE : (i + 1) * TILE]
-        for p in range(blocks):
-            product = mm_nt(g[:, p * TILE : (p + 1) * TILE], wd[p, 0:MODEL, :])
+            return carry
+
+        lax.fori_loop(0, blocks, low_rank, 0, unroll=UNROLL)
+
+        def down_blocks(p, carry):
+            product = mm_nt(gs[slot, :, columns(p)], wd[p, 0:MODEL, :])
             where = [dnq[PER_ROW * p + i] for i in range(PER_ROW)]
             sums = [ga[q] + product[:, i * TILE : (i + 1) * TILE] for i, q in enumerate(where)]
             for q, value in zip(where, sums):
                 ga[q] = value
+            return carry
+
+        lax.fori_loop(0, blocks, down_blocks, 0, unroll=UNROLL)
 
         def slopes(q, carry):
             gp[slot, q] = (ga[q] * slope[slot, q].astype(F32)).astype(BF16)
             return carry
 
         lax.fori_loop(0, hidden, slopes, 0, unroll=8)
-        up = jnp.zeros((rows, RANK), F32)
-        for p in range(blocks):
-            up += mm_nt(
-                lanes([gp[slot, PER_ROW * p + i] for i in range(PER_ROW)]),
-                low_rows(wu, p),
+
+        def from_hidden(p, total):
+            return total + mm_nt(
+                lanes([gp[slot, PER_ROW * p + i] for i in range(PER_ROW)]), low_rows(wu, p)
             )
-        up = up.astype(BF16)
+
+        up = lax.fori_loop(0, blocks, from_hidden, none, unroll=UNROLL).astype(BF16)
         lat[slot, 0, :, 0:RANK] = up
-        xf, scaling = normalised(xs[slot])
-        along = jnp.zeros((rows, TILE), F32)
-        for p in range(blocks):
+        xf, scaling = normalised(xs.at[slot])
+        unit[...] = xf * scaling
+
+        def up_blocks(p, along):
             left = lanes([gp[slot, upq[PER_ROW * p + i]] for i in range(PER_ROW)])
             piece = lanes([wu[p, i * TILE : (i + 1) * TILE, :] for i in range(PER_ROW)])
             product = mm_nt(left, piece)
             product += mm(up, wu[p, MODEL:HIDDEN, :])
-            cols = slice(p * TILE, (p + 1) * TILE)
-            norm[:, cols] = product
-            along += product * (xf[:, cols] * scaling)
+            norm[:, columns(p)] = product
+            return along + product * unit[:, columns(p)]
+
+        along = jnp.zeros((rows, TILE), F32)
+        along = lax.fori_loop(0, blocks, up_blocks, along, unroll=UNROLL)
         mean = jnp.sum(along, axis=-1, keepdims=True) * (1.0 / (blocks * TILE))
         y[...] = (
-            g.astype(F32) + scaling * (norm[...] - (xf * scaling) * mean)
+            gs[slot].astype(F32) + scaling * (norm[...] - unit[...] * mean)
         ).astype(BF16)
 
 
@@ -385,7 +412,10 @@
         in_specs=[SMEM] * 3 + [VMEM] * (4 + len(kept)),
         out_specs=(VMEM,) * (1 + len(kept)),
         input_output_aliases={7 + i: 1 + i for i in range(len(kept))},
-        scratch_shapes=[pltpu.VMEM((hidden, rows, TILE), F32)],
+        scratch_shapes=[
+            pltpu.VMEM((hidden, rows, TILE), F32),
+            pltpu.VMEM((hidden // PER_ROW, rows, TILE), BF16),
+        ],
         compiler_params=pltpu.CompilerParams(vmem_limit_bytes=LAYER_VMEM),
         cost_estimate=pl.CostEstimate(flops=10**9, bytes_accessed=10**7, transcendentals=0),
         name="layer_forward",
@@ -402,7 +432,11 @@
         in_specs=[SMEM] * 3 + [VMEM] * (5 + len(kept)),
         out_specs=(VMEM,) * (1 + len(kept)),
         input_output_aliases={8 + i: 1 + i for i in range(len(kept))},
-        scratch_shapes=[pltpu.VMEM((hidden, rows, TILE), F32), pltpu.VMEM((rows, width), F32)],
+        scratch_shapes=[
+            pltpu.VMEM((hidden, rows, TILE), F32),
+            pltpu.VMEM((rows, width), F32),
+            pltpu.VMEM((rows, width), F32),
+        ],
         compiler_params=pltpu.CompilerParams(vmem_limit_bytes=LAYER_VMEM),
         cost_estimate=pl.CostEstimate(flops=10**9, bytes_accessed=10**7, transcendentals=0),
         name="layer_backward",
@@ -482,6 +516,18 @@
 def buffers(after, *shapes):
     shapes = [(shape, BF16) for shape in shapes]
     return near_call(lambda *refs: None, "buffers", shapes, (), (after,))
+
+
+def hops(moment, micro, sections, backward):
+    first = moment // MOMENT_GROUP * MOMENT_GROUP
+    steps = [
+        step
+        for step in range(sections - 1)
+        if any(0 <= first + i - 2 * step < micro for i in range(MOMENT_GROUP))
+    ]
+    if backward:
+        return [(sections - 1 - step, sections - 2 - step) for step in steps]
+    return [(step, step + 1) for step in steps]
 
 
 def per_device(
@@ -523,10 +569,9 @@
         result, xs, outs, act, slope, flat = forward_call(
             moment, place, upq, dnq, inputs, arrived, packed, (xs, outs, act, slope, flat)
         )
-        route = [(s, s + 1) for s in range(sections - 1) if 0 <= moment - 2 * s < micro]
         arrived = travelling
-        if route:
-            travelling = lax.ppermute(result, "section", route)
+        if moment < moments - 2:
+            travelling = lax.ppermute(result, "section", hops(moment, micro, sections, False))
 
     gs, blat, arrived, travelling = buffers(act, wide, thin, (rows, width), (rows, width))
     gp = slope
@@ -534,12 +579,9 @@
         result, gs, gp, blat = backward_call(
             moment, sections, place, upq, dnq, cotangent, arrived, packed, xs, (gs, gp, blat)
         )
-        route = [
-            (s, s - 1) for s in range(1, sections) if 0 <= moment - 2 * (sections - 1 - s) < micro
-        ]
         arrived = travelling
-        if route:
-            travelling = lax.ppermute(result, "section", route)
+        if moment < moments - 2:
+            travelling = lax.ppermute(result, "section", hops(moment, micro, sections, True))
 
     terms = [
         near_call(

time: 529 us -> 458 us (0.87)
  the two profiles are of different devices: /device:TPU:65 before, /device:TPU:1 now
where the time goes in v3:
time: 458 us; the launch traced here: 453 us
  waiting for transfers between devices  235 us (51%)
  starting transfers between devices  116 us (25%)
  Pallas kernels  91.8 us (20%)
  local copies, waits for them, and re-layouts  8.72 us (2%)
    ppermute x16, waiting for transfers between devices, per_device(): lax.ppermute(result, 'section', hops(moment, micro, sections, True))  144 us
    ppermute x19, starting transfers between devices, dp_send(): return lax.ppermute(value, 'dp', route)  86.9 us
    ppermute x19, waiting for transfers between devices, dp_send(): return lax.ppermute(value, 'dp', route)  86.8 us
    pallas_call x18, Pallas kernels, forward_call(): pl.pallas_call(partial(forward_kernel, moment), out_shape=(pltpu.VMEM(inc...  40.3 us
    pallas_call x18, Pallas kernels, backward_call(): pl.pallas_call(partial(backward_kernel, moment, sections), out_shape=(plt...  34.8 us
    pallas_call x12, Pallas kernels, near_call(): pl.pallas_call(kernel, out_shape=tuple((made(*shape) for shape in shapes)...  16.7 us
    ppermute x16, starting transfers between devices, per_device(): lax.ppermute(result, 'section', hops(moment, micro, sections, False))  15.7 us
    ppermute x16, starting transfers between devices, per_device(): lax.ppermute(result, 'section', hops(moment, micro, sections, True))  13.3 us
  transfers between devices with their start and end apart: 51, of which 18 were waited for; matrix products, arithmetic and copies ran while one was open for 0% of the time, Pallas kernels for 15%

profile of v3, /device:TPU:1, one launch (start us, length us, event | category | flops | bytes accessed | tf_op | source)
XLA Modules:
  0.0 452.7 jit_solution(14308579853587905420)
XLA Ops:
  11.0 4.4 collective-permute-start.3
  18.7 4.4 collective-permute-done.3.refs_3_
  23.1 5.6 %collective-permute-done.2.refs_2_ = bf16[2,592,128]{2,1,0:T(8,128)(2,1)S(1)} collective-permute-done((bf16[2,592,128]{2,1,0:T(8,128)(2,1)S(1)}, bf16[2,592,128]{2,1,0:T(8,128)(2,1)S(1)}, u32[]{:S(2)}, u32[]{:S(2)}) %collective-permute-start.2) | collective-permute-done | bytes 303136 | tf_op jit(solution)/shard_map/ppermute | solution.py:470
  34.6 23.5 %collective-permute-done.6.refs_3_ = bf16[4,2,592,128]{3,2,1,0:T(8,128)(2,1)S(1)} collective-permute-done((bf16[4,2,592,128]{3,2,1,0:T(8,128)(2,1)S(1)}, bf16[4,2,592,128]{3,2,1,0:T(8,128)(2,1)S(1)}, u32[]{:S(2)}, u32[]{:S(2)}) %collective-permute-start.6) | collective-permute-done | bytes 1212448 | tf_op jit(solution)/shard_map/ppermute | solution.py:470
  58.1 25.8 %collective-permute-start.10 = (bf16[4,2,592,128]{3,2,1,0:T(8,128)(2,1)S(1)}, bf16[4,2,592,128]{3,2,1,0:T(8,128)(2,1)S(1)}, u32[]{:S(2)}, u32[]{:S(2)}) collective-permute-start(bf16[4,2,592,128]{3,2,1,0:T(8,128)(2,1)S(1)} %collective-permute-done.6.refs_3_), channel_id=1, source_target_pairs={{0,1},{1,0},{2,3},{3,2},{4,5},{5,4},{6,7},{7,6},{8,9},{9,8},{10,11... | collective-permute-start | bytes 3637256 | tf_op jit(solution)/shard_map/ppermute | solution.py:470
  92.3 5.2 %layer_forward.18 = (bf16[32,4096]{1,0:T(8,128)(2,1)S(1)}, bf16[4,32,4096]{2,1,0:T(8,128)(2,1)S(1)}, bf16[4,32,4096]{2,1,0:T(8,128)(2,1)S(1)}, bf16[4,128,32,128...) custom-call(s32[4]{0:T(128)S(1)} %pad_add_fusion.place, ...), custom_call_target="tpu_custom_call", output_to_operand_aliasing={{1}: (7, {}), {2}: (8, {}), {3}: (9, {}), {4}: (10, {}), {5... | custom-call | flops 1000000000 | bytes 10000000 | tf_op jit(solution)/shard_map/layer_forward/pallas_call | solution.py:408
  98.9 5.3 %layer_forward.19 = (bf16[32,4096]{1,0:T(8,128)(2,1)S(1)}, bf16[4,32,4096]{2,1,0:T(8,128)(2,1)S(1)}, bf16[4,32,4096]{2,1,0:T(8,128)(2,1)S(1)}, bf16[4,128,32,128...) custom-call(s32[4]{0:T(128)S(1)} %pad_add_fusion.place, ...), custom_call_target="tpu_custom_call", output_to_operand_aliasing={{1}: (7, {}), {2}: (8, {}), {3}: (9, {}), {4}: (10, {}), {5... | custom-call | flops 1000000000 | bytes 10000000 | tf_op jit(solution)/shard_map/layer_forward/pallas_call | solution.py:408
  105.5 5.5 %layer_forward.20 = (bf16[32,4096]{1,0:T(8,128)(2,1)S(1)}, bf16[4,32,4096]{2,1,0:T(8,128)(2,1)S(1)}, bf16[4,32,4096]{2,1,0:T(8,128)(2,1)S(1)}, bf16[4,128,32,128...) custom-call(s32[4]{0:T(128)S(1)} %pad_add_fusion.place, ...), custom_call_target="tpu_custom_call", output_to_operand_aliasing={{1}: (7, {}), {2}: (8, {}), {3}: (9, {}), {4}: (10, {}), {5... | custom-call | flops 1000000000 | bytes 10000000 | tf_op jit(solution)/shard_map/layer_forward/pallas_call | solution.py:408
  114.1 5.3 %layer_forward.21 = (bf16[32,4096]{1,0:T(8,128)(2,1)S(1)}, bf16[4,32,4096]{2,1,0:T(8,128)(2,1)S(1)}, bf16[4,32,4096]{2,1,0:T(8,128)(2,1)S(1)}, bf16[4,128,32,128...) custom-call(s32[4]{0:T(128)S(1)} %pad_add_fusion.place, ...), custom_call_target="tpu_custom_call", output_to_operand_aliasing={{1}: (7, {}), {2}: (8, {}), {3}: (9, {}), {4}: (10, {}), {5... | custom-call | flops 1000000000 | bytes 10000000 | tf_op jit(solution)/shard_map/layer_forward/pallas_call | solution.py:408
  133.6 10.1 %layer_forward.29 = (bf16[32,4096]{1,0:T(8,128)(2,1)S(1)}, bf16[4,32,4096]{2,1,0:T(8,128)(2,1)S(1)}, bf16[4,32,4096]{2,1,0:T(8,128)(2,1)S(1)}, bf16[4,128,32,128...) custom-call(s32[4]{0:T(128)S(1)} %pad_add_fusion.place, ...), custom_call_target="tpu_custom_call", output_to_operand_aliasing={{1}: (7, {}), {2}: (8, {}), {3}: (9, {}), {4}: (10, {}), {5... | custom-call | flops 1000000000 | bytes 10000000 | tf_op jit(solution)/shard_map/layer_forward/pallas_call | solution.py:408
  172.8 136.6 %collective-permute-done.40.incoming = bf16[32,4096]{1,0:T(8,128)(2,1)S(1)} collective-permute-done((bf16[32,4096]{1,0:T(8,128)(2,1)S(1)}, bf16[32,4096]{1,0:T(8,128)(2,1)S(1)}, u32[]{:S(2)}, u32[]{:S(2)}) %collective-permute-start.40) | collective-permute-done | bytes 262176 | tf_op jit(solution)/shard_map/ppermute | solution.py:584
  309.4 6.2 %layer_backward.32 = (bf16[32,4096]{1,0:T(8,128)(2,1)S(1)}, bf16[4,32,4096]{2,1,0:T(8,128)(2,1)S(1)}, bf16[4,128,32,128]{3,2,1,0:T(8,128)(2,1)S(1)}, bf16[4,2,32,128]{3,2,1,0:T(8,128)(2,1)S(1)}) custom-call(s32[4]{0:T(128)S(1)} %pad_add_fusion.place, s32[128]{0:T(128)S(1)} %get-tuple-element.218.upq, ...), custom_call_target="tpu_custom_call", output_to_operand_aliasing={{1}: (8, {}), {2}: (9, {}), {3}: (10, {})} | custom-call | flops 1000000000 | bytes 10000000 | tf_op jit(solution)/shard_map/layer_backward/pallas_call | solution.py:428
  316.9 5.8 %collective-permute-done.39.incoming = bf16[32,4096]{1,0:T(8,128)(2,1)S(1)} collective-permute-done((bf16[32,4096]{1,0:T(8,128)(2,1)S(1)}, bf16[32,4096]{1,0:T(8,128)(2,1)S(1)}, u32[]{:S(2)}, u32[]{:S(2)}) %collective-permute-start.39) | collective-permute-done | bytes 262176 | tf_op jit(solution)/shard_map/ppermute | solution.py:584
  322.7 6.2 %layer_backward.33 = (bf16[32,4096]{1,0:T(8,128)(2,1)S(1)}, bf16[4,32,4096]{2,1,0:T(8,128)(2,1)S(1)}, bf16[4,128,32,128]{3,2,1,0:T(8,128)(2,1)S(1)}, bf16[4,2,32,128]{3,2,1,0:T(8,128)(2,1)S(1)}) custom-call(s32[4]{0:T(128)S(1)} %pad_add_fusion.place, s32[128]{0:T(128)S(1)} %get-tuple-element.218.upq, ...), custom_call_target="tpu_custom_call", output_to_operand_aliasing={{1}: (8, {}), {2}: (9, {}), {3}: (10, {})} | custom-call | flops 1000000000 | bytes 10000000 | tf_op jit(solution)/shard_map/layer_backward/pallas_call | solution.py:428
  330.9 6.9 %layer_backward.34 = (bf16[32,4096]{1,0:T(8,128)(2,1)}, bf16[4,32,4096]{2,1,0:T(8,128)(2,1)S(1)}, bf16[4,128,32,128]{3,2,1,0:T(8,128)(2,1)S(1)}, bf16[4,2,32,128]{3,2,1,0:T(8,128)(2,1)S(1)}) custom-call(s32[4]{0:T(128)S(1)} %pad_add_fusion.place, s32[128]{0:T(128)S(1)} %get-tuple-element.218.upq, ...), custom_call_target="tpu_custom_call", output_to_operand_aliasing={{1}: (8, {}), {2}: (9, {}), {3}: (10, {})} | custom-call | flops 1000000000 | bytes 10000000 | tf_op jit(solution)/shard_map/layer_backward/pallas_call | solution.py:428
  339.1 6.9 %layer_backward.35 = (bf16[32,4096]{1,0:T(8,128)(2,1)}, bf16[4,32,4096]{2,1,0:T(8,128)(2,1)S(1)}, bf16[4,128,32,128]{3,2,1,0:T(8,128)(2,1)S(1)}, bf16[4,2,32,128]{3,2,1,0:T(8,128)(2,1)S(1)}) custom-call(s32[4]{0:T(128)S(1)} %pad_add_fusion.place, s32[128]{0:T(128)S(1)} %get-tuple-element.218.upq, ...), custom_call_target="tpu_custom_call", output_to_operand_aliasing={{1}: (8, {}), {2}: (9, {}), {3}: (10, {})} | custom-call | flops 1000000000 | bytes 10000000 | tf_op jit(solution)/shard_map/layer_backward/pallas_call | solution.py:428
  346.0 6.1 %grads.3 = bf16[4,4,2,592,128]{4,3,2,1,0:T(8,128)(2,1)S(1)} custom-call(s32[4]{0:T(128)S(1)} %pad_add_fusion.place, s32[128]{0:T(128)S(1)} %get-tuple-element.218.upq, s32[128]{0:T(128)S(1)} %get-tuple-element.219.dnq, bf16[4,32,4096]{2,1,0:T(8,128)(2,1)S(1)} %get-tuple-element.333.xs, bf16[4,32,4096]{2,1,0:T(8,128)(2,1)S(1)} %get-tuple-element.407.gs, ...), custom_call_target="tpu_custom_call" | custom-call | tf_op jit(solution)/shard_map/grads/pallas_call | solution.py:449
  352.1 14.7 %collective-permute-start.43 = (bf16[4,4,2,592,128]{4,3,2,1,0:T(8,128)(2,1)S(1)}, bf16[4,4,2,592,128]{4,3,2,1,0:T(8,128)(2,1)S(1)}, u32[]{:S(2)}, u32[]{:S(2)}) collective-permute-start(bf16[4,4,2,592,128]{4,3,2,1,0:T(8,128)(2,1)S(1)} %grads.3), channel_id=1, source_target_pairs={{0,1},{1,0},{2,3},{3,2},{4,5},{5,4},{6,7},{7,6},{8,9},{9,8},{10,11... | collective-permute-start | bytes 14549000 | tf_op jit(solution)/shard_map/ppermute | solution.py:470
  366.9 5.5 %grads.2.mine = bf16[4,4,2,592,128]{4,3,2,1,0:T(8,128)(2,1)S(1)} custom-call(s32[4]{0:T(128)S(1)} %pad_add_fusion.place, s32[128]{0:T(128)S(1)} %get-tuple-element.218.upq, s32[128]{0:T(128)S(1)} %get-tuple-element.219.dnq, bf16[4,32,4096]{2,1,0:T(8,128)(2,1)S(1)} %get-tuple-element.333.xs, bf16[4,32,4096]{2,1,0:T(8,128)(2,1)S(1)} %get-tuple-element.407.gs, ...), custom_call_target="tpu_custom_call" | custom-call | tf_op jit(solution)/shard_map/grads/pallas_call | solution.py:449
  378.6 26.9 %collective-permute-done.44.refs_1_ = bf16[4,2,592,128]{3,2,1,0:T(8,128)(2,1)S(1)} collective-permute-done((bf16[4,2,592,128]{3,2,1,0:T(8,128)(2,1)S(1)}, bf16[4,2,592,128]{3,2,1,0:T(8,128)(2,1)S(1)}, u32[]{:S(2)}, u32[]{:S(2)}) %collective-permute-start.44) | collective-permute-done | bytes 1212448 | tf_op jit(solution)/shard_map/ppermute | solution.py:470
  407.0 6.5 %collective-permute-start.48 = (bf16[2,592,128]{2,1,0:T(8,128)(2,1)S(1)}, bf16[2,592,128]{2,1,0:T(8,128)(2,1)S(1)}, u32[]{:S(2)}, u32[]{:S(2)}) collective-permute-start(bf16[2,592,128]{2,1,0:T(8,128)(2,1)S(1)} %get-tuple-element.417), channel_id=1, source_target_pairs={{0,4},{1,17},{2,6},{3,19},{4,0},{5,21},{6,2},{7,23},{8,12},{9,25},... | collective-permute-start | bytes 909320 | tf_op jit(solution)/shard_map/ppermute | solution.py:470
  414.3 4.9 %collective-permute-done.47.refs_1_ = bf16[2,592,128]{2,1,0:T(8,128)(2,1)S(1)} collective-permute-done((bf16[2,592,128]{2,1,0:T(8,128)(2,1)S(1)}, bf16[2,592,128]{2,1,0:T(8,128)(2,1)S(1)}, u32[]{:S(2)}, u32[]{:S(2)}) %collective-permute-start.47) | collective-permute-done | bytes 303136 | tf_op jit(solution)/shard_map/ppermute | solution.py:470
  419.2 11.8 %collective-permute-done.48.refs_2_ = bf16[2,592,128]{2,1,0:T(8,128)(2,1)S(1)} collective-permute-done((bf16[2,592,128]{2,1,0:T(8,128)(2,1)S(1)}, bf16[2,592,128]{2,1,0:T(8,128)(2,1)S(1)}, u32[]{:S(2)}, u32[]{:S(2)}) %collective-permute-start.48) | collective-permute-done | bytes 303136 | tf_op jit(solution)/shard_map/ppermute | solution.py:470
  431.2 18.7 %collective-permute-start.50 = (f32[592,128]{1,0:T(8,128)S(1)}, f32[592,128]{1,0:T(8,128)S(1)}, u32[]{:S(2)}, u32[]{:S(2)}) collective-permute-start(f32[592,128]{1,0:T(8,128)S(1)} %get-tuple-element.420), channel_id=1, source_target_pairs={{0,1},{1,0},{2,3},{3,2},{4,5},{5,4},{6,7},{7,6},{8,9},{9,8},{10,11... | collective-permute-start | bytes 909320 | tf_op jit(solution)/shard_map/ppermute | solution.py:470
  (145 shorter events, 92.0 us)
Async XLA Ops:
  11.0 12.0 %collective-permute-start.3 = (bf16[2,592,128]{2,1,0:T(8,128)(2,1)S(1)}, bf16[2,592,128]{2,1,0:T(8,128)(2,1)S(1)}, u32[]{:S(2)}, u32[]{:S(2)}) collective-permute-start(bf16[2,592,128]{2,1,0:T(8,128)(2,1)S(1)} %pair.1.refs_0_), channel_id=1, source_target_pairs={{0,6},{1,25},{2,0},{3,27},{4,2},{5,29},{6,4},{7,31},{8,14},{9,1},{... | collective-permute-start | bytes 909320 | tf_op jit(solution)/shard_map/ppermute | solution.py:470
  15.4 13.3 %collective-permute-start.2 = (bf16[2,592,128]{2,1,0:T(8,128)(2,1)S(1)}, bf16[2,592,128]{2,1,0:T(8,128)(2,1)S(1)}, u32[]{:S(2)}, u32[]{:S(2)}) collective-permute-start(bf16[2,592,128]{2,1,0:T(8,128)(2,1)S(1)} %pair.1.refs_0_), channel_id=1, source_target_pairs={{0,4},{1,17},{2,6},{3,19},{4,0},{5,21},{6,2},{7,23},{8,12},{9,25},... | collective-permute-start | bytes 909320 | tf_op jit(solution)/shard_map/ppermute | solution.py:470
  16.4 12.3 %collective-permute-start.1 = (bf16[2,592,128]{2,1,0:T(8,128)(2,1)S(1)}, bf16[2,592,128]{2,1,0:T(8,128)(2,1)S(1)}, u32[]{:S(2)}, u32[]{:S(2)}) collective-permute-start(bf16[2,592,128]{2,1,0:T(8,128)(2,1)S(1)} %pair.1.refs_0_), channel_id=1, source_target_pairs={{0,2},{1,9},{2,4},{3,11},{4,6},{5,13},{6,0},{7,15},{8,10},{9,17},{... | collective-permute-start | bytes 909320 | tf_op jit(solution)/shard_map/ppermute | solution.py:470
  28.8 29.3 %collective-permute-start.6 = (bf16[4,2,592,128]{3,2,1,0:T(8,128)(2,1)S(1)}, bf16[4,2,592,128]{3,2,1,0:T(8,128)(2,1)S(1)}, u32[]{:S(2)}, u32[]{:S(2)}) collective-permute-start(bf16[4,2,592,128]{3,2,1,0:T(8,128)(2,1)S(1)} %line.1.refs_0_), channel_id=1, source_target_pairs={{0,24},{1,7},{2,26},{3,1},{4,28},{5,3},{6,30},{7,5},{8,0},{9,15},{... | collective-permute-start | bytes 3637256 | tf_op jit(solution)/shard_map/ppermute | solution.py:470
  31.6 52.3 %collective-permute-start.5 = (bf16[4,2,592,128]{3,2,1,0:T(8,128)(2,1)S(1)}, bf16[4,2,592,128]{3,2,1,0:T(8,128)(2,1)S(1)}, u32[]{:S(2)}, u32[]{:S(2)}) collective-permute-start(bf16[4,2,592,128]{3,2,1,0:T(8,128)(2,1)S(1)} %line.1.refs_0_), channel_id=1, source_target_pairs={{0,16},{1,5},{2,18},{3,7},{4,20},{5,1},{6,22},{7,3},{8,24},{9,13},... | collective-permute-start | bytes 3637256 | tf_op jit(solution)/shard_map/ppermute | solution.py:470
  31.9 52.0 %collective-permute-start.4 = (bf16[4,2,592,128]{3,2,1,0:T(8,128)(2,1)S(1)}, bf16[4,2,592,128]{3,2,1,0:T(8,128)(2,1)S(1)}, u32[]{:S(2)}, u32[]{:S(2)}) collective-permute-start(bf16[4,2,592,128]{3,2,1,0:T(8,128)(2,1)S(1)} %line.1.refs_0_), channel_id=1, source_target_pairs={{0,8},{1,3},{2,10},{3,5},{4,12},{5,7},{6,14},{7,1},{8,16},{9,11},{... | collective-permute-start | bytes 3637256 | tf_op jit(solution)/shard_map/ppermute | solution.py:470
  32.6 51.8 %collective-permute-start.7 = (bf16[4,2,592,128]{3,2,1,0:T(8,128)(2,1)S(1)}, bf16[4,2,592,128]{3,2,1,0:T(8,128)(2,1)S(1)}, u32[]{:S(2)}, u32[]{:S(2)}) collective-permute-start(bf16[4,2,592,128]{3,2,1,0:T(8,128)(2,1)S(1)} %line.1.refs_0_), channel_id=1, source_target_pairs={{0,1},{1,0},{2,3},{3,2},{4,5},{5,4},{6,7},{7,6},{8,9},{9,8},{10,11... | collective-permute-start | bytes 3637256 | tf_op jit(solution)/shard_map/ppermute | solution.py:470
  58.1 28.4 %collective-permute-start.10 = (bf16[4,2,592,128]{3,2,1,0:T(8,128)(2,1)S(1)}, bf16[4,2,592,128]{3,2,1,0:T(8,128)(2,1)S(1)}, u32[]{:S(2)}, u32[]{:S(2)}) collective-permute-start(bf16[4,2,592,128]{3,2,1,0:T(8,128)(2,1)S(1)} %collective-permute-done.6.refs_3_), channel_id=1, source_target_pairs={{0,1},{1,0},{2,3},{3,2},{4,5},{5,4},{6,7},{7,6},{8,9},{9,8},{10,11... | collective-permute-start | bytes 3637256 | tf_op jit(solution)/shard_map/ppermute | solution.py:470
  97.6 7.9 %collective-permute-start.12 = (bf16[32,4096]{1,0:T(8,128)(2,1)S(1)}, bf16[32,4096]{1,0:T(8,128)(2,1)S(1)}, u32[]{:S(2)}, u32[]{:S(2)}) collective-permute-start(bf16[32,4096]{1,0:T(8,128)(2,1)S(1)} %get-tuple-element.237), channel_id=1, source_target_pairs={{0,32},{32,64},{1,33},{33,65},{2,34},{34,66},{3,35},{35,67},{4,36}... | collective-permute-start | bytes 786440 | tf_op jit(solution)/shard_map/ppermute | solution.py:574
  104.2 9.9 %collective-permute-start.11 = (bf16[32,4096]{1,0:T(8,128)(2,1)S(1)}, bf16[32,4096]{1,0:T(8,128)(2,1)S(1)}, u32[]{:S(2)}, u32[]{:S(2)}) collective-permute-start(bf16[32,4096]{1,0:T(8,128)(2,1)S(1)} %get-tuple-element.236), channel_id=1, source_target_pairs={{0,32},{32,64},{1,33},{33,65},{2,34},{34,66},{3,35},{35,67},{4,36}... | collective-permute-start | bytes 786440 | tf_op jit(solution)/shard_map/ppermute | solution.py:574
  111.0 10.3 %collective-permute-start.14 = (bf16[32,4096]{1,0:T(8,128)(2,1)S(1)}, bf16[32,4096]{1,0:T(8,128)(2,1)S(1)}, u32[]{:S(2)}, u32[]{:S(2)}) collective-permute-start(bf16[32,4096]{1,0:T(8,128)(2,1)S(1)} %get-tuple-element.249), channel_id=1, source_target_pairs={{0,32},{32,64},{1,33},{33,65},{2,34},{34,66},{3,35},{35,67},{4,36}... | collective-permute-start | bytes 786440 | tf_op jit(solution)/shard_map/ppermute | solution.py:574
  132.9 11.5 %collective-permute-start.22 = (bf16[32,4096]{1,0:T(8,128)(2,1)S(1)}, bf16[32,4096]{1,0:T(8,128)(2,1)S(1)}, u32[]{:S(2)}, u32[]{:S(2)}) collective-permute-start(bf16[32,4096]{1,0:T(8,128)(2,1)S(1)} %get-tuple-element.297), channel_id=1, source_target_pairs={{96,128},{128,160},{160,192},{97,129},{129,161},{161,193},{98,130}... | collective-permute-start | bytes 786440 | tf_op jit(solution)/shard_map/ppermute | solution.py:574
  169.6 139.8 %collective-permute-start.40 = (bf16[32,4096]{1,0:T(8,128)(2,1)S(1)}, bf16[32,4096]{1,0:T(8,128)(2,1)S(1)}, u32[]{:S(2)}, u32[]{:S(2)}) collective-permute-start(bf16[32,4096]{1,0:T(8,128)(2,1)S(1)} %get-tuple-element.392), channel_id=1, source_target_pairs={{64,32},{32,0},{65,33},{33,1},{66,34},{34,2},{67,35},{35,3},{68,36... | collective-permute-start | bytes 786440 | tf_op jit(solution)/shard_map/ppermute | solution.py:584
  171.5 151.2 %collective-permute-start.39 = (bf16[32,4096]{1,0:T(8,128)(2,1)S(1)}, bf16[32,4096]{1,0:T(8,128)(2,1)S(1)}, u32[]{:S(2)}, u32[]{:S(2)}) collective-permute-start(bf16[32,4096]{1,0:T(8,128)(2,1)S(1)} %get-tuple-element.391), channel_id=1, source_target_pairs={{64,32},{32,0},{65,33},{33,1},{66,34},{34,2},{67,35},{35,3},{68,36... | collective-permute-start | bytes 786440 | tf_op jit(solution)/shard_map/ppermute | solution.py:584
  315.6 15.3 %collective-permute-start.42 = (bf16[32,4096]{1,0:T(8,128)(2,1)S(1)}, bf16[32,4096]{1,0:T(8,128)(2,1)S(1)}, u32[]{:S(2)}, u32[]{:S(2)}) collective-permute-start(bf16[32,4096]{1,0:T(8,128)(2,1)S(1)} %get-tuple-element.400), channel_id=1, source_target_pairs={{64,32},{32,0},{65,33},{33,1},{66,34},{34,2},{67,35},{35,3},{68,36... | collective-permute-start | bytes 786440 | tf_op jit(solution)/shard_map/ppermute | solution.py:584
  329.0 10.1 %collective-permute-start.41 = (bf16[32,4096]{1,0:T(8,128)(2,1)S(1)}, bf16[32,4096]{1,0:T(8,128)(2,1)S(1)}, u32[]{:S(2)}, u32[]{:S(2)}) collective-permute-start(bf16[32,4096]{1,0:T(8,128)(2,1)S(1)} %get-tuple-element.399), channel_id=1, source_target_pairs={{64,32},{32,0},{65,33},{33,1},{66,34},{34,2},{67,35},{35,3},{68,36... | collective-permute-start | bytes 786440 | tf_op jit(solution)/shard_map/ppermute | solution.py:584
  352.1 22.5 %collective-permute-start.43 = (bf16[4,4,2,592,128]{4,3,2,1,0:T(8,128)(2,1)S(1)}, bf16[4,4,2,592,128]{4,3,2,1,0:T(8,128)(2,1)S(1)}, u32[]{:S(2)}, u32[]{:S(2)}) collective-permute-start(bf16[4,4,2,592,128]{4,3,2,1,0:T(8,128)(2,1)S(1)} %grads.3), channel_id=1, source_target_pairs={{0,1},{1,0},{2,3},{3,2},{4,5},{5,4},{6,7},{7,6},{8,9},{9,8},{10,11... | collective-permute-start | bytes 14549000 | tf_op jit(solution)/shard_map/ppermute | solution.py:470
  375.7 29.8 %collective-permute-start.44 = (bf16[4,2,592,128]{3,2,1,0:T(8,128)(2,1)S(1)}, bf16[4,2,592,128]{3,2,1,0:T(8,128)(2,1)S(1)}, u32[]{:S(2)}, u32[]{:S(2)}) collective-permute-start(bf16[4,2,592,128]{3,2,1,0:T(8,128)(2,1)S(1)} %get-tuple-element.412), channel_id=1, source_target_pairs={{0,8},{1,3},{2,10},{3,5},{4,12},{5,7},{6,14},{7,1},{8,16},{9,11},{... | collective-permute-start | bytes 3637256 | tf_op jit(solution)/shard_map/ppermute | solution.py:470
  375.8 29.7 %collective-permute-start.45 = (bf16[4,2,592,128]{3,2,1,0:T(8,128)(2,1)S(1)}, bf16[4,2,592,128]{3,2,1,0:T(8,128)(2,1)S(1)}, u32[]{:S(2)}, u32[]{:S(2)}) collective-permute-start(bf16[4,2,592,128]{3,2,1,0:T(8,128)(2,1)S(1)} %get-tuple-element.413), channel_id=1, source_target_pairs={{0,16},{1,5},{2,18},{3,7},{4,20},{5,1},{6,22},{7,3},{8,24},{9,13},... | collective-permute-start | bytes 3637256 | tf_op jit(solution)/shard_map/ppermute | solution.py:470
  377.0 29.3 %collective-permute-start.46 = (bf16[4,2,592,128]{3,2,1,0:T(8,128)(2,1)S(1)}, bf16[4,2,592,128]{3,2,1,0:T(8,128)(2,1)S(1)}, u32[]{:S(2)}, u32[]{:S(2)}) collective-permute-start(bf16[4,2,592,128]{3,2,1,0:T(8,128)(2,1)S(1)} %get-tuple-element.414), channel_id=1, source_target_pairs={{0,24},{1,7},{2,26},{3,1},{4,28},{5,3},{6,30},{7,5},{8,0},{9,15},{... | collective-permute-start | bytes 3637256 | tf_op jit(solution)/shard_map/ppermute | solution.py:470
  406.9 12.4 %collective-permute-start.47 = (bf16[2,592,128]{2,1,0:T(8,128)(2,1)S(1)}, bf16[2,592,128]{2,1,0:T(8,128)(2,1)S(1)}, u32[]{:S(2)}, u32[]{:S(2)}) collective-permute-start(bf16[2,592,128]{2,1,0:T(8,128)(2,1)S(1)} %get-tuple-element.416), channel_id=1, source_target_pairs={{0,2},{1,9},{2,4},{3,11},{4,6},{5,13},{6,0},{7,15},{8,10},{9,17},{... | collective-permute-start | bytes 909320 | tf_op jit(solution)/shard_map/ppermute | solution.py:470
  407.0 24.1 %collective-permute-start.48 = (bf16[2,592,128]{2,1,0:T(8,128)(2,1)S(1)}, bf16[2,592,128]{2,1,0:T(8,128)(2,1)S(1)}, u32[]{:S(2)}, u32[]{:S(2)}) collective-permute-start(bf16[2,592,128]{2,1,0:T(8,128)(2,1)S(1)} %get-tuple-element.417), channel_id=1, source_target_pairs={{0,4},{1,17},{2,6},{3,19},{4,0},{5,21},{6,2},{7,23},{8,12},{9,25},... | collective-permute-start | bytes 909320 | tf_op jit(solution)/shard_map/ppermute | solution.py:470
  413.4 17.6 %collective-permute-start.49 = (bf16[2,592,128]{2,1,0:T(8,128)(2,1)S(1)}, bf16[2,592,128]{2,1,0:T(8,128)(2,1)S(1)}, u32[]{:S(2)}, u32[]{:S(2)}) collective-permute-start(bf16[2,592,128]{2,1,0:T(8,128)(2,1)S(1)} %get-tuple-element.418), channel_id=1, source_target_pairs={{0,6},{1,25},{2,0},{3,27},{4,2},{5,29},{6,4},{7,31},{8,14},{9,1},{... | collective-permute-start | bytes 909320 | tf_op jit(solution)/shard_map/ppermute | solution.py:470
  431.2 19.9 %collective-permute-start.50 = (f32[592,128]{1,0:T(8,128)S(1)}, f32[592,128]{1,0:T(8,128)S(1)}, u32[]{:S(2)}, u32[]{:S(2)}) collective-permute-start(f32[592,128]{1,0:T(8,128)S(1)} %get-tuple-element.420), channel_id=1, source_target_pairs={{0,1},{1,0},{2,3},{3,2},{4,5},{5,4},{6,7},{7,6},{8,9},{9,8},{10,11... | collective-permute-start | bytes 909320 | tf_op jit(solution)/shard_map/ppermute | solution.py:470
  (35 other events, 77.8 us)

commit v4 on v3

--- a/solution.py
+++ b/solution.py
@@ -23,6 +23,7 @@
 DOWN = 1
 ALONG = 4
 CORES = 2
+Z_SECTIONS = 4
 SMALL_VMEM = 12 * 1024 * 1024
 UNROLL = 16
 MOMENT_GROUP = 4
@@ -233,11 +234,16 @@
         ).astype(BF16)
 
 
+def far_along_z(place, side):
+    return jnp.logical_and(side == UP, place[3] < Z_SECTIONS)
+
+
 def place_of(place, p, side):
     dz = lax.rem(p // (ALONG * CORES) - place[0] + ALONG, ALONG)
     dy = lax.rem(lax.rem(p // CORES, ALONG) - place[1] + ALONG, ALONG)
     other = lax.rem(lax.rem(p, CORES) + side, CORES)
-    return (dz, dy, other) if side == UP else (dy, dz, other)
+    long_z = far_along_z(place, side)
+    return jnp.where(long_z, dz, dy), jnp.where(long_z, dy, dz), other
 
 
 def column(ref, p):
@@ -313,22 +319,34 @@
 
 
 def pack_kernel(
-    place, up_blocks, up_left, up_right, down_blocks, down_left, down_right, mine, other
+    place, up_blocks, up_left, up_right, down_blocks, down_left, down_right, inputs, cotangent,
+    mine, other, near_inputs, near_cotangent, sem,
 ):
-    for side, tiles, model, hidden in (
-        (UP, up_blocks, up_left, up_right),
-        (DOWN, down_blocks, down_right, down_left),
-    ):
-        for out, core in ((mine, side), (other, 1 - side)):
-
-            @pl.when(place[2] == core)
-            def _():
-                for i in range(PER_ROW):
-                    out[i * TILE : (i + 1) * TILE, :] = tiles[i]
-                out[MODEL:HIDDEN, :] = model[...]
-                for i in range(PER_ROW):
-                    rows = slice(HIDDEN + RANK * i, HIDDEN + RANK * (i + 1))
-                    out[rows, :] = hidden[:, i * TILE : (i + 1) * TILE]
+    def copies(up, down):
+        pairs = [(inputs, near_inputs), (cotangent, near_cotangent)]
+        for out, tiles, model, hidden in (
+            (up, up_blocks, up_left, up_right),
+            (down, down_blocks, down_right, down_left),
+        ):
+            pairs.append((model, out.at[MODEL:HIDDEN, :]))
+            for i in range(PER_ROW):
+                rows = slice(HIDDEN + RANK * i, HIDDEN + RANK * (i + 1))
+                cols = slice(i * TILE, (i + 1) * TILE)
+                pairs.append((tiles.at[i], out.at[cols, :]))
+                pairs.append((hidden.at[:, cols], out.at[rows, :]))
+        made = [pltpu.make_async_copy(*pair, sem.at[i]) for i, pair in enumerate(pairs)]
+        for copy in made[2:] + made[:2]:
+            copy.start()
+        for copy in made:
+            copy.wait()
+
+    @pl.when(place[2] == UP)
+    def _():
+        copies(mine, other)
+
+    @pl.when(place[2] == DOWN)
+    def _():
+        copies(other, mine)
 
 
 def stack_kernel(*refs):
@@ -340,13 +358,15 @@
     mine, other, sides = refs[:ALONG], refs[ALONG : 2 * ALONG], refs[2 * ALONG :]
     z, y, core = place[0], place[1], place[2]
     for side, out in zip((UP, DOWN), sides):
+        long_z = far_along_z(place, side)
         for pieces, holder in ((mine, side), (other, 1 - side)):
 
             @pl.when(core == holder)
             def _():
                 for outer in range(ALONG):
                     for inner in range(ALONG):
-                        dz, dy = (outer, inner) if side == UP else (inner, outer)
+                        dz = jnp.where(long_z, outer, inner)
+                        dy = outer + inner - dz
                         back_z = lax.rem(z - dz + ALONG, ALONG)
                         back_y = lax.rem(y - dy + ALONG, ALONG)
                         chip = back_z * ALONG + back_y
@@ -457,29 +477,39 @@
     )(*scalars, *map(near, arrays))
 
 
-def dp_send(value, *steps):
-    def index(z, y, c):
-        return ((z % ALONG) * ALONG + y % ALONG) * CORES + c % CORES
+def send(value, step):
+    sections = lax.axis_size("section")
+
+    def index(section, z, y, c):
+        return ((section * ALONG + z % ALONG) * ALONG + y % ALONG) * CORES + c % CORES
 
     route = []
-    for z in range(ALONG):
-        for y in range(ALONG):
-            for c in range(CORES):
-                dz, dy, dc = steps[c % len(steps)]
-                route.append((index(z, y, c), index(z + dz, y + dy, c + dc)))
-    return lax.ppermute(value, "dp", route)
+    for section in range(sections):
+        for z in range(ALONG):
+            for y in range(ALONG):
+                for c in range(CORES):
+                    dz, dy, dc = step(section, c)
+                    target = index(section, z + dz, y + dy, c + dc)
+                    route.append((index(section, z, y, c), target))
+    return lax.ppermute(value, ("section", "dp"), route)
 
 
 def swap_cores(value):
-    return dp_send(value, (0, 0, 1))
+    return send(value, lambda section, core: (0, 0, 1))
 
 
 def along_first(value, d):
-    return dp_send(value, (0, d, 0), (d, 0, 0))
+    return send(
+        value,
+        lambda section, core: (0, d, 0) if core == UP and section < Z_SECTIONS else (d, 0, 0),
+    )
 
 
 def along_second(value, d):
-    return dp_send(value, (d, 0, 0), (0, d, 0))
+    return send(
+        value,
+        lambda section, core: (d, 0, 0) if core == UP and section < Z_SECTIONS else (0, d, 0),
+    )
 
 
 FAR = range(1, ALONG)
@@ -549,16 +579,17 @@
     place, upq, dnq = lax.optimization_barrier((place, up_index[0, :, 1], down_index[0, :, 0]))
     side = ((SIDE, TILE), BF16)
     factors = [item[0].T for item in (up_left, up_right, down_left, down_right)]
-    packed = gather(
-        place,
-        *near_call(
-            pack_kernel,
-            "pack",
-            (side, side),
-            (place,),
-            (up_blocks[0], *factors[:2], down_blocks[0], *factors[2:]),
-        ),
-    )
+    near_tokens = (inputs.shape, BF16)
+    mine, other, inputs, cotangent = pl.pallas_call(
+        pack_kernel,
+        out_shape=tuple(pltpu.VMEM(*shape) for shape in (side, side, near_tokens, near_tokens)),
+        in_specs=[SMEM] + [HBM] * 8,
+        out_specs=(VMEM,) * 4,
+        scratch_shapes=[pltpu.SemaphoreType.DMA((2 + 2 * (1 + 2 * PER_ROW),))],
+        compiler_params=pltpu.CompilerParams(vmem_limit_bytes=SMALL_VMEM),
+        name="pack",
+    )(place, up_blocks[0], *factors[:2], down_blocks[0], *factors[2:], inputs, cotangent)
+    packed = gather(place, mine, other)
 
     wide, tall, thin = (micro, rows, width), (micro, hidden, rows, TILE), (micro, 2, rows, TILE)
     xs, outs, act, slope, flat, arrived, travelling = buffers(

time: 458 us -> 456 us (level)
  the two profiles are of different devices: /device:TPU:1 before, /device:TPU:65 now
where the time goes in v4:
time: 456 us; the launch traced here: 452 us
  waiting for transfers between devices  235 us (52%)
  starting transfers between devices  114 us (25%)
  Pallas kernels  92.4 us (20%)
  local copies, waits for them, and re-layouts  8.73 us (2%)
    ppermute x16, waiting for transfers between devices, per_device(): lax.ppermute(result, 'section', hops(moment, micro, sections, True))  144 us
    ppermute x19, waiting for transfers between devices, send(): return lax.ppermute(value, ('section', 'dp'), route)  87 us
    ppermute x19, starting transfers between devices, send(): return lax.ppermute(value, ('section', 'dp'), route)  85 us
    pallas_call x18, Pallas kernels, forward_call(): pl.pallas_call(partial(forward_kernel, moment), out_shape=(pltpu.VMEM(inc...  40.2 us
    pallas_call x18, Pallas kernels, backward_call(): pl.pallas_call(partial(backward_kernel, moment, sections), out_shape=(plt...  34.8 us
    pallas_call x11, Pallas kernels, near_call(): pl.pallas_call(kernel, out_shape=tuple((made(*shape) for shape in shapes)...  16.2 us
    ppermute x16, starting transfers between devices, per_device(): lax.ppermute(result, 'section', hops(moment, micro, sections, False))  15.8 us
    ppermute x16, starting transfers between devices, per_device(): lax.ppermute(result, 'section', hops(moment, micro, sections, True))  13.3 us
  transfers between devices with their start and end apart: 51, of which 17 were waited for; matrix products, arithmetic and copies ran while one was open for 0% of the time, Pallas kernels for 15%

profile of v4, /device:TPU:65, one launch (start us, length us, event | category | flops | bytes accessed | tf_op | source)
XLA Modules:
  0.0 451.7 jit_solution(16377779736680256168)
XLA Ops:
  20.4 6.0 %collective-permute-done.3.refs_3_ = bf16[2,592,128]{2,1,0:T(8,128)(2,1)S(1)} collective-permute-done((bf16[2,592,128]{2,1,0:T(8,128)(2,1)S(1)}, bf16[2,592,128]{2,1,0:T(8,128)(2,1)S(1)}, u32[]{:S(2)}, u32[]{:S(2)}) %collective-permute-start.3) | collective-permute-done | bytes 303136 | tf_op jit(solution)/shard_map/ppermute | solution.py:494
  36.3 23.1 %collective-permute-done.6.refs_3_ = bf16[4,2,592,128]{3,2,1,0:T(8,128)(2,1)S(1)} collective-permute-done((bf16[4,2,592,128]{3,2,1,0:T(8,128)(2,1)S(1)}, bf16[4,2,592,128]{3,2,1,0:T(8,128)(2,1)S(1)}, u32[]{:S(2)}, u32[]{:S(2)}) %collective-permute-start.6) | collective-permute-done | bytes 1212448 | tf_op jit(solution)/shard_map/ppermute | solution.py:494
  59.4 6.3 %collective-permute-start.9 = (bf16[4,2,592,128]{3,2,1,0:T(8,128)(2,1)S(1)}, bf16[4,2,592,128]{3,2,1,0:T(8,128)(2,1)S(1)}, u32[]{:S(2)}, u32[]{:S(2)}) collective-permute-start(bf16[4,2,592,128]{3,2,1,0:T(8,128)(2,1)S(1)} %collective-permute-done.5.refs_2_), channel_id=1, source_target_pairs={{0,1},{1,0},{2,3},{3,2},{4,5},{5,4},{6,7},{7,6},{8,9},{9,8},{10,11... | collective-permute-start | bytes 3637256 | tf_op jit(solution)/shard_map/ppermute | solution.py:494
  65.7 9.3 %collective-permute-start.8 = (bf16[4,2,592,128]{3,2,1,0:T(8,128)(2,1)S(1)}, bf16[4,2,592,128]{3,2,1,0:T(8,128)(2,1)S(1)}, u32[]{:S(2)}, u32[]{:S(2)}) collective-permute-start(bf16[4,2,592,128]{3,2,1,0:T(8,128)(2,1)S(1)} %collective-permute-done.4.refs_1_), channel_id=1, source_target_pairs={{0,1},{1,0},{2,3},{3,2},{4,5},{5,4},{6,7},{7,6},{8,9},{9,8},{10,11... | collective-permute-start | bytes 3637256 | tf_op jit(solution)/shard_map/ppermute | solution.py:494
  78.8 5.3 %layer_forward.18 = (bf16[32,4096]{1,0:T(8,128)(2,1)S(1)}, bf16[4,32,4096]{2,1,0:T(8,128)(2,1)S(1)}, bf16[4,32,4096]{2,1,0:T(8,128)(2,1)S(1)}, bf16[4,128,32,128...) custom-call(s32[4]{0:T(128)S(1)} %pad_add_fusion.place, ...), custom_call_target="tpu_custom_call", output_to_operand_aliasing={{1}: (7, {}), {2}: (8, {}), {3}: (9, {}), {4}: (10, {}), {5... | custom-call | flops 1000000000 | bytes 10000000 | tf_op jit(solution)/shard_map/layer_forward/pallas_call | solution.py:428
  85.4 5.2 %layer_forward.19 = (bf16[32,4096]{1,0:T(8,128)(2,1)S(1)}, bf16[4,32,4096]{2,1,0:T(8,128)(2,1)S(1)}, bf16[4,32,4096]{2,1,0:T(8,128)(2,1)S(1)}, bf16[4,128,32,128...) custom-call(s32[4]{0:T(128)S(1)} %pad_add_fusion.place, ...), custom_call_target="tpu_custom_call", output_to_operand_aliasing={{1}: (7, {}), {2}: (8, {}), {3}: (9, {}), {4}: (10, {}), {5... | custom-call | flops 1000000000 | bytes 10000000 | tf_op jit(solution)/shard_map/layer_forward/pallas_call | solution.py:428
  91.9 5.5 %layer_forward.20 = (bf16[32,4096]{1,0:T(8,128)(2,1)S(1)}, bf16[4,32,4096]{2,1,0:T(8,128)(2,1)S(1)}, bf16[4,32,4096]{2,1,0:T(8,128)(2,1)S(1)}, bf16[4,128,32,128...) custom-call(s32[4]{0:T(128)S(1)} %pad_add_fusion.place, ...), custom_call_target="tpu_custom_call", output_to_operand_aliasing={{1}: (7, {}), {2}: (8, {}), {3}: (9, {}), {4}: (10, {}), {5... | custom-call | flops 1000000000 | bytes 10000000 | tf_op jit(solution)/shard_map/layer_forward/pallas_call | solution.py:428
  100.6 5.2 %layer_forward.21 = (bf16[32,4096]{1,0:T(8,128)(2,1)S(1)}, bf16[4,32,4096]{2,1,0:T(8,128)(2,1)S(1)}, bf16[4,32,4096]{2,1,0:T(8,128)(2,1)S(1)}, bf16[4,128,32,128...) custom-call(s32[4]{0:T(128)S(1)} %pad_add_fusion.place, ...), custom_call_target="tpu_custom_call", output_to_operand_aliasing={{1}: (7, {}), {2}: (8, {}), {3}: (9, {}), {4}: (10, {}), {5... | custom-call | flops 1000000000 | bytes 10000000 | tf_op jit(solution)/shard_map/layer_forward/pallas_call | solution.py:428
  120.1 10.1 %layer_forward.29 = (bf16[32,4096]{1,0:T(8,128)(2,1)S(1)}, bf16[4,32,4096]{2,1,0:T(8,128)(2,1)S(1)}, bf16[4,32,4096]{2,1,0:T(8,128)(2,1)S(1)}, bf16[4,128,32,128...) custom-call(s32[4]{0:T(128)S(1)} %pad_add_fusion.place, ...), custom_call_target="tpu_custom_call", output_to_operand_aliasing={{1}: (7, {}), {2}: (8, {}), {3}: (9, {}), {4}: (10, {}), {5... | custom-call | flops 1000000000 | bytes 10000000 | tf_op jit(solution)/shard_map/layer_forward/pallas_call | solution.py:428
  158.1 136.6 %collective-permute-done.40.incoming = bf16[32,4096]{1,0:T(8,128)(2,1)S(1)} collective-permute-done((bf16[32,4096]{1,0:T(8,128)(2,1)S(1)}, bf16[32,4096]{1,0:T(8,128)(2,1)S(1)}, u32[]{:S(2)}, u32[]{:S(2)}) %collective-permute-start.40) | collective-permute-done | bytes 262176 | tf_op jit(solution)/shard_map/ppermute | solution.py:615
  294.7 6.2 %layer_backward.32 = (bf16[32,4096]{1,0:T(8,128)(2,1)S(1)}, bf16[4,32,4096]{2,1,0:T(8,128)(2,1)S(1)}, bf16[4,128,32,128]{3,2,1,0:T(8,128)(2,1)S(1)}, bf16[4,2,32,128]{3,2,1,0:T(8,128)(2,1)S(1)}) custom-call(s32[4]{0:T(128)S(1)} %pad_add_fusion.place, s32[128]{0:T(128)S(1)} %get-tuple-element.220.upq, ...), custom_call_target="tpu_custom_call", output_to_operand_aliasing={{1}: (8, {}), {2}: (9, {}), {3}: (10, {})} | custom-call | flops 1000000000 | bytes 10000000 | tf_op jit(solution)/shard_map/layer_backward/pallas_call | solution.py:448
  302.2 5.7 %collective-permute-done.39.incoming = bf16[32,4096]{1,0:T(8,128)(2,1)S(1)} collective-permute-done((bf16[32,4096]{1,0:T(8,128)(2,1)S(1)}, bf16[32,4096]{1,0:T(8,128)(2,1)S(1)}, u32[]{:S(2)}, u32[]{:S(2)}) %collective-permute-start.39) | collective-permute-done | bytes 262176 | tf_op jit(solution)/shard_map/ppermute | solution.py:615
  307.9 6.2 %layer_backward.33 = (bf16[32,4096]{1,0:T(8,128)(2,1)S(1)}, bf16[4,32,4096]{2,1,0:T(8,128)(2,1)S(1)}, bf16[4,128,32,128]{3,2,1,0:T(8,128)(2,1)S(1)}, bf16[4,2,32,128]{3,2,1,0:T(8,128)(2,1)S(1)}) custom-call(s32[4]{0:T(128)S(1)} %pad_add_fusion.place, s32[128]{0:T(128)S(1)} %get-tuple-element.220.upq, ...), custom_call_target="tpu_custom_call", output_to_operand_aliasing={{1}: (8, {}), {2}: (9, {}), {3}: (10, {})} | custom-call | flops 1000000000 | bytes 10000000 | tf_op jit(solution)/shard_map/layer_backward/pallas_call | solution.py:448
  316.1 6.9 %layer_backward.34 = (bf16[32,4096]{1,0:T(8,128)(2,1)}, bf16[4,32,4096]{2,1,0:T(8,128)(2,1)S(1)}, bf16[4,128,32,128]{3,2,1,0:T(8,128)(2,1)S(1)}, bf16[4,2,32,128]{3,2,1,0:T(8,128)(2,1)S(1)}) custom-call(s32[4]{0:T(128)S(1)} %pad_add_fusion.place, s32[128]{0:T(128)S(1)} %get-tuple-element.220.upq, ...), custom_call_target="tpu_custom_call", output_to_operand_aliasing={{1}: (8, {}), {2}: (9, {}), {3}: (10, {})} | custom-call | flops 1000000000 | bytes 10000000 | tf_op jit(solution)/shard_map/layer_backward/pallas_call | solution.py:448
  324.2 6.9 %layer_backward.35 = (bf16[32,4096]{1,0:T(8,128)(2,1)}, bf16[4,32,4096]{2,1,0:T(8,128)(2,1)S(1)}, bf16[4,128,32,128]{3,2,1,0:T(8,128)(2,1)S(1)}, bf16[4,2,32,128]{3,2,1,0:T(8,128)(2,1)S(1)}) custom-call(s32[4]{0:T(128)S(1)} %pad_add_fusion.place, s32[128]{0:T(128)S(1)} %get-tuple-element.220.upq, ...), custom_call_target="tpu_custom_call", output_to_operand_aliasing={{1}: (8, {}), {2}: (9, {}), {3}: (10, {})} | custom-call | flops 1000000000 | bytes 10000000 | tf_op jit(solution)/shard_map/layer_backward/pallas_call | solution.py:448
  331.2 6.1 %grads.3 = bf16[4,4,2,592,128]{4,3,2,1,0:T(8,128)(2,1)S(1)} custom-call(s32[4]{0:T(128)S(1)} %pad_add_fusion.place, s32[128]{0:T(128)S(1)} %get-tuple-element.220.upq, s32[128]{0:T(128)S(1)} %get-tuple-element.221.dnq, bf16[4,32,4096]{2,1,0:T(8,128)(2,1)S(1)} %get-tuple-element.336.xs, bf16[4,32,4096]{2,1,0:T(8,128)(2,1)S(1)} %get-tuple-element.411.gs, ...), custom_call_target="tpu_custom_call" | custom-call | tf_op jit(solution)/shard_map/grads/pallas_call | solution.py:469
  337.3 14.8 %collective-permute-start.43 = (bf16[4,4,2,592,128]{4,3,2,1,0:T(8,128)(2,1)S(1)}, bf16[4,4,2,592,128]{4,3,2,1,0:T(8,128)(2,1)S(1)}, u32[]{:S(2)}, u32[]{:S(2)}) collective-permute-start(bf16[4,4,2,592,128]{4,3,2,1,0:T(8,128)(2,1)S(1)} %grads.3), channel_id=1, source_target_pairs={{0,1},{1,0},{2,3},{3,2},{4,5},{5,4},{6,7},{7,6},{8,9},{9,8},{10,11... | collective-permute-start | bytes 14549000 | tf_op jit(solution)/shard_map/ppermute | solution.py:494
  352.1 5.5 %grads.2.mine = bf16[4,4,2,592,128]{4,3,2,1,0:T(8,128)(2,1)S(1)} custom-call(s32[4]{0:T(128)S(1)} %pad_add_fusion.place, s32[128]{0:T(128)S(1)} %get-tuple-element.220.upq, s32[128]{0:T(128)S(1)} %get-tuple-element.221.dnq, bf16[4,32,4096]{2,1,0:T(8,128)(2,1)S(1)} %get-tuple-element.336.xs, bf16[4,32,4096]{2,1,0:T(8,128)(2,1)S(1)} %get-tuple-element.411.gs, ...), custom_call_target="tpu_custom_call" | custom-call | tf_op jit(solution)/shard_map/grads/pallas_call | solution.py:469
  366.1 12.1 %collective-permute-done.44.refs_1_ = bf16[4,2,592,128]{3,2,1,0:T(8,128)(2,1)S(1)} collective-permute-done((bf16[4,2,592,128]{3,2,1,0:T(8,128)(2,1)S(1)}, bf16[4,2,592,128]{3,2,1,0:T(8,128)(2,1)S(1)}, u32[]{:S(2)}, u32[]{:S(2)}) %collective-permute-start.44) | collective-permute-done | bytes 1212448 | tf_op jit(solution)/shard_map/ppermute | solution.py:494
  378.3 14.3 %collective-permute-done.45.refs_2_ = bf16[4,2,592,128]{3,2,1,0:T(8,128)(2,1)S(1)} collective-permute-done((bf16[4,2,592,128]{3,2,1,0:T(8,128)(2,1)S(1)}, bf16[4,2,592,128]{3,2,1,0:T(8,128)(2,1)S(1)}, u32[]{:S(2)}, u32[]{:S(2)}) %collective-permute-start.45) | collective-permute-done | bytes 1212448 | tf_op jit(solution)/shard_map/ppermute | solution.py:494
  393.2 14.1 %collective-permute-start.47 = (bf16[2,592,128]{2,1,0:T(8,128)(2,1)S(1)}, bf16[2,592,128]{2,1,0:T(8,128)(2,1)S(1)}, u32[]{:S(2)}, u32[]{:S(2)}) collective-permute-start(bf16[2,592,128]{2,1,0:T(8,128)(2,1)S(1)} %get-tuple-element.420), channel_id=1, source_target_pairs={{0,2},{1,9},{2,4},{3,11},{4,6},{5,13},{6,0},{7,15},{8,10},{9,17},{... | collective-permute-start | bytes 909320 | tf_op jit(solution)/shard_map/ppermute | solution.py:494
  409.5 11.5 %collective-permute-done.47.refs_1_ = bf16[2,592,128]{2,1,0:T(8,128)(2,1)S(1)} collective-permute-done((bf16[2,592,128]{2,1,0:T(8,128)(2,1)S(1)}, bf16[2,592,128]{2,1,0:T(8,128)(2,1)S(1)}, u32[]{:S(2)}, u32[]{:S(2)}) %collective-permute-start.47) | collective-permute-done | bytes 303136 | tf_op jit(solution)/shard_map/ppermute | solution.py:494
  421.0 7.3 %collective-permute-done.48.refs_2_ = bf16[2,592,128]{2,1,0:T(8,128)(2,1)S(1)} collective-permute-done((bf16[2,592,128]{2,1,0:T(8,128)(2,1)S(1)}, bf16[2,592,128]{2,1,0:T(8,128)(2,1)S(1)}, u32[]{:S(2)}, u32[]{:S(2)}) %collective-permute-start.48) | collective-permute-done | bytes 303136 | tf_op jit(solution)/shard_map/ppermute | solution.py:494
  431.5 17.3 %collective-permute-start.50 = (f32[592,128]{1,0:T(8,128)S(1)}, f32[592,128]{1,0:T(8,128)S(1)}, u32[]{:S(2)}, u32[]{:S(2)}) collective-permute-start(f32[592,128]{1,0:T(8,128)S(1)} %get-tuple-element.424), channel_id=1, source_target_pairs={{0,1},{1,0},{2,3},{3,2},{4,5},{5,4},{6,7},{7,6},{8,9},{9,8},{10,11... | collective-permute-start | bytes 909320 | tf_op jit(solution)/shard_map/ppermute | solution.py:494
  (145 shorter events, 102.3 us)
Async XLA Ops:
  11.6 14.7 %collective-permute-start.3 = (bf16[2,592,128]{2,1,0:T(8,128)(2,1)S(1)}, bf16[2,592,128]{2,1,0:T(8,128)(2,1)S(1)}, u32[]{:S(2)}, u32[]{:S(2)}) collective-permute-start(bf16[2,592,128]{2,1,0:T(8,128)(2,1)S(1)} %pair.1.refs_0_), channel_id=1, source_target_pairs={{0,6},{1,25},{2,0},{3,27},{4,2},{5,29},{6,4},{7,31},{8,14},{9,1},{... | collective-permute-start | bytes 909320 | tf_op jit(solution)/shard_map/ppermute | solution.py:494
  12.8 13.6 %collective-permute-start.2 = (bf16[2,592,128]{2,1,0:T(8,128)(2,1)S(1)}, bf16[2,592,128]{2,1,0:T(8,128)(2,1)S(1)}, u32[]{:S(2)}, u32[]{:S(2)}) collective-permute-start(bf16[2,592,128]{2,1,0:T(8,128)(2,1)S(1)} %pair.1.refs_0_), channel_id=1, source_target_pairs={{0,4},{1,17},{2,6},{3,19},{4,0},{5,21},{6,2},{7,23},{8,12},{9,25},... | collective-permute-start | bytes 909320 | tf_op jit(solution)/shard_map/ppermute | solution.py:494
  17.9 12.0 %collective-permute-start.1 = (bf16[2,592,128]{2,1,0:T(8,128)(2,1)S(1)}, bf16[2,592,128]{2,1,0:T(8,128)(2,1)S(1)}, u32[]{:S(2)}, u32[]{:S(2)}) collective-permute-start(bf16[2,592,128]{2,1,0:T(8,128)(2,1)S(1)} %pair.1.refs_0_), channel_id=1, source_target_pairs={{0,2},{1,9},{2,4},{3,11},{4,6},{5,13},{6,0},{7,15},{8,10},{9,17},{... | collective-permute-start | bytes 909320 | tf_op jit(solution)/shard_map/ppermute | solution.py:494
  30.0 29.4 %collective-permute-start.6 = (bf16[4,2,592,128]{3,2,1,0:T(8,128)(2,1)S(1)}, bf16[4,2,592,128]{3,2,1,0:T(8,128)(2,1)S(1)}, u32[]{:S(2)}, u32[]{:S(2)}) collective-permute-start(bf16[4,2,592,128]{3,2,1,0:T(8,128)(2,1)S(1)} %line.1.refs_0_), channel_id=1, source_target_pairs={{0,24},{1,7},{2,26},{3,1},{4,28},{5,3},{6,30},{7,5},{8,0},{9,15},{... | collective-permute-start | bytes 3637256 | tf_op jit(solution)/shard_map/ppermute | solution.py:494
  32.9 26.5 %collective-permute-start.5 = (bf16[4,2,592,128]{3,2,1,0:T(8,128)(2,1)S(1)}, bf16[4,2,592,128]{3,2,1,0:T(8,128)(2,1)S(1)}, u32[]{:S(2)}, u32[]{:S(2)}) collective-permute-start(bf16[4,2,592,128]{3,2,1,0:T(8,128)(2,1)S(1)} %line.1.refs_0_), channel_id=1, source_target_pairs={{0,16},{1,5},{2,18},{3,7},{4,20},{5,1},{6,22},{7,3},{8,24},{9,13},... | collective-permute-start | bytes 3637256 | tf_op jit(solution)/shard_map/ppermute | solution.py:494
  33.3 32.5 %collective-permute-start.4 = (bf16[4,2,592,128]{3,2,1,0:T(8,128)(2,1)S(1)}, bf16[4,2,592,128]{3,2,1,0:T(8,128)(2,1)S(1)}, u32[]{:S(2)}, u32[]{:S(2)}) collective-permute-start(bf16[4,2,592,128]{3,2,1,0:T(8,128)(2,1)S(1)} %line.1.refs_0_), channel_id=1, source_target_pairs={{0,8},{1,3},{2,10},{3,5},{4,12},{5,7},{6,14},{7,1},{8,16},{9,11},{... | collective-permute-start | bytes 3637256 | tf_op jit(solution)/shard_map/ppermute | solution.py:494
  33.9 41.1 %collective-permute-start.7 = (bf16[4,2,592,128]{3,2,1,0:T(8,128)(2,1)S(1)}, bf16[4,2,592,128]{3,2,1,0:T(8,128)(2,1)S(1)}, u32[]{:S(2)}, u32[]{:S(2)}) collective-permute-start(bf16[4,2,592,128]{3,2,1,0:T(8,128)(2,1)S(1)} %line.1.refs_0_), channel_id=1, source_target_pairs={{0,1},{1,0},{2,3},{3,2},{4,5},{5,4},{6,7},{7,6},{8,9},{9,8},{10,11... | collective-permute-start | bytes 3637256 | tf_op jit(solution)/shard_map/ppermute | solution.py:494
  59.4 15.7 %collective-permute-start.10 = (bf16[4,2,592,128]{3,2,1,0:T(8,128)(2,1)S(1)}, bf16[4,2,592,128]{3,2,1,0:T(8,128)(2,1)S(1)}, u32[]{:S(2)}, u32[]{:S(2)}) collective-permute-start(bf16[4,2,592,128]{3,2,1,0:T(8,128)(2,1)S(1)} %collective-permute-done.6.refs_3_), channel_id=1, source_target_pairs={{0,1},{1,0},{2,3},{3,2},{4,5},{5,4},{6,7},{7,6},{8,9},{9,8},{10,11... | collective-permute-start | bytes 3637256 | tf_op jit(solution)/shard_map/ppermute | solution.py:494
  59.4 15.6 %collective-permute-start.9 = (bf16[4,2,592,128]{3,2,1,0:T(8,128)(2,1)S(1)}, bf16[4,2,592,128]{3,2,1,0:T(8,128)(2,1)S(1)}, u32[]{:S(2)}, u32[]{:S(2)}) collective-permute-start(bf16[4,2,592,128]{3,2,1,0:T(8,128)(2,1)S(1)} %collective-permute-done.5.refs_2_), channel_id=1, source_target_pairs={{0,1},{1,0},{2,3},{3,2},{4,5},{5,4},{6,7},{7,6},{8,9},{9,8},{10,11... | collective-permute-start | bytes 3637256 | tf_op jit(solution)/shard_map/ppermute | solution.py:494
  65.7 11.8 %collective-permute-start.8 = (bf16[4,2,592,128]{3,2,1,0:T(8,128)(2,1)S(1)}, bf16[4,2,592,128]{3,2,1,0:T(8,128)(2,1)S(1)}, u32[]{:S(2)}, u32[]{:S(2)}) collective-permute-start(bf16[4,2,592,128]{3,2,1,0:T(8,128)(2,1)S(1)} %collective-permute-done.4.refs_1_), channel_id=1, source_target_pairs={{0,1},{1,0},{2,3},{3,2},{4,5},{5,4},{6,7},{7,6},{8,9},{9,8},{10,11... | collective-permute-start | bytes 3637256 | tf_op jit(solution)/shard_map/ppermute | solution.py:494
  97.5 10.3 %collective-permute-start.14 = (bf16[32,4096]{1,0:T(8,128)(2,1)S(1)}, bf16[32,4096]{1,0:T(8,128)(2,1)S(1)}, u32[]{:S(2)}, u32[]{:S(2)}) collective-permute-start(bf16[32,4096]{1,0:T(8,128)(2,1)S(1)} %get-tuple-element.252), channel_id=1, source_target_pairs={{0,32},{32,64},{1,33},{33,65},{2,34},{34,66},{3,35},{35,67},{4,36}... | collective-permute-start | bytes 786440 | tf_op jit(solution)/shard_map/ppermute | solution.py:605
  119.4 11.5 %collective-permute-start.22 = (bf16[32,4096]{1,0:T(8,128)(2,1)S(1)}, bf16[32,4096]{1,0:T(8,128)(2,1)S(1)}, u32[]{:S(2)}, u32[]{:S(2)}) collective-permute-start(bf16[32,4096]{1,0:T(8,128)(2,1)S(1)} %get-tuple-element.300), channel_id=1, source_target_pairs={{96,128},{128,160},{160,192},{97,129},{129,161},{161,193},{98,130}... | collective-permute-start | bytes 786440 | tf_op jit(solution)/shard_map/ppermute | solution.py:605
  154.9 139.8 %collective-permute-start.40 = (bf16[32,4096]{1,0:T(8,128)(2,1)S(1)}, bf16[32,4096]{1,0:T(8,128)(2,1)S(1)}, u32[]{:S(2)}, u32[]{:S(2)}) collective-permute-start(bf16[32,4096]{1,0:T(8,128)(2,1)S(1)} %get-tuple-element.396), channel_id=1, source_target_pairs={{64,32},{32,0},{65,33},{33,1},{66,34},{34,2},{67,35},{35,3},{68,36... | collective-permute-start | bytes 786440 | tf_op jit(solution)/shard_map/ppermute | solution.py:615
  156.8 151.1 %collective-permute-start.39 = (bf16[32,4096]{1,0:T(8,128)(2,1)S(1)}, bf16[32,4096]{1,0:T(8,128)(2,1)S(1)}, u32[]{:S(2)}, u32[]{:S(2)}) collective-permute-start(bf16[32,4096]{1,0:T(8,128)(2,1)S(1)} %get-tuple-element.395), channel_id=1, source_target_pairs={{64,32},{32,0},{65,33},{33,1},{66,34},{34,2},{67,35},{35,3},{68,36... | collective-permute-start | bytes 786440 | tf_op jit(solution)/shard_map/ppermute | solution.py:615
  300.9 15.2 %collective-permute-start.42 = (bf16[32,4096]{1,0:T(8,128)(2,1)S(1)}, bf16[32,4096]{1,0:T(8,128)(2,1)S(1)}, u32[]{:S(2)}, u32[]{:S(2)}) collective-permute-start(bf16[32,4096]{1,0:T(8,128)(2,1)S(1)} %get-tuple-element.404), channel_id=1, source_target_pairs={{64,32},{32,0},{65,33},{33,1},{66,34},{34,2},{67,35},{35,3},{68,36... | collective-permute-start | bytes 786440 | tf_op jit(solution)/shard_map/ppermute | solution.py:615
  314.1 10.1 %collective-permute-start.41 = (bf16[32,4096]{1,0:T(8,128)(2,1)S(1)}, bf16[32,4096]{1,0:T(8,128)(2,1)S(1)}, u32[]{:S(2)}, u32[]{:S(2)}) collective-permute-start(bf16[32,4096]{1,0:T(8,128)(2,1)S(1)} %get-tuple-element.403), channel_id=1, source_target_pairs={{64,32},{32,0},{65,33},{33,1},{66,34},{34,2},{67,35},{35,3},{68,36... | collective-permute-start | bytes 786440 | tf_op jit(solution)/shard_map/ppermute | solution.py:615
  337.3 22.5 %collective-permute-start.43 = (bf16[4,4,2,592,128]{4,3,2,1,0:T(8,128)(2,1)S(1)}, bf16[4,4,2,592,128]{4,3,2,1,0:T(8,128)(2,1)S(1)}, u32[]{:S(2)}, u32[]{:S(2)}) collective-permute-start(bf16[4,4,2,592,128]{4,3,2,1,0:T(8,128)(2,1)S(1)} %grads.3), channel_id=1, source_target_pairs={{0,1},{1,0},{2,3},{3,2},{4,5},{5,4},{6,7},{7,6},{8,9},{9,8},{10,11... | collective-permute-start | bytes 14549000 | tf_op jit(solution)/shard_map/ppermute | solution.py:494
  360.9 17.4 %collective-permute-start.44 = (bf16[4,2,592,128]{3,2,1,0:T(8,128)(2,1)S(1)}, bf16[4,2,592,128]{3,2,1,0:T(8,128)(2,1)S(1)}, u32[]{:S(2)}, u32[]{:S(2)}) collective-permute-start(bf16[4,2,592,128]{3,2,1,0:T(8,128)(2,1)S(1)} %get-tuple-element.416), channel_id=1, source_target_pairs={{0,8},{1,3},{2,10},{3,5},{4,12},{5,7},{6,14},{7,1},{8,16},{9,11},{... | collective-permute-start | bytes 3637256 | tf_op jit(solution)/shard_map/ppermute | solution.py:494
  362.7 29.9 %collective-permute-start.45 = (bf16[4,2,592,128]{3,2,1,0:T(8,128)(2,1)S(1)}, bf16[4,2,592,128]{3,2,1,0:T(8,128)(2,1)S(1)}, u32[]{:S(2)}, u32[]{:S(2)}) collective-permute-start(bf16[4,2,592,128]{3,2,1,0:T(8,128)(2,1)S(1)} %get-tuple-element.417), channel_id=1, source_target_pairs={{0,16},{1,5},{2,18},{3,7},{4,20},{5,1},{6,22},{7,3},{8,24},{9,13},... | collective-permute-start | bytes 3637256 | tf_op jit(solution)/shard_map/ppermute | solution.py:494
  365.4 27.2 %collective-permute-start.46 = (bf16[4,2,592,128]{3,2,1,0:T(8,128)(2,1)S(1)}, bf16[4,2,592,128]{3,2,1,0:T(8,128)(2,1)S(1)}, u32[]{:S(2)}, u32[]{:S(2)}) collective-permute-start(bf16[4,2,592,128]{3,2,1,0:T(8,128)(2,1)S(1)} %get-tuple-element.418), channel_id=1, source_target_pairs={{0,24},{1,7},{2,26},{3,1},{4,28},{5,3},{6,30},{7,5},{8,0},{9,15},{... | collective-permute-start | bytes 3637256 | tf_op jit(solution)/shard_map/ppermute | solution.py:494
  393.2 27.8 %collective-permute-start.47 = (bf16[2,592,128]{2,1,0:T(8,128)(2,1)S(1)}, bf16[2,592,128]{2,1,0:T(8,128)(2,1)S(1)}, u32[]{:S(2)}, u32[]{:S(2)}) collective-permute-start(bf16[2,592,128]{2,1,0:T(8,128)(2,1)S(1)} %get-tuple-element.420), channel_id=1, source_target_pairs={{0,2},{1,9},{2,4},{3,11},{4,6},{5,13},{6,0},{7,15},{8,10},{9,17},{... | collective-permute-start | bytes 909320 | tf_op jit(solution)/shard_map/ppermute | solution.py:494
  407.3 21.0 %collective-permute-start.48 = (bf16[2,592,128]{2,1,0:T(8,128)(2,1)S(1)}, bf16[2,592,128]{2,1,0:T(8,128)(2,1)S(1)}, u32[]{:S(2)}, u32[]{:S(2)}) collective-permute-start(bf16[2,592,128]{2,1,0:T(8,128)(2,1)S(1)} %get-tuple-element.421), channel_id=1, source_target_pairs={{0,4},{1,17},{2,6},{3,19},{4,0},{5,21},{6,2},{7,23},{8,12},{9,25},... | collective-permute-start | bytes 909320 | tf_op jit(solution)/shard_map/ppermute | solution.py:494
  409.5 21.9 %collective-permute-start.49 = (bf16[2,592,128]{2,1,0:T(8,128)(2,1)S(1)}, bf16[2,592,128]{2,1,0:T(8,128)(2,1)S(1)}, u32[]{:S(2)}, u32[]{:S(2)}) collective-permute-start(bf16[2,592,128]{2,1,0:T(8,128)(2,1)S(1)} %get-tuple-element.422), channel_id=1, source_target_pairs={{0,6},{1,25},{2,0},{3,27},{4,2},{5,29},{6,4},{7,31},{8,14},{9,1},{... | collective-permute-start | bytes 909320 | tf_op jit(solution)/shard_map/ppermute | solution.py:494
  431.5 18.5 %collective-permute-start.50 = (f32[592,128]{1,0:T(8,128)S(1)}, f32[592,128]{1,0:T(8,128)S(1)}, u32[]{:S(2)}, u32[]{:S(2)}) collective-permute-start(f32[592,128]{1,0:T(8,128)S(1)} %get-tuple-element.424), channel_id=1, source_target_pairs={{0,1},{1,0},{2,3},{3,2},{4,5},{5,4},{6,7},{7,6},{8,9},{9,8},{10,11... | collective-permute-start | bytes 909320 | tf_op jit(solution)/shard_map/ppermute | solution.py:494
  (35 other events, 82.9 us)

commit v5 on v4

--- a/solution.py
+++ b/solution.py
@@ -280,7 +280,7 @@
         put_low(out, where, mm_tn(grad_down_latent, here))
         return carry
 
-    lax.fori_loop(0, blocks, one, 0, unroll=2)
+    lax.fori_loop(0, blocks, one, 0, unroll=8)
 
 
 def up_grads(place, upq, xs, gp, flat, blat, out, normed):
@@ -303,7 +303,7 @@
         put_low(out, where, mm_tn(up_latent, here))
         return carry
 
-    lax.fori_loop(0, blocks, one, 0, unroll=2)
+    lax.fori_loop(0, blocks, one, 0, unroll=8)
 
 
 def grads_kernel(keep, place, upq, dnq, xs, gs, act, gp, flat, blat, out, normed):
@@ -588,7 +588,15 @@
         scratch_shapes=[pltpu.SemaphoreType.DMA((2 + 2 * (1 + 2 * PER_ROW),))],
         compiler_params=pltpu.CompilerParams(vmem_limit_bytes=SMALL_VMEM),
         name="pack",
-    )(place, up_blocks[0], *factors[:2], down_blocks[0], *factors[2:], inputs, cotangent)
+    )(
+        place,
+        *(
+            pltpu.with_memory_space_constraint(item, pltpu.HBM)
+            for item in (
+                up_blocks[0], *factors[:2], down_blocks[0], *factors[2:], inputs, cotangent
+            )
+        ),
+    )
     packed = gather(place, mine, other)
 
     wide, tall, thin = (micro, rows, width), (micro, hidden, rows, TILE), (micro, 2, rows, TILE)

time: 456 us -> 448 us (0.982)
  local copies, waits for them, and re-layouts: 8.73 us -> 1.67 us
    unnamed x17 -> x1, local copies, waits for them, and re-layouts: 8.03 us -> 0.97 us
  transfers between devices with their start and end apart: 51 -> 51, of which waited for: 17 -> 17; matrix products, arithmetic and copies ran while one was open for 0% -> 0% of each run, Pallas kernels for 15% -> 14%
where the time goes in v5:
time: 448 us; the launch traced here: 444 us
  waiting for transfers between devices  236 us (53%)
  starting transfers between devices  115 us (26%)
  Pallas kernels  89.5 us (20%)
    ppermute x16, waiting for transfers between devices, per_device(): lax.ppermute(result, 'section', hops(moment, micro, sections, True))  144 us
    ppermute x19, waiting for transfers between devices, send(): return lax.ppermute(value, ('section', 'dp'), route)  88.7 us
    ppermute x19, starting transfers between devices, send(): return lax.ppermute(value, ('section', 'dp'), route)  85.4 us
    pallas_call x18, Pallas kernels, forward_call(): pl.pallas_call(partial(forward_kernel, moment), out_shape=(pltpu.VMEM(inc...  40.2 us
    pallas_call x18, Pallas kernels, backward_call(): pl.pallas_call(partial(backward_kernel, moment, sections), out_shape=(plt...  34.8 us
    ppermute x16, starting transfers between devices, per_device(): lax.ppermute(result, 'section', hops(moment, micro, sections, False))  15.9 us
    ppermute x16, starting transfers between devices, per_device(): lax.ppermute(result, 'section', hops(moment, micro, sections, True))  13.3 us
    pallas_call x11, Pallas kernels, near_call(): pl.pallas_call(kernel, out_shape=tuple((made(*shape) for shape in shapes)...  12 us
  transfers between devices with their start and end apart: 51, of which 17 were waited for; matrix products, arithmetic and copies ran while one was open for 0% of the time, Pallas kernels for 14%

profile of v5, /device:TPU:65, one launch (start us, length us, event | category | flops | bytes accessed | tf_op | source)
XLA Modules:
  0.0 443.9 jit_solution(10442390816252076097)
XLA Ops:
  7.0 5.2 %collective-permute-start.2 = (bf16[2,592,128]{2,1,0:T(8,128)(2,1)S(1)}, bf16[2,592,128]{2,1,0:T(8,128)(2,1)S(1)}, u32[]{:S(2)}, u32[]{:S(2)}) collective-permute-start(bf16[2,592,128]{2,1,0:T(8,128)(2,1)S(1)} %pair.1.refs_0_), channel_id=1, source_target_pairs={{0,4},{1,17},{2,6},{3,19},{4,0},{5,21},{6,2},{7,23},{8,12},{9,25},... | collective-permute-start | bytes 909320 | tf_op jit(solution)/shard_map/ppermute | solution.py:494
  14.6 6.0 %collective-permute-done.3.refs_3_ = bf16[2,592,128]{2,1,0:T(8,128)(2,1)S(1)} collective-permute-done((bf16[2,592,128]{2,1,0:T(8,128)(2,1)S(1)}, bf16[2,592,128]{2,1,0:T(8,128)(2,1)S(1)}, u32[]{:S(2)}, u32[]{:S(2)}) %collective-permute-start.3) | collective-permute-done | bytes 303136 | tf_op jit(solution)/shard_map/ppermute | solution.py:494
  30.5 23.1 %collective-permute-done.6.refs_3_ = bf16[4,2,592,128]{3,2,1,0:T(8,128)(2,1)S(1)} collective-permute-done((bf16[4,2,592,128]{3,2,1,0:T(8,128)(2,1)S(1)}, bf16[4,2,592,128]{3,2,1,0:T(8,128)(2,1)S(1)}, u32[]{:S(2)}, u32[]{:S(2)}) %collective-permute-start.6) | collective-permute-done | bytes 1212448 | tf_op jit(solution)/shard_map/ppermute | solution.py:494
  53.6 6.3 %collective-permute-start.9 = (bf16[4,2,592,128]{3,2,1,0:T(8,128)(2,1)S(1)}, bf16[4,2,592,128]{3,2,1,0:T(8,128)(2,1)S(1)}, u32[]{:S(2)}, u32[]{:S(2)}) collective-permute-start(bf16[4,2,592,128]{3,2,1,0:T(8,128)(2,1)S(1)} %collective-permute-done.5.refs_2_), channel_id=1, source_target_pairs={{0,1},{1,0},{2,3},{3,2},{4,5},{5,4},{6,7},{7,6},{8,9},{9,8},{10,11... | collective-permute-start | bytes 3637256 | tf_op jit(solution)/shard_map/ppermute | solution.py:494
  60.0 9.3 %collective-permute-start.8 = (bf16[4,2,592,128]{3,2,1,0:T(8,128)(2,1)S(1)}, bf16[4,2,592,128]{3,2,1,0:T(8,128)(2,1)S(1)}, u32[]{:S(2)}, u32[]{:S(2)}) collective-permute-start(bf16[4,2,592,128]{3,2,1,0:T(8,128)(2,1)S(1)} %collective-permute-done.4.refs_1_), channel_id=1, source_target_pairs={{0,1},{1,0},{2,3},{3,2},{4,5},{5,4},{6,7},{7,6},{8,9},{9,8},{10,11... | collective-permute-start | bytes 3637256 | tf_op jit(solution)/shard_map/ppermute | solution.py:494
  73.0 5.3 %layer_forward.18 = (bf16[32,4096]{1,0:T(8,128)(2,1)S(1)}, bf16[4,32,4096]{2,1,0:T(8,128)(2,1)S(1)}, bf16[4,32,4096]{2,1,0:T(8,128)(2,1)S(1)}, bf16[4,128,32,128...) custom-call(s32[4]{0:T(128)S(1)} %pad_add_fusion.place, ...), custom_call_target="tpu_custom_call", output_to_operand_aliasing={{1}: (7, {}), {2}: (8, {}), {3}: (9, {}), {4}: (10, {}), {5... | custom-call | flops 1000000000 | bytes 10000000 | tf_op jit(solution)/shard_map/layer_forward/pallas_call | solution.py:428
  79.6 5.2 %layer_forward.19 = (bf16[32,4096]{1,0:T(8,128)(2,1)S(1)}, bf16[4,32,4096]{2,1,0:T(8,128)(2,1)S(1)}, bf16[4,32,4096]{2,1,0:T(8,128)(2,1)S(1)}, bf16[4,128,32,128...) custom-call(s32[4]{0:T(128)S(1)} %pad_add_fusion.place, ...), custom_call_target="tpu_custom_call", output_to_operand_aliasing={{1}: (7, {}), {2}: (8, {}), {3}: (9, {}), {4}: (10, {}), {5... | custom-call | flops 1000000000 | bytes 10000000 | tf_op jit(solution)/shard_map/layer_forward/pallas_call | solution.py:428
  86.2 5.5 %layer_forward.20 = (bf16[32,4096]{1,0:T(8,128)(2,1)S(1)}, bf16[4,32,4096]{2,1,0:T(8,128)(2,1)S(1)}, bf16[4,32,4096]{2,1,0:T(8,128)(2,1)S(1)}, bf16[4,128,32,128...) custom-call(s32[4]{0:T(128)S(1)} %pad_add_fusion.place, ...), custom_call_target="tpu_custom_call", output_to_operand_aliasing={{1}: (7, {}), {2}: (8, {}), {3}: (9, {}), {4}: (10, {}), {5... | custom-call | flops 1000000000 | bytes 10000000 | tf_op jit(solution)/shard_map/layer_forward/pallas_call | solution.py:428
  94.9 5.2 %layer_forward.21 = (bf16[32,4096]{1,0:T(8,128)(2,1)S(1)}, bf16[4,32,4096]{2,1,0:T(8,128)(2,1)S(1)}, bf16[4,32,4096]{2,1,0:T(8,128)(2,1)S(1)}, bf16[4,128,32,128...) custom-call(s32[4]{0:T(128)S(1)} %pad_add_fusion.place, ...), custom_call_target="tpu_custom_call", output_to_operand_aliasing={{1}: (7, {}), {2}: (8, {}), {3}: (9, {}), {4}: (10, {}), {5... | custom-call | flops 1000000000 | bytes 10000000 | tf_op jit(solution)/shard_map/layer_forward/pallas_call | solution.py:428
  114.5 10.1 %layer_forward.29 = (bf16[32,4096]{1,0:T(8,128)(2,1)S(1)}, bf16[4,32,4096]{2,1,0:T(8,128)(2,1)S(1)}, bf16[4,32,4096]{2,1,0:T(8,128)(2,1)S(1)}, bf16[4,128,32,128...) custom-call(s32[4]{0:T(128)S(1)} %pad_add_fusion.place, ...), custom_call_target="tpu_custom_call", output_to_operand_aliasing={{1}: (7, {}), {2}: (8, {}), {3}: (9, {}), {4}: (10, {}), {5... | custom-call | flops 1000000000 | bytes 10000000 | tf_op jit(solution)/shard_map/layer_forward/pallas_call | solution.py:428
  152.5 136.5 %collective-permute-done.40.incoming = bf16[32,4096]{1,0:T(8,128)(2,1)S(1)} collective-permute-done((bf16[32,4096]{1,0:T(8,128)(2,1)S(1)}, bf16[32,4096]{1,0:T(8,128)(2,1)S(1)}, u32[]{:S(2)}, u32[]{:S(2)}) %collective-permute-start.40) | collective-permute-done | bytes 262176 | tf_op jit(solution)/shard_map/ppermute | solution.py:623
  289.0 6.2 %layer_backward.32 = (bf16[32,4096]{1,0:T(8,128)(2,1)S(1)}, bf16[4,32,4096]{2,1,0:T(8,128)(2,1)S(1)}, bf16[4,128,32,128]{3,2,1,0:T(8,128)(2,1)S(1)}, bf16[4,2,32,128]{3,2,1,0:T(8,128)(2,1)S(1)}) custom-call(s32[4]{0:T(128)S(1)} %pad_add_fusion.place, s32[128]{0:T(128)S(1)} %get-tuple-element.220.upq, ...), custom_call_target="tpu_custom_call", output_to_operand_aliasing={{1}: (8, {}), {2}: (9, {}), {3}: (10, {})} | custom-call | flops 1000000000 | bytes 10000000 | tf_op jit(solution)/shard_map/layer_backward/pallas_call | solution.py:448
  296.5 5.6 %collective-permute-done.39.incoming = bf16[32,4096]{1,0:T(8,128)(2,1)S(1)} collective-permute-done((bf16[32,4096]{1,0:T(8,128)(2,1)S(1)}, bf16[32,4096]{1,0:T(8,128)(2,1)S(1)}, u32[]{:S(2)}, u32[]{:S(2)}) %collective-permute-start.39) | collective-permute-done | bytes 262176 | tf_op jit(solution)/shard_map/ppermute | solution.py:623
  302.2 6.2 %layer_backward.33 = (bf16[32,4096]{1,0:T(8,128)(2,1)S(1)}, bf16[4,32,4096]{2,1,0:T(8,128)(2,1)S(1)}, bf16[4,128,32,128]{3,2,1,0:T(8,128)(2,1)S(1)}, bf16[4,2,32,128]{3,2,1,0:T(8,128)(2,1)S(1)}) custom-call(s32[4]{0:T(128)S(1)} %pad_add_fusion.place, s32[128]{0:T(128)S(1)} %get-tuple-element.220.upq, ...), custom_call_target="tpu_custom_call", output_to_operand_aliasing={{1}: (8, {}), {2}: (9, {}), {3}: (10, {})} | custom-call | flops 1000000000 | bytes 10000000 | tf_op jit(solution)/shard_map/layer_backward/pallas_call | solution.py:448
  310.4 6.9 %layer_backward.34 = (bf16[32,4096]{1,0:T(8,128)(2,1)}, bf16[4,32,4096]{2,1,0:T(8,128)(2,1)S(1)}, bf16[4,128,32,128]{3,2,1,0:T(8,128)(2,1)S(1)}, bf16[4,2,32,128]{3,2,1,0:T(8,128)(2,1)S(1)}) custom-call(s32[4]{0:T(128)S(1)} %pad_add_fusion.place, s32[128]{0:T(128)S(1)} %get-tuple-element.220.upq, ...), custom_call_target="tpu_custom_call", output_to_operand_aliasing={{1}: (8, {}), {2}: (9, {}), {3}: (10, {})} | custom-call | flops 1000000000 | bytes 10000000 | tf_op jit(solution)/shard_map/layer_backward/pallas_call | solution.py:448
  318.5 6.9 %layer_backward.35 = (bf16[32,4096]{1,0:T(8,128)(2,1)}, bf16[4,32,4096]{2,1,0:T(8,128)(2,1)S(1)}, bf16[4,128,32,128]{3,2,1,0:T(8,128)(2,1)S(1)}, bf16[4,2,32,128]{3,2,1,0:T(8,128)(2,1)S(1)}) custom-call(s32[4]{0:T(128)S(1)} %pad_add_fusion.place, s32[128]{0:T(128)S(1)} %get-tuple-element.220.upq, ...), custom_call_target="tpu_custom_call", output_to_operand_aliasing={{1}: (8, {}), {2}: (9, {}), {3}: (10, {})} | custom-call | flops 1000000000 | bytes 10000000 | tf_op jit(solution)/shard_map/layer_backward/pallas_call | solution.py:448
  329.5 14.7 %collective-permute-start.43 = (bf16[4,4,2,592,128]{4,3,2,1,0:T(8,128)(2,1)S(1)}, bf16[4,4,2,592,128]{4,3,2,1,0:T(8,128)(2,1)S(1)}, u32[]{:S(2)}, u32[]{:S(2)}) collective-permute-start(bf16[4,4,2,592,128]{4,3,2,1,0:T(8,128)(2,1)S(1)} %grads.3), channel_id=1, source_target_pairs={{0,1},{1,0},{2,3},{3,2},{4,5},{5,4},{6,7},{7,6},{8,9},{9,8},{10,11... | collective-permute-start | bytes 14549000 | tf_op jit(solution)/shard_map/ppermute | solution.py:494
  347.7 4.3 collective-permute-done.43.came
  358.4 11.7 %collective-permute-done.44.refs_1_ = bf16[4,2,592,128]{3,2,1,0:T(8,128)(2,1)S(1)} collective-permute-done((bf16[4,2,592,128]{3,2,1,0:T(8,128)(2,1)S(1)}, bf16[4,2,592,128]{3,2,1,0:T(8,128)(2,1)S(1)}, u32[]{:S(2)}, u32[]{:S(2)}) %collective-permute-start.44) | collective-permute-done | bytes 1212448 | tf_op jit(solution)/shard_map/ppermute | solution.py:494
  370.2 14.3 %collective-permute-done.45.refs_2_ = bf16[4,2,592,128]{3,2,1,0:T(8,128)(2,1)S(1)} collective-permute-done((bf16[4,2,592,128]{3,2,1,0:T(8,128)(2,1)S(1)}, bf16[4,2,592,128]{3,2,1,0:T(8,128)(2,1)S(1)}, u32[]{:S(2)}, u32[]{:S(2)}) %collective-permute-start.45) | collective-permute-done | bytes 1212448 | tf_op jit(solution)/shard_map/ppermute | solution.py:494
  385.1 14.5 %collective-permute-start.47 = (bf16[2,592,128]{2,1,0:T(8,128)(2,1)S(1)}, bf16[2,592,128]{2,1,0:T(8,128)(2,1)S(1)}, u32[]{:S(2)}, u32[]{:S(2)}) collective-permute-start(bf16[2,592,128]{2,1,0:T(8,128)(2,1)S(1)} %get-tuple-element.420), channel_id=1, source_target_pairs={{0,2},{1,9},{2,4},{3,11},{4,6},{5,13},{6,0},{7,15},{8,10},{9,17},{... | collective-permute-start | bytes 909320 | tf_op jit(solution)/shard_map/ppermute | solution.py:494
  401.8 11.4 %collective-permute-done.47.refs_1_ = bf16[2,592,128]{2,1,0:T(8,128)(2,1)S(1)} collective-permute-done((bf16[2,592,128]{2,1,0:T(8,128)(2,1)S(1)}, bf16[2,592,128]{2,1,0:T(8,128)(2,1)S(1)}, u32[]{:S(2)}, u32[]{:S(2)}) %collective-permute-start.47) | collective-permute-done | bytes 303136 | tf_op jit(solution)/shard_map/ppermute | solution.py:494
  413.2 7.4 %collective-permute-done.48.refs_2_ = bf16[2,592,128]{2,1,0:T(8,128)(2,1)S(1)} collective-permute-done((bf16[2,592,128]{2,1,0:T(8,128)(2,1)S(1)}, bf16[2,592,128]{2,1,0:T(8,128)(2,1)S(1)}, u32[]{:S(2)}, u32[]{:S(2)}) %collective-permute-start.48) | collective-permute-done | bytes 303136 | tf_op jit(solution)/shard_map/ppermute | solution.py:494
  423.8 17.3 %collective-permute-start.50 = (f32[592,128]{1,0:T(8,128)S(1)}, f32[592,128]{1,0:T(8,128)S(1)}, u32[]{:S(2)}, u32[]{:S(2)}) collective-permute-start(f32[592,128]{1,0:T(8,128)S(1)} %get-tuple-element.424), channel_id=1, source_target_pairs={{0,1},{1,0},{2,3},{3,2},{4,5},{5,4},{6,7},{7,6},{8,9},{9,8},{10,11... | collective-permute-start | bytes 909320 | tf_op jit(solution)/shard_map/ppermute | solution.py:494
  (129 shorter events, 96.9 us)
Async XLA Ops:
  5.8 14.7 %collective-permute-start.3 = (bf16[2,592,128]{2,1,0:T(8,128)(2,1)S(1)}, bf16[2,592,128]{2,1,0:T(8,128)(2,1)S(1)}, u32[]{:S(2)}, u32[]{:S(2)}) collective-permute-start(bf16[2,592,128]{2,1,0:T(8,128)(2,1)S(1)} %pair.1.refs_0_), channel_id=1, source_target_pairs={{0,6},{1,25},{2,0},{3,27},{4,2},{5,29},{6,4},{7,31},{8,14},{9,1},{... | collective-permute-start | bytes 909320 | tf_op jit(solution)/shard_map/ppermute | solution.py:494
  7.0 13.6 %collective-permute-start.2 = (bf16[2,592,128]{2,1,0:T(8,128)(2,1)S(1)}, bf16[2,592,128]{2,1,0:T(8,128)(2,1)S(1)}, u32[]{:S(2)}, u32[]{:S(2)}) collective-permute-start(bf16[2,592,128]{2,1,0:T(8,128)(2,1)S(1)} %pair.1.refs_0_), channel_id=1, source_target_pairs={{0,4},{1,17},{2,6},{3,19},{4,0},{5,21},{6,2},{7,23},{8,12},{9,25},... | collective-permute-start | bytes 909320 | tf_op jit(solution)/shard_map/ppermute | solution.py:494
  12.2 12.0 %collective-permute-start.1 = (bf16[2,592,128]{2,1,0:T(8,128)(2,1)S(1)}, bf16[2,592,128]{2,1,0:T(8,128)(2,1)S(1)}, u32[]{:S(2)}, u32[]{:S(2)}) collective-permute-start(bf16[2,592,128]{2,1,0:T(8,128)(2,1)S(1)} %pair.1.refs_0_), channel_id=1, source_target_pairs={{0,2},{1,9},{2,4},{3,11},{4,6},{5,13},{6,0},{7,15},{8,10},{9,17},{... | collective-permute-start | bytes 909320 | tf_op jit(solution)/shard_map/ppermute | solution.py:494
  24.3 29.4 %collective-permute-start.6 = (bf16[4,2,592,128]{3,2,1,0:T(8,128)(2,1)S(1)}, bf16[4,2,592,128]{3,2,1,0:T(8,128)(2,1)S(1)}, u32[]{:S(2)}, u32[]{:S(2)}) collective-permute-start(bf16[4,2,592,128]{3,2,1,0:T(8,128)(2,1)S(1)} %line.1.refs_0_), channel_id=1, source_target_pairs={{0,24},{1,7},{2,26},{3,1},{4,28},{5,3},{6,30},{7,5},{8,0},{9,15},{... | collective-permute-start | bytes 3637256 | tf_op jit(solution)/shard_map/ppermute | solution.py:494
  27.1 26.5 %collective-permute-start.5 = (bf16[4,2,592,128]{3,2,1,0:T(8,128)(2,1)S(1)}, bf16[4,2,592,128]{3,2,1,0:T(8,128)(2,1)S(1)}, u32[]{:S(2)}, u32[]{:S(2)}) collective-permute-start(bf16[4,2,592,128]{3,2,1,0:T(8,128)(2,1)S(1)} %line.1.refs_0_), channel_id=1, source_target_pairs={{0,16},{1,5},{2,18},{3,7},{4,20},{5,1},{6,22},{7,3},{8,24},{9,13},... | collective-permute-start | bytes 3637256 | tf_op jit(solution)/shard_map/ppermute | solution.py:494
  27.5 32.5 %collective-permute-start.4 = (bf16[4,2,592,128]{3,2,1,0:T(8,128)(2,1)S(1)}, bf16[4,2,592,128]{3,2,1,0:T(8,128)(2,1)S(1)}, u32[]{:S(2)}, u32[]{:S(2)}) collective-permute-start(bf16[4,2,592,128]{3,2,1,0:T(8,128)(2,1)S(1)} %line.1.refs_0_), channel_id=1, source_target_pairs={{0,8},{1,3},{2,10},{3,5},{4,12},{5,7},{6,14},{7,1},{8,16},{9,11},{... | collective-permute-start | bytes 3637256 | tf_op jit(solution)/shard_map/ppermute | solution.py:494
  28.2 41.1 %collective-permute-start.7 = (bf16[4,2,592,128]{3,2,1,0:T(8,128)(2,1)S(1)}, bf16[4,2,592,128]{3,2,1,0:T(8,128)(2,1)S(1)}, u32[]{:S(2)}, u32[]{:S(2)}) collective-permute-start(bf16[4,2,592,128]{3,2,1,0:T(8,128)(2,1)S(1)} %line.1.refs_0_), channel_id=1, source_target_pairs={{0,1},{1,0},{2,3},{3,2},{4,5},{5,4},{6,7},{7,6},{8,9},{9,8},{10,11... | collective-permute-start | bytes 3637256 | tf_op jit(solution)/shard_map/ppermute | solution.py:494
  53.6 15.7 %collective-permute-start.10 = (bf16[4,2,592,128]{3,2,1,0:T(8,128)(2,1)S(1)}, bf16[4,2,592,128]{3,2,1,0:T(8,128)(2,1)S(1)}, u32[]{:S(2)}, u32[]{:S(2)}) collective-permute-start(bf16[4,2,592,128]{3,2,1,0:T(8,128)(2,1)S(1)} %collective-permute-done.6.refs_3_), channel_id=1, source_target_pairs={{0,1},{1,0},{2,3},{3,2},{4,5},{5,4},{6,7},{7,6},{8,9},{9,8},{10,11... | collective-permute-start | bytes 3637256 | tf_op jit(solution)/shard_map/ppermute | solution.py:494
  53.6 15.6 %collective-permute-start.9 = (bf16[4,2,592,128]{3,2,1,0:T(8,128)(2,1)S(1)}, bf16[4,2,592,128]{3,2,1,0:T(8,128)(2,1)S(1)}, u32[]{:S(2)}, u32[]{:S(2)}) collective-permute-start(bf16[4,2,592,128]{3,2,1,0:T(8,128)(2,1)S(1)} %collective-permute-done.5.refs_2_), channel_id=1, source_target_pairs={{0,1},{1,0},{2,3},{3,2},{4,5},{5,4},{6,7},{7,6},{8,9},{9,8},{10,11... | collective-permute-start | bytes 3637256 | tf_op jit(solution)/shard_map/ppermute | solution.py:494
  60.0 11.8 %collective-permute-start.8 = (bf16[4,2,592,128]{3,2,1,0:T(8,128)(2,1)S(1)}, bf16[4,2,592,128]{3,2,1,0:T(8,128)(2,1)S(1)}, u32[]{:S(2)}, u32[]{:S(2)}) collective-permute-start(bf16[4,2,592,128]{3,2,1,0:T(8,128)(2,1)S(1)} %collective-permute-done.4.refs_1_), channel_id=1, source_target_pairs={{0,1},{1,0},{2,3},{3,2},{4,5},{5,4},{6,7},{7,6},{8,9},{9,8},{10,11... | collective-permute-start | bytes 3637256 | tf_op jit(solution)/shard_map/ppermute | solution.py:494
  91.7 10.4 %collective-permute-start.14 = (bf16[32,4096]{1,0:T(8,128)(2,1)S(1)}, bf16[32,4096]{1,0:T(8,128)(2,1)S(1)}, u32[]{:S(2)}, u32[]{:S(2)}) collective-permute-start(bf16[32,4096]{1,0:T(8,128)(2,1)S(1)} %get-tuple-element.252), channel_id=1, source_target_pairs={{0,32},{32,64},{1,33},{33,65},{2,34},{34,66},{3,35},{35,67},{4,36}... | collective-permute-start | bytes 786440 | tf_op jit(solution)/shard_map/ppermute | solution.py:613
  113.8 11.5 %collective-permute-start.22 = (bf16[32,4096]{1,0:T(8,128)(2,1)S(1)}, bf16[32,4096]{1,0:T(8,128)(2,1)S(1)}, u32[]{:S(2)}, u32[]{:S(2)}) collective-permute-start(bf16[32,4096]{1,0:T(8,128)(2,1)S(1)} %get-tuple-element.300), channel_id=1, source_target_pairs={{96,128},{128,160},{160,192},{97,129},{129,161},{161,193},{98,130}... | collective-permute-start | bytes 786440 | tf_op jit(solution)/shard_map/ppermute | solution.py:613
  149.3 139.7 %collective-permute-start.40 = (bf16[32,4096]{1,0:T(8,128)(2,1)S(1)}, bf16[32,4096]{1,0:T(8,128)(2,1)S(1)}, u32[]{:S(2)}, u32[]{:S(2)}) collective-permute-start(bf16[32,4096]{1,0:T(8,128)(2,1)S(1)} %get-tuple-element.396), channel_id=1, source_target_pairs={{64,32},{32,0},{65,33},{33,1},{66,34},{34,2},{67,35},{35,3},{68,36... | collective-permute-start | bytes 786440 | tf_op jit(solution)/shard_map/ppermute | solution.py:623
  151.2 151.0 %collective-permute-start.39 = (bf16[32,4096]{1,0:T(8,128)(2,1)S(1)}, bf16[32,4096]{1,0:T(8,128)(2,1)S(1)}, u32[]{:S(2)}, u32[]{:S(2)}) collective-permute-start(bf16[32,4096]{1,0:T(8,128)(2,1)S(1)} %get-tuple-element.395), channel_id=1, source_target_pairs={{64,32},{32,0},{65,33},{33,1},{66,34},{34,2},{67,35},{35,3},{68,36... | collective-permute-start | bytes 786440 | tf_op jit(solution)/shard_map/ppermute | solution.py:623
  295.2 15.1 %collective-permute-start.42 = (bf16[32,4096]{1,0:T(8,128)(2,1)S(1)}, bf16[32,4096]{1,0:T(8,128)(2,1)S(1)}, u32[]{:S(2)}, u32[]{:S(2)}) collective-permute-start(bf16[32,4096]{1,0:T(8,128)(2,1)S(1)} %get-tuple-element.404), channel_id=1, source_target_pairs={{64,32},{32,0},{65,33},{33,1},{66,34},{34,2},{67,35},{35,3},{68,36... | collective-permute-start | bytes 786440 | tf_op jit(solution)/shard_map/ppermute | solution.py:623
  308.4 10.1 %collective-permute-start.41 = (bf16[32,4096]{1,0:T(8,128)(2,1)S(1)}, bf16[32,4096]{1,0:T(8,128)(2,1)S(1)}, u32[]{:S(2)}, u32[]{:S(2)}) collective-permute-start(bf16[32,4096]{1,0:T(8,128)(2,1)S(1)} %get-tuple-element.403), channel_id=1, source_target_pairs={{64,32},{32,0},{65,33},{33,1},{66,34},{34,2},{67,35},{35,3},{68,36... | collective-permute-start | bytes 786440 | tf_op jit(solution)/shard_map/ppermute | solution.py:623
  329.5 22.5 %collective-permute-start.43 = (bf16[4,4,2,592,128]{4,3,2,1,0:T(8,128)(2,1)S(1)}, bf16[4,4,2,592,128]{4,3,2,1,0:T(8,128)(2,1)S(1)}, u32[]{:S(2)}, u32[]{:S(2)}) collective-permute-start(bf16[4,4,2,592,128]{4,3,2,1,0:T(8,128)(2,1)S(1)} %grads.3), channel_id=1, source_target_pairs={{0,1},{1,0},{2,3},{3,2},{4,5},{5,4},{6,7},{7,6},{8,9},{9,8},{10,11... | collective-permute-start | bytes 14549000 | tf_op jit(solution)/shard_map/ppermute | solution.py:494
  353.1 17.1 %collective-permute-start.44 = (bf16[4,2,592,128]{3,2,1,0:T(8,128)(2,1)S(1)}, bf16[4,2,592,128]{3,2,1,0:T(8,128)(2,1)S(1)}, u32[]{:S(2)}, u32[]{:S(2)}) collective-permute-start(bf16[4,2,592,128]{3,2,1,0:T(8,128)(2,1)S(1)} %get-tuple-element.416), channel_id=1, source_target_pairs={{0,8},{1,3},{2,10},{3,5},{4,12},{5,7},{6,14},{7,1},{8,16},{9,11},{... | collective-permute-start | bytes 3637256 | tf_op jit(solution)/shard_map/ppermute | solution.py:494
  354.6 29.9 %collective-permute-start.45 = (bf16[4,2,592,128]{3,2,1,0:T(8,128)(2,1)S(1)}, bf16[4,2,592,128]{3,2,1,0:T(8,128)(2,1)S(1)}, u32[]{:S(2)}, u32[]{:S(2)}) collective-permute-start(bf16[4,2,592,128]{3,2,1,0:T(8,128)(2,1)S(1)} %get-tuple-element.417), channel_id=1, source_target_pairs={{0,16},{1,5},{2,18},{3,7},{4,20},{5,1},{6,22},{7,3},{8,24},{9,13},... | collective-permute-start | bytes 3637256 | tf_op jit(solution)/shard_map/ppermute | solution.py:494
  357.3 27.2 %collective-permute-start.46 = (bf16[4,2,592,128]{3,2,1,0:T(8,128)(2,1)S(1)}, bf16[4,2,592,128]{3,2,1,0:T(8,128)(2,1)S(1)}, u32[]{:S(2)}, u32[]{:S(2)}) collective-permute-start(bf16[4,2,592,128]{3,2,1,0:T(8,128)(2,1)S(1)} %get-tuple-element.418), channel_id=1, source_target_pairs={{0,24},{1,7},{2,26},{3,1},{4,28},{5,3},{6,30},{7,5},{8,0},{9,15},{... | collective-permute-start | bytes 3637256 | tf_op jit(solution)/shard_map/ppermute | solution.py:494
  385.1 28.1 %collective-permute-start.47 = (bf16[2,592,128]{2,1,0:T(8,128)(2,1)S(1)}, bf16[2,592,128]{2,1,0:T(8,128)(2,1)S(1)}, u32[]{:S(2)}, u32[]{:S(2)}) collective-permute-start(bf16[2,592,128]{2,1,0:T(8,128)(2,1)S(1)} %get-tuple-element.420), channel_id=1, source_target_pairs={{0,2},{1,9},{2,4},{3,11},{4,6},{5,13},{6,0},{7,15},{8,10},{9,17},{... | collective-permute-start | bytes 909320 | tf_op jit(solution)/shard_map/ppermute | solution.py:494
  399.6 21.0 %collective-permute-start.48 = (bf16[2,592,128]{2,1,0:T(8,128)(2,1)S(1)}, bf16[2,592,128]{2,1,0:T(8,128)(2,1)S(1)}, u32[]{:S(2)}, u32[]{:S(2)}) collective-permute-start(bf16[2,592,128]{2,1,0:T(8,128)(2,1)S(1)} %get-tuple-element.421), channel_id=1, source_target_pairs={{0,4},{1,17},{2,6},{3,19},{4,0},{5,21},{6,2},{7,23},{8,12},{9,25},... | collective-permute-start | bytes 909320 | tf_op jit(solution)/shard_map/ppermute | solution.py:494
  401.8 21.9 %collective-permute-start.49 = (bf16[2,592,128]{2,1,0:T(8,128)(2,1)S(1)}, bf16[2,592,128]{2,1,0:T(8,128)(2,1)S(1)}, u32[]{:S(2)}, u32[]{:S(2)}) collective-permute-start(bf16[2,592,128]{2,1,0:T(8,128)(2,1)S(1)} %get-tuple-element.422), channel_id=1, source_target_pairs={{0,6},{1,25},{2,0},{3,27},{4,2},{5,29},{6,4},{7,31},{8,14},{9,1},{... | collective-permute-start | bytes 909320 | tf_op jit(solution)/shard_map/ppermute | solution.py:494
  423.8 18.5 %collective-permute-start.50 = (f32[592,128]{1,0:T(8,128)S(1)}, f32[592,128]{1,0:T(8,128)S(1)}, u32[]{:S(2)}, u32[]{:S(2)}) collective-permute-start(f32[592,128]{1,0:T(8,128)S(1)} %get-tuple-element.424), channel_id=1, source_target_pairs={{0,1},{1,0},{2,3},{3,2},{4,5},{5,4},{6,7},{7,6},{8,9},{9,8},{10,11... | collective-permute-start | bytes 909320 | tf_op jit(solution)/shard_map/ppermute | solution.py:494
  (27 other events, 76.1 us)
